TPU v7x, 32 devices: a whole 2x2x4 slice. The times are simulated.
32 devices in a mesh: dp: 4 (over y, x), mp: 8 (over z, core).
Axes of the slice: x: 2, y: 2, z: 4, core: 2. Of those that a mesh axis runs over, the one named last changes fastest.
Arguments:
- inputs: bfloat16 [128, 10240], P('dp', 'mp'), may hold values from -6 to 6
- out_grads: bfloat16 [128, 10240], P('dp', 'mp'), may hold values from -6 to 6
- w_in: bfloat16 [10240, 18432], P('mp', 'dp'), may hold values from -0.0625 to 0.0625
- w_out: bfloat16 [18432, 10240], P('dp', 'mp'), may hold values from -0.046875 to 0.046875
Outputs:
- in_grads: float32 [128, 10240], P('dp', 'mp')
- grad_w_in: bfloat16 [10240, 18432], P('mp', 'dp')
- grad_w_out: bfloat16 [18432, 10240], P('dp', 'mp')
All inputs are finite; a program needn't handle non-finite values.
Results may differ from a plain program's by a relative error of at most 0.005.
Values may be sent and summed in bfloat16 or wider, within the bound.
No kernel may reach another device: no remote copies, remote signals or barrier semaphores. Data moves between devices by JAX's collectives and lax.ppermute only.
A program may use at most 128 MiB of HBM per device.

v0:
```python
import math

import jax
import jax.numpy as jnp
from jax import lax
from jax.sharding import PartitionSpec as P


def gelu_parts(preact):
    cumul = 0.5 * (1.0 + jax.scipy.special.erf(preact * (1.0 / math.sqrt(2.0))))
    density = jnp.exp(-0.5 * preact * preact) * (1.0 / math.sqrt(2.0 * math.pi))
    return (preact * cumul, cumul + preact * density)


def contract_rows(left, right):
    return lax.dot_general(
        left, right, (((0,), (0,)), ((), ())), preferred_element_type=jnp.float32
    )


def contract_cols(left, right):
    return lax.dot_general(
        left, right, (((1,), (1,)), ((), ())), preferred_element_type=jnp.float32
    )


def finish(preact, grad_act):
    gelu_value, gelu_slope = gelu_parts(preact)
    activation = gelu_value.astype(jnp.bfloat16)
    grad_preact = (grad_act * gelu_slope).astype(jnp.bfloat16)
    return (activation, grad_preact)


def local(inputs, out_grads, w_in, w_out):
    inputs_all, grads_all = (
        lax.all_gather(inputs, "dp", axis=0, tiled=True),
        lax.all_gather(out_grads, "dp", axis=0, tiled=True),
    )
    total_rows = inputs_all.shape[0]
    partial_pre = jnp.dot(inputs_all, w_in, preferred_element_type=jnp.float32)
    partial_grad = contract_cols(grads_all, w_out)
    preact, grad_act = lax.psum((partial_pre, partial_grad), "mp")
    activation, grad_preact = finish(preact, grad_act)
    factor = 1.0 / math.sqrt(total_rows)
    grad_in = (contract_rows(inputs_all, grad_preact) * factor).astype(jnp.bfloat16)
    grad_out = (contract_rows(activation, grads_all) * factor).astype(jnp.bfloat16)
    partial_all = contract_cols(grad_preact, w_in)
    in_total = lax.psum_scatter(partial_all, "dp", scatter_dimension=0, tiled=True)
    return (in_total, grad_in, grad_out)


def solution(mesh):
    return jax.shard_map(
        local,
        mesh=mesh,
        in_specs=(P("dp", "mp"), P("dp", "mp"), P("mp", "dp"), P("dp", "mp")),
        out_specs=(P("dp", "mp"), P("mp", "dp"), P("dp", "mp")),
        check_vma=False,
    )
```

profile of v0, /device:TPU:0, one launch (start us, length us, event | category | flops | bytes accessed | tf_op | source)
XLA Modules:
  0.0 195.0 jit_solution(13236998892808391300)
XLA Ops:
  7.2 0.0 all-reduce.3.cloned.1.call-start
  7.2 11.0 %all_gather.6 = bf16[128,1280]{1,0:T(8,128)(2,1)S(1)} all-gather(bf16[32,1280]{1,0:T(8,128)(2,1)} %param.5), channel_id=1, replica_groups=mesh['dp'=4,'mp'=8] {'dp'}, dimensions={0}, use_global_device_ids=true | all-gather | bytes 409600 | tf_op jit(solution)/shard_map/all_gather | solution.py:37
  18.2 8.9 %all_gather.7 = bf16[128,1280]{1,0:T(8,128)(2,1)S(1)} all-gather(bf16[32,1280]{1,0:T(8,128)(2,1)} %param.4), channel_id=1, replica_groups=mesh['dp'=4,'mp'=8] {'dp'}, dimensions={0}, use_global_device_ids=true | all-gather | bytes 409600 | tf_op jit(solution)/shard_map/all_gather | solution.py:36
  27.1 0.0 copy-start
  27.1 9.8 %fusion.7 = f32[128,4608]{1,0:T(8,128)} fusion(bf16[128,1280]{1,0:T(8,128)(2,1)S(1)} %all_gather.6, bf16[4608,1280]{1,0:T(8,128)(2,1)} %param.7), kind=kOutput, calls=%fused_computation.12 | convolution fusion | flops 1509949440 | bytes 14483456 | tf_op jit(solution)/shard_map/dot_general | solution.py:22
  36.9 0.0 copy-done
  36.9 3.1 %fusion.8 = f32[128,4608]{1,0:T(8,128)} fusion(bf16[128,1280]{1,0:T(8,128)(2,1)S(1)} %all_gather.7, bf16[1280,4608]{1,0:T(8,128)(2,1)S(1)} %copy-done), kind=kOutput, calls=%fused_computation.13 | convolution fusion | flops 1509949440 | bytes 14483456 | tf_op jit(solution)/shard_map/dot_general | solution.py:40
  40.0 0.0 all-reduce.3.cloned.1.call-update
  40.1 0.0 reduce-scatter.2.cloned.1.call-start
  40.1 107.1 %all-reduce.3.cloned.1.call-done = (f32[128,4608]{1,0:T(8,128)}, f32[128,4608]{1,0:T(8,128)}) async-done(((f32[128,4608]{1,0:T(8,128)}, f32[128,4608]{1,0:T(8,128)}), (f32[128,4608]{1,0:T(8,128)}, f32[128,4608]{1,0:T(8,128)})) %all-reduce.3.cloned.1.call-update) | async-done | bytes 4718608 | tf_op jit(solution)/shard_map/psum | solution.py:42
  147.3 2.8 %fusion.6 = bf16[128,4608]{1,0:T(8,128)(2,1)S(1)} fusion(f32[128,4608]{1,0:T(8,128)} %get-tuple-element.6, f32[128,4608]{1,0:T(8,128)} %get-tuple-element.7), kind=kLoop, calls=%fused_computation.9 | loop fusion | flops 5898240 | bytes 5898240 | tf_op jit(solution)/shard_map/convert_element_type | solution.py:30
  150.1 9.0 %fusion.9 = f32[128,1280]{1,0:T(8,128)} fusion(bf16[128,4608]{1,0:T(8,128)(2,1)S(1)} %fusion.6, bf16[1280,4608]{1,0:T(8,128)(2,1)} %param.6), kind=kOutput, calls=%fused_computation.14 | convolution fusion | flops 1509949440 | bytes 13631488 | tf_op jit(solution)/shard_map/dot_general | solution.py:22
  159.1 0.0 reduce-scatter.2.cloned.1.call-update
  159.1 6.3 %fusion = bf16[1280,4608]{0,1:T(8,128)(2,1)} fusion(bf16[128,4608]{1,0:T(8,128)(2,1)S(1)} %fusion.6, bf16[128,1280]{1,0:T(8,128)(2,1)S(1)} %all_gather.7), kind=kOutput, calls=%fused_computation.2 | convolution fusion | flops 1521745920 | bytes 13303808 | tf_op jit(solution)/shard_map/dot_general | solution.py:16
  165.4 0.0 copy-start.1
  165.4 16.5 %copy.7 = bf16[1280,4608]{1,0:T(8,128)(2,1)} copy(bf16[1280,4608]{0,1:T(8,128)(2,1)} %fusion) | data formatting | bytes 23592960
  181.8 0.0 copy-done.1
  181.8 6.3 %multiply_convert_fusion = bf16[4608,1280]{1,0:T(8,128)(2,1)} fusion(bf16[128,1280]{1,0:T(8,128)(2,1)S(1)} %all_gather.6, f32[128,4608]{1,0:T(8,128)S(1)} %copy-done.1), kind=kOutput, calls=%fused_computation | convolution fusion | flops 1524695040 | bytes 14483456 | tf_op jit(solution)/shard_map/dot_general | solution.py:16
  188.1 0.0 reduce-scatter.2.cloned.1.call-done
Async XLA Ops:
  7.2 140.1 %all-reduce.3.cloned.1.call-start = ((), (), s32[]{:S(2)}) async-start(), calls=%async_computation.2 | async-start | bytes 9437184 | tf_op jit(solution)/shard_map/psum | solution.py:42
  27.1 9.8 %copy-start = (bf16[1280,4608]{1,0:T(8,128)(2,1)S(1)}, bf16[1280,4608]{1,0:T(8,128)(2,1)}, u32[]{:S(2)}) copy-start(bf16[1280,4608]{1,0:T(8,128)(2,1)} %param.6) | copy-start | bytes 35389444
  40.1 148.1 %reduce-scatter.2.cloned.1.call-start = ((), (), s32[]{:S(2)}) async-start(), calls=%async_computation.1 | async-start | bytes 819200 | tf_op jit(solution)/shard_map/reduce_scatter | solution.py:48
  165.4 16.5 %copy-start.1 = (f32[128,4608]{1,0:T(8,128)S(1)}, f32[128,4608]{1,0:T(8,128)}, u32[]{:S(2)}) copy-start(f32[128,4608]{1,0:T(8,128)} %get-tuple-element.7) | copy-start | bytes 7077892
Sparse Core Ops, SparseCore 0:
  40.2 107.0 all-reduce.2
  159.2 25.4 reduce-scatter.1
where the time goes:
time: 196 us; the launch traced here: 195 us
  waiting for transfers between devices  107 us (55%)
  matrix products  34.4 us (18%)
  blocking collectives  19.9 us (10%)
  local copies, waits for them, and re-layouts  16.5 us (8%)
  between operations  14 us (7%)
  other arithmetic  2.83 us (1%)
    psum x1, waiting for transfers between devices, local(): preact, grad_act = lax.psum((partial_pre, partial_grad), 'mp')  107 us
    dot_general x2, matrix products, contract_cols(): lax.dot_general(left, right, (((1,), (1,)), ((), ())), preferred_element_...  18.8 us
    unnamed x5, local copies, waits for them, and re-layouts  16.5 us
    dot_general x2, matrix products, contract_rows(): lax.dot_general(left, right, (((0,), (0,)), ((), ())), preferred_element_...  12.5 us
    all_gather x1, blocking collectives, local(): lax.all_gather(out_grads, 'dp', axis=0, tiled=True)  11 us
    all_gather x1, blocking collectives, local(): lax.all_gather(inputs, 'dp', axis=0, tiled=True)  8.9 us
  transfers between devices with their start and end apart: 2, of which 1 were waited for; matrix products, arithmetic and copies ran while one was open for 15% of the time, Pallas kernels for 0%

commit v1 on v0

v1 whole, which is shorter than its diff:
```python
import functools
import math

import jax
import jax.numpy as jnp
from jax import lax
from jax.experimental import pallas as pl
from jax.experimental.pallas import tpu as pltpu
from jax.sharding import PartitionSpec as P

BF16 = jnp.bfloat16
F32 = jnp.float32
CHUNKS = 2
BLOCK = 768
VMEM_BYTES = 40 * 1024 * 1024


def gelu_parts(preact):
    cumul = 0.5 * (1.0 + jax.scipy.special.erf(preact * (1.0 / math.sqrt(2.0))))
    density = jnp.exp(-0.5 * preact * preact) * (1.0 / math.sqrt(2.0 * math.pi))
    return (preact * cumul, cumul + preact * density)


def contract(left, right, left_dim, right_dim):
    return lax.dot_general(
        left,
        right,
        (((left_dim,), (right_dim,)), ((), ())),
        preferred_element_type=F32,
    )


def bit_reversed(count):
    bits = count.bit_length() - 1
    return [
        sum(((slot >> bit) & 1) << (bits - 1 - bit) for bit in range(bits))
        for slot in range(count)
    ]


def exchange(array, axis, size, step):
    return lax.ppermute(array, axis, [(i, i ^ step) for i in range(size)])


def whole(*shape):
    return pl.BlockSpec(shape, lambda step: (0,) * len(shape))


def params():
    return pltpu.CompilerParams(vmem_limit_bytes=VMEM_BYTES)


def cost(flops, size):
    return pl.CostEstimate(flops=flops, bytes_accessed=size, transcendentals=0)


def slot_matrix(rank, total, slots):
    piece = total // slots
    blocks = jnp.array(bit_reversed(slots), jnp.int32) ^ rank
    source = (blocks[:, None] * piece + jnp.arange(piece, dtype=jnp.int32)).reshape(-1)
    return (source[:, None] == jnp.arange(total, dtype=jnp.int32)).astype(BF16)


def forward(xs, gs, w_in, w_out, start, width):
    total, features = xs.shape
    half = total // 2
    first, steps = start // BLOCK, width // BLOCK

    def kernel(xs_ref, gs_ref, wi_ref, wo_ref, keep_ref, send_ref):
        pre = contract(xs_ref[...], wi_ref[...], 1, 0)
        grad = contract(gs_ref[...], wo_ref[...], 1, 1)
        keep_ref[0] = pre[:half]
        keep_ref[1] = grad[:half]
        send_ref[0] = pre[half:].astype(BF16)
        send_ref[1] = grad[half:].astype(BF16)

    return pl.pallas_call(
        kernel,
        grid=(steps,),
        out_shape=(
            jax.ShapeDtypeStruct((2, half, width), F32),
            jax.ShapeDtypeStruct((2, half, width), BF16),
        ),
        in_specs=[
            pl.BlockSpec((total, features), lambda i: (0, 0)),
            pl.BlockSpec((total, features), lambda i: (0, 0)),
            pl.BlockSpec((features, BLOCK), lambda i: (0, first + i)),
            pl.BlockSpec((BLOCK, features), lambda i: (first + i, 0)),
        ],
        out_specs=(
            pl.BlockSpec((2, half, BLOCK), lambda i: (0, 0, i)),
            pl.BlockSpec((2, half, BLOCK), lambda i: (0, 0, i)),
        ),
        compiler_params=params(),
        cost_estimate=cost(4 * total * features * width, 4 * features * width),
        name="forward",
    )(xs, gs, w_in, w_out)


def input_grads(lower, upper, order, w_in, carried, start, width):
    half = lower.shape[1]
    features = w_in.shape[0]
    first, steps = start // BLOCK, width // BLOCK

    def kernel(*refs):
        low_ref, up_ref, order_ref, wi_ref = refs[:4]
        out_ref = refs[-1]
        step = pl.program_id(0)
        grad = jnp.concatenate([low_ref[0], up_ref[0]], axis=0)
        grad = contract(order_ref[...], grad, 1, 0).astype(BF16)
        value = contract(grad, wi_ref[...], 1, 1)

        @pl.when(step == 0)
        def _():
            out_ref[...] = value if carried is None else refs[4][...] + value

        @pl.when(step > 0)
        def _():
            out_ref[...] += value

    block = pl.BlockSpec((1, half, BLOCK), lambda i: (1, 0, i))
    return pl.pallas_call(
        kernel,
        grid=(steps,),
        out_shape=jax.ShapeDtypeStruct((2 * half, features), F32),
        in_specs=[
            block,
            block,
            whole(2 * half, 2 * half),
            pl.BlockSpec((features, BLOCK), lambda i: (0, first + i)),
        ]
        + ([] if carried is None else [whole(2 * half, features)]),
        out_specs=whole(2 * half, features),
        compiler_params=params(),
        cost_estimate=cost(4 * half * features * width, 2 * features * width),
        name="input_grads",
    )(lower, upper, order, w_in, *([] if carried is None else [carried]))


def weight_grads(xt, gs, finals, hidden, factor):
    features, total = xt.shape
    half = total // 2
    chunks = len(finals)
    steps = hidden // chunks // BLOCK

    def kernel(xt_ref, gs_ref, *refs):
        in_ref, out_ref = refs[-2:]
        step = pl.program_id(0)

        def work(la_ref, ua_ref, lg_ref, ug_ref):
            act = jnp.concatenate([la_ref[0], ua_ref[0]], axis=0)
            grad = jnp.concatenate([lg_ref[0], ug_ref[0]], axis=0)
            turned = act.astype(F32).T.astype(BF16)
            in_ref[...] = (contract(xt_ref[...], grad, 1, 0) * factor).astype(BF16)
            out_ref[...] = (contract(turned, gs_ref[...], 1, 0) * factor).astype(BF16)

        for chunk in range(chunks):
            here = (step >= chunk * steps) & (step < (chunk + 1) * steps)
            pl.when(here)(functools.partial(work, *refs[4 * chunk : 4 * chunk + 4]))

    def block(chunk, which):
        def place(i):
            return which, 0, jnp.clip(i - chunk * steps, 0, steps - 1)

        return pl.BlockSpec((1, half, BLOCK), place)

    specs, operands = [], []
    for chunk, (lower, upper) in enumerate(finals):
        specs += [block(chunk, 0), block(chunk, 0), block(chunk, 1), block(chunk, 1)]
        operands += [lower, upper, lower, upper]
    return pl.pallas_call(
        kernel,
        grid=(chunks * steps,),
        out_shape=(
            jax.ShapeDtypeStruct((features, hidden), BF16),
            jax.ShapeDtypeStruct((hidden, features), BF16),
        ),
        in_specs=[whole(features, total), whole(total, features)] + specs,
        out_specs=(
            pl.BlockSpec((features, BLOCK), lambda i: (0, i)),
            pl.BlockSpec((BLOCK, features), lambda i: (i, 0)),
        ),
        compiler_params=params(),
        cost_estimate=cost(4 * total * features * hidden, 4 * features * hidden),
        name="weight_grads",
    )(xt, gs, *operands)


def halve(keep, received):
    half, width = keep.shape[1] // 2, keep.shape[2]

    def kernel(keep_ref, received_ref, next_ref, send_ref):
        next_ref[...] = keep_ref[:, :half] + received_ref[:, :half].astype(F32)
        send_ref[...] = (keep_ref[:, half:] + received_ref[:, half:].astype(F32)).astype(BF16)

    return pl.pallas_call(
        kernel,
        out_shape=(
            jax.ShapeDtypeStruct((2, half, width), F32),
            jax.ShapeDtypeStruct((2, half, width), BF16),
        ),
        grid=(1,),
        in_specs=[whole(2, 2 * half, width)] * 2,
        out_specs=(whole(2, half, width),) * 2,
        compiler_params=params(),
        cost_estimate=cost(4 * half * width, 24 * half * width),
        name="halve",
    )(keep, received)


def activate(keep, received):
    def kernel(keep_ref, received_ref, out_ref):
        value, slope = gelu_parts(keep_ref[0] + received_ref[0].astype(F32))
        grad = keep_ref[1] + received_ref[1].astype(F32)
        out_ref[0] = value.astype(BF16)
        out_ref[1] = (grad * slope).astype(BF16)

    return pl.pallas_call(
        kernel,
        out_shape=jax.ShapeDtypeStruct(keep.shape, BF16),
        grid=(1,),
        in_specs=[whole(*keep.shape)] * 2,
        out_specs=whole(*keep.shape),
        compiler_params=params(),
        cost_estimate=cost(20 * keep.size, 8 * keep.size),
        name="activate",
    )(keep, received)


def scatter_sum(keep, send, size):
    step = 1
    while 2 * step < size:
        keep, send = halve(keep, exchange(send, "mp", size, step))
        step *= 2
    return activate(keep, exchange(send, "mp", size, step))


def gather_rows(own, size):
    step = size // 2
    while step > 1:
        own = jnp.concatenate([own, exchange(own, "mp", size, step)], axis=1)
        step //= 2
    return own, exchange(own, "mp", size, 1)


def local(inputs, out_grads, w_in, w_out, dp, mp):
    hidden = w_in.shape[1]
    width = hidden // CHUNKS
    rows = inputs.shape[0]
    factor = 1.0 / math.sqrt(rows * dp)
    order = slot_matrix(lax.axis_index("mp").astype(jnp.int32), rows * dp, mp)

    def gather_tokens(own):
        return jnp.concatenate([own] + [exchange(own, "dp", dp, j) for j in range(1, dp)])

    gathered_x, gathered_g = gather_tokens(inputs), gather_tokens(out_grads)
    xs = contract(order, gathered_x, 1, 0).astype(BF16)
    gs = contract(order, gathered_g, 1, 0).astype(BF16)
    xt = contract(gathered_x, order, 0, 1).astype(BF16)

    finals = []
    for chunk in range(CHUNKS):
        keep, send = forward(xs, gs, w_in, w_out, chunk * width, width)
        finals.append(gather_rows(scatter_sum(keep, send, mp), mp))

    partial = None
    for chunk, (lower, upper) in enumerate(finals):
        partial = input_grads(lower, upper, order.T, w_in, partial, chunk * width, width)
    in_total = partial[:rows]
    for j in range(1, dp):
        part = partial[j * rows : (j + 1) * rows].astype(BF16)
        in_total = in_total + exchange(part, "dp", dp, j).astype(F32)
    return (in_total, *weight_grads(xt, gs, finals, hidden, factor))


def solution(mesh):
    sizes = dict(mesh.shape)
    return jax.shard_map(
        functools.partial(local, dp=sizes["dp"], mp=sizes["mp"]),
        mesh=mesh,
        in_specs=(P("dp", "mp"), P("dp", "mp"), P("mp", "dp"), P("dp", "mp")),
        out_specs=(P("dp", "mp"), P("mp", "dp"), P("dp", "mp")),
        check_vma=False,
    )
```

time: 196 us -> 112 us (0.57)
  waiting for transfers between devices: 107 us -> 48.4 us
  matrix products: 34.4 us -> 0.89 us
  Pallas kernels: 0 us -> 28.4 us
  starting transfers between devices: 0.08 us -> 21.5 us
  blocking collectives: 19.9 us -> 0 us
  between operations: 14 us -> 0.88 us
  local copies, waits for them, and re-layouts: 16.5 us -> 9.71 us
    psum x1 -> x0, waiting for transfers between devices: 107 us -> none  [local(): preact, grad_act = lax.psum((partial_pre, partial_grad), 'mp')]
    ppermute x0 -> x21, waiting for transfers between devices: none -> 48.4 us  [exchange(): return lax.ppermute(array, axis, [(i, i ^ step) for i in range(size)])]
    dot_general x5 -> x3, matrix products: 34.4 us -> 0.89 us  [contract(): lax.dot_general(left, right, (((left_dim,), (right_dim,)), ((), ())), pre...]
    pallas_call x0 -> x11, Pallas kernels: none -> 28.4 us  [the longest x2 10.7 us: forward(): pl.pallas_call(kernel, grid=(steps,), out_shape=(jax.ShapeDtypeStruct((2,...]
    ppermute x0 -> x21, starting transfers between devices: none -> 21.5 us  [exchange(): return lax.ppermute(array, axis, [(i, i ^ step) for i in range(size)])]
    all_gather x2 -> x0, blocking collectives: 19.9 us -> none  [the longest x1 11 us: local(): lax.all_gather(out_grads, 'dp', axis=0, tiled=True)]
    unnamed x5 -> x9, local copies, waits for them, and re-layouts: 16.5 us -> 9.61 us
    convert_element_type x1, other arithmetic: 2.83 us -> 0.01 us  [slot_matrix(): return (source[:, None] == jnp.arange(total, dtype=jnp.int32)).astype(BF16)]
  transfers between devices with their start and end apart: 2 -> 21, of which waited for: 1 -> 10; matrix products, arithmetic and copies ran while one was open for 15% -> 2% of each run, Pallas kernels for 0% -> 18%
where the time goes in v1:
time: 112 us; the launch traced here: 111 us
  waiting for transfers between devices  48.4 us (43%)
  Pallas kernels  28.4 us (25%)
  starting transfers between devices  21.5 us (19%)
  local copies, waits for them, and re-layouts  9.71 us (9%)
  other arithmetic  1.6 us (1%)
    ppermute x21, waiting for transfers between devices, exchange(): return lax.ppermute(array, axis, [(i, i ^ step) for i in range(size)])  48.4 us
    ppermute x21, starting transfers between devices, exchange(): return lax.ppermute(array, axis, [(i, i ^ step) for i in range(size)])  21.5 us
    pallas_call x2, Pallas kernels, forward(): pl.pallas_call(kernel, grid=(steps,), out_shape=(jax.ShapeDtypeStruct((2,...  10.7 us
    pallas_call x1, Pallas kernels, weight_grads(): pl.pallas_call(kernel, grid=(chunks * steps,), out_shape=(jax.ShapeDtypeS...  10.7 us
    unnamed x9, local copies, waits for them, and re-layouts  9.61 us
    pallas_call x2, Pallas kernels, input_grads(): pl.pallas_call(kernel, grid=(steps,), out_shape=jax.ShapeDtypeStruct((2 *...  6.56 us
  transfers between devices with their start and end apart: 21, of which 10 were waited for; matrix products, arithmetic and copies ran while one was open for 2% of the time, Pallas kernels for 18%

profile of v1, /device:TPU:0, one launch (start us, length us, event | category | flops | bytes accessed | tf_op | source)
XLA Modules:
  0.0 111.4 jit_solution(16757623735069993153)
XLA Ops:
  0.6 3.0 %collective-permute-start = (bf16[32,1280]{1,0:T(8,128)(2,1)}, bf16[32,1280]{1,0:T(8,128)(2,1)S(1)}, u32[]{:S(2)}, u32[]{:S(2)}) collective-permute-start(bf16[32,1280]{1,0:T(8,128)(2,1)} %param.5), channel_id=1, source_target_pairs={{0,8},{8,0},{16,24},{24,16},{1,9},{9,1},{17,25},{25,17},{2,10},{10... | collective-permute-start | bytes 245768 | tf_op jit(solution)/shard_map/ppermute | solution.py:42
  3.6 1.5 %collective-permute-start.1 = (bf16[32,1280]{1,0:T(8,128)(2,1)}, bf16[32,1280]{1,0:T(8,128)(2,1)S(1)}, u32[]{:S(2)}, u32[]{:S(2)}) collective-permute-start(bf16[32,1280]{1,0:T(8,128)(2,1)} %param.5), channel_id=1, source_target_pairs={{0,16},{8,24},{16,0},{24,8},{1,17},{9,25},{17,1},{25,9},{2,18},{10... | collective-permute-start | bytes 245768 | tf_op jit(solution)/shard_map/ppermute | solution.py:42
  5.2 1.9 %collective-permute-start.3 = (bf16[32,1280]{1,0:T(8,128)(2,1)}, bf16[32,1280]{1,0:T(8,128)(2,1)S(1)}, u32[]{:S(2)}, u32[]{:S(2)}) collective-permute-start(bf16[32,1280]{1,0:T(8,128)(2,1)} %param.6), channel_id=1, source_target_pairs={{0,8},{8,0},{16,24},{24,16},{1,9},{9,1},{17,25},{25,17},{2,10},{10... | collective-permute-start | bytes 245768 | tf_op jit(solution)/shard_map/ppermute | solution.py:42
  7.1 1.5 %collective-permute-start.4 = (bf16[32,1280]{1,0:T(8,128)(2,1)}, bf16[32,1280]{1,0:T(8,128)(2,1)S(1)}, u32[]{:S(2)}, u32[]{:S(2)}) collective-permute-start(bf16[32,1280]{1,0:T(8,128)(2,1)} %param.6), channel_id=1, source_target_pairs={{0,16},{8,24},{16,0},{24,8},{1,17},{9,25},{17,1},{25,9},{2,18},{10... | collective-permute-start | bytes 245768 | tf_op jit(solution)/shard_map/ppermute | solution.py:42
  8.7 0.9 constant_dynamic-update-slice_fusion.3
  9.5 0.7 xor_multiply_fusion
  10.2 0.1 iota_add_fusion
  10.3 0.1 add.32
  10.4 0.1 collective-permute-start.5
  10.5 0.4 collective-permute-done.2
  10.9 0.3 convolution_convert_fusion.2.xs_ref
  11.2 0.6 collective-permute-done.4
  11.8 4.2 %collective-permute-done.5 = bf16[32,1280]{1,0:T(8,128)(2,1)S(1)} collective-permute-done((bf16[32,1280]{1,0:T(8,128)(2,1)}, bf16[32,1280]{1,0:T(8,128)(2,1)S(1)}, u32[]{:S(2)}, u32[]{:S(2)}) %collective-permute-start.5) | collective-permute-done | bytes 81952 | tf_op jit(solution)/shard_map/ppermute | solution.py:42
  16.0 0.3 convolution_convert_fusion.1.gs_ref
  16.3 4.3 %copy-done = bf16[1280,4608]{1,0:T(8,128)(2,1)S(1)} copy-done((bf16[1280,4608]{1,0:T(8,128)(2,1)S(1)}, bf16[1280,4608]{1,0:T(8,128)(2,1)}, u32[]{:S(2)}) %copy-start) | copy-done | bytes 11796504
  20.6 5.4 %forward.3 = (f32[2,64,2304]{2,1,0:T(8,128)S(1)}, bf16[2,64,2304]{2,1,0:T(8,128)(2,1)S(1)}) custom-call(bf16[128,1280]{1,0:T(8,128)(2,1)S(1)} %convolution_convert_fusion.2.xs_ref, bf16[128,1280]{1,0:T(8,128)(2,1)S(1)} %convolution_convert_fusion.1.gs_ref, bf16[1280,4608]{1,0:T(8,128)(2,1)S(1)} %copy-done, bf16[4608,1280]{1,0:T(8,128)(2,1)} %wo_ref.3), custom_call_target="tpu_custom_call" | custom-call | flops 1509949440 | bytes 11796480 | tf_op jit(solution)/shard_map/forward/pallas_call | solution.py:77
  26.0 0.1 collective-permute-start.12
  26.1 5.4 %forward.2 = (f32[2,64,2304]{2,1,0:T(8,128)S(1)}, bf16[2,64,2304]{2,1,0:T(8,128)(2,1)S(1)}) custom-call(bf16[128,1280]{1,0:T(8,128)(2,1)S(1)} %convolution_convert_fusion.2.xs_ref, bf16[128,1280]{1,0:T(8,128)(2,1)S(1)} %convolution_convert_fusion.1.gs_ref, bf16[1280,4608]{1,0:T(8,128)(2,1)S(1)} %copy-done, bf16[4608,1280]{1,0:T(8,128)(2,1)} %wo_ref.3), custom_call_target="tpu_custom_call" | custom-call | flops 1509949440 | bytes 11796480 | tf_op jit(solution)/shard_map/forward/pallas_call | solution.py:77
  31.4 0.6 collective-permute-start.6
  32.0 0.1 halve.6
  32.1 1.6 %collective-permute-start.13 = (bf16[2,32,2304]{2,1,0:T(8,128)(2,1)S(1)}, bf16[2,32,2304]{2,1,0:T(8,128)(2,1)S(1)}, u32[]{:S(2)}, u32[]{:S(2)}) collective-permute-start(bf16[2,32,2304]{2,1,0:T(8,128)(2,1)S(1)} %get-tuple-element.26), channel_id=1, source_target_pairs={{0,2},{1,3},{2,0},{3,1},{4,6},{5,7},{6,4},{7,5},{8,10},{9,11},{10,... | collective-permute-start | bytes 884744 | tf_op jit(solution)/shard_map/ppermute | solution.py:42
  33.7 0.1 halve.4
  33.9 1.5 %collective-permute-start.7 = (bf16[2,32,2304]{2,1,0:T(8,128)(2,1)S(1)}, bf16[2,32,2304]{2,1,0:T(8,128)(2,1)S(1)}, u32[]{:S(2)}, u32[]{:S(2)}) collective-permute-start(bf16[2,32,2304]{2,1,0:T(8,128)(2,1)S(1)} %get-tuple-element.20), channel_id=1, source_target_pairs={{0,2},{1,3},{2,0},{3,1},{4,6},{5,7},{6,4},{7,5},{8,10},{9,11},{10,... | collective-permute-start | bytes 884744 | tf_op jit(solution)/shard_map/ppermute | solution.py:42
  35.4 6.7 %collective-permute-done.13.received_ref = bf16[2,32,2304]{2,1,0:T(8,128)(2,1)S(1)} collective-permute-done((bf16[2,32,2304]{2,1,0:T(8,128)(2,1)S(1)}, bf16[2,32,2304]{2,1,0:T(8,128)(2,1)S(1)}, u32[]{:S(2)}, u32[]{:S(2)}) %collective-permute-start.13) | collective-permute-done | bytes 294944 | tf_op jit(solution)/shard_map/ppermute | solution.py:42
  42.1 2.6 %collective-permute-start.14 = (bf16[2,16,2304]{2,1,0:T(8,128)(2,1)S(1)}, bf16[2,16,2304]{2,1,0:T(8,128)(2,1)S(1)}, u32[]{:S(2)}, u32[]{:S(2)}) collective-permute-start(bf16[2,16,2304]{2,1,0:T(8,128)(2,1)S(1)} %get-tuple-element.28), channel_id=1, source_target_pairs={{0,4},{1,5},{2,6},{3,7},{4,0},{5,1},{6,2},{7,3},{8,12},{9,13},{10,... | collective-permute-start | bytes 442376 | tf_op jit(solution)/shard_map/ppermute | solution.py:42
  44.7 5.8 %collective-permute-done.7.received_ref = bf16[2,32,2304]{2,1,0:T(8,128)(2,1)S(1)} collective-permute-done((bf16[2,32,2304]{2,1,0:T(8,128)(2,1)S(1)}, bf16[2,32,2304]{2,1,0:T(8,128)(2,1)S(1)}, u32[]{:S(2)}, u32[]{:S(2)}) %collective-permute-start.7) | collective-permute-done | bytes 294944 | tf_op jit(solution)/shard_map/ppermute | solution.py:42
  50.6 1.0 collective-permute-start.8
  51.7 0.1 activate.3
  51.8 2.0 %collective-permute-start.15 = (bf16[2,16,2304]{2,1,0:T(8,128)(2,1)S(1)}, bf16[2,16,2304]{2,1,0:T(8,128)(2,1)S(1)}, u32[]{:S(2)}, u32[]{:S(2)}) collective-permute-start(bf16[2,16,2304]{2,1,0:T(8,128)(2,1)S(1)} %activate.3), channel_id=1, source_target_pairs={{0,4},{1,5},{2,6},{3,7},{4,0},{5,1},{6,2},{7,3},{8,12},{9,13},{10,... | collective-permute-start | bytes 442376 | tf_op jit(solution)/shard_map/ppermute | solution.py:42
  53.8 9.4 %collective-permute-done.8.received_ref = bf16[2,16,2304]{2,1,0:T(8,128)(2,1)S(1)} collective-permute-done((bf16[2,16,2304]{2,1,0:T(8,128)(2,1)S(1)}, bf16[2,16,2304]{2,1,0:T(8,128)(2,1)S(1)}, u32[]{:S(2)}, u32[]{:S(2)}) %collective-permute-start.8) | collective-permute-done | bytes 147488 | tf_op jit(solution)/shard_map/ppermute | solution.py:42
  63.2 0.1 activate.2
  63.3 0.1 collective-permute-start.9
  63.4 6.1 %collective-permute-done.15 = bf16[2,16,2304]{2,1,0:T(8,128)(2,1)S(1)} collective-permute-done((bf16[2,16,2304]{2,1,0:T(8,128)(2,1)S(1)}, bf16[2,16,2304]{2,1,0:T(8,128)(2,1)S(1)}, u32[]{:S(2)}, u32[]{:S(2)}) %collective-permute-start.15) | collective-permute-done | bytes 147488 | tf_op jit(solution)/shard_map/ppermute | solution.py:42
  69.5 0.1 collective-permute-start.16
  69.6 2.8 %collective-permute-done.9 = bf16[2,16,2304]{2,1,0:T(8,128)(2,1)S(1)} collective-permute-done((bf16[2,16,2304]{2,1,0:T(8,128)(2,1)S(1)}, bf16[2,16,2304]{2,1,0:T(8,128)(2,1)S(1)}, u32[]{:S(2)}, u32[]{:S(2)}) %collective-permute-start.9) | collective-permute-done | bytes 147488 | tf_op jit(solution)/shard_map/ppermute | solution.py:42
  72.4 0.1 collective-permute-start.10
  72.5 7.0 %collective-permute-done.16 = bf16[2,32,2304]{2,1,0:T(8,128)(2,1)S(1)} collective-permute-done((bf16[2,32,2304]{2,1,0:T(8,128)(2,1)S(1)}, bf16[2,32,2304]{2,1,0:T(8,128)(2,1)S(1)}, u32[]{:S(2)}, u32[]{:S(2)}) %collective-permute-start.16) | collective-permute-done | bytes 294944 | tf_op jit(solution)/shard_map/ppermute | solution.py:42
  79.7 5.3 %collective-permute-done.10 = bf16[2,32,2304]{2,1,0:T(8,128)(2,1)S(1)} collective-permute-done((bf16[2,32,2304]{2,1,0:T(8,128)(2,1)S(1)}, bf16[2,32,2304]{2,1,0:T(8,128)(2,1)S(1)}, u32[]{:S(2)}, u32[]{:S(2)}) %collective-permute-start.10) | collective-permute-done | bytes 294944 | tf_op jit(solution)/shard_map/ppermute | solution.py:42
  85.0 0.1 collective-permute-start.11
  85.1 0.3 convolution_convert_fusion.xt_ref
  85.5 4.3 %copy-done.1 = bf16[1280,4608]{1,0:T(8,128)(2,1)S(1)} copy-done((bf16[1280,4608]{1,0:T(8,128)(2,1)S(1)}, bf16[1280,4608]{1,0:T(8,128)(2,1)}, u32[]{:S(2)}) %copy-start.1) | copy-done | bytes 11796504
  89.8 3.2 %input_grads.2.refs_4_ = f32[128,1280]{1,0:T(8,128)S(1)} custom-call(bf16[2,64,2304]{2,1,0:T(8,128)(2,1)S(1)} %pad_maximum_fusion.1.refs_0_.refs_2_, bf16[2,64,2304]{2,1,0:T(8,128)(2,1)S(1)} %collective-permute-done.17.refs_1_.refs_3_, bf16[128,128]{1,0:T(8,128)(2,1)S(1)} %fusion.9.refs_2_, bf16[1280,4608]{1,0:T(8,128)(2,1)S(1)} %copy-done.1), custom_call_target="tpu_custom_call" | custom-call | flops 754974720 | bytes 5898240 | tf_op jit(solution)/shard_map/input_grads/pallas_call | solution.py:122
  93.1 3.3 %input_grads.3 = f32[128,1280]{1,0:T(8,128)S(1)} custom-call(bf16[2,64,2304]{2,1,0:T(8,128)(2,1)S(1)} %pad_maximum_fusion.refs_0_.refs_4_.refs_6_, bf16[2,64,2304]{2,1,0:T(8,128)(2,1)S(1)} %collective-permute-done.11.refs_1_.refs_5_.refs_7_, bf16[128,128]{1,0:T(8,128)(2,1)S(1)} %fusion.9.refs_2_, bf16[1280,4608]{1,0:T(8,128)(2,1)S(1)} %copy-done.1, ...), custom_call_target="tpu_custom_call" | custom-call | flops 754974720 | bytes 5898240 | tf_op jit(solution)/shard_map/input_grads/pallas_call | solution.py:122
  96.5 0.6 collective-permute-start.18
  97.1 0.7 collective-permute-start.19
  97.7 2.3 %collective-permute-start.20 = (bf16[32,1280]{1,0:T(8,128)(2,1)S(1)}, bf16[32,1280]{1,0:T(8,128)(2,1)S(1)}, u32[]{:S(2)}, u32[]{:S(2)}) collective-permute-start(bf16[32,1280]{1,0:T(8,128)(2,1)S(1)} %get-tuple-element.32), channel_id=1, source_target_pairs={{0,24},{8,16},{16,8},{24,0},{1,25},{9,17},{17,9},{25,1},{2,26},{10... | collective-permute-start | bytes 245768 | tf_op jit(solution)/shard_map/ppermute | solution.py:42
  100.0 10.7 %weight_grads.1 = (bf16[1280,4608]{1,0:T(8,128)(2,1)}, bf16[4608,1280]{1,0:T(8,128)(2,1)}) custom-call(bf16[1280,128]{1,0:T(8,128)(2,1)S(1)} %convolution_convert_fusion.xt_ref, bf16[128,1280]{1,0:T(8,128)(2,1)S(1)} %convolution_convert_fusion.1.gs_ref, bf16[2,64,2304]{2,1,0:T(8,128)(2,1)S(1)} %pad_maximum_fusion.1.refs_0_.refs_2_, ...), custom_call_target="tpu_custom_call" | custom-call | flops 3019898880 | bytes 23592960 | tf_op jit(solution)/shard_map/weight_grads/pallas_call | solution.py:171
  110.7 0.7 fusion.8
  (29 shorter events, 0.4 us)
Async XLA Ops:
  0.6 15.4 %copy-start.2 = (bf16[32,1280]{1,0:T(8,128)(2,1)S(1)}, bf16[32,1280]{1,0:T(8,128)(2,1)}, u32[]{:S(2)}) copy-start(bf16[32,1280]{1,0:T(8,128)(2,1)} %param.6) | copy-start | bytes 245764
  0.6 9.7 %collective-permute-start = (bf16[32,1280]{1,0:T(8,128)(2,1)}, bf16[32,1280]{1,0:T(8,128)(2,1)S(1)}, u32[]{:S(2)}, u32[]{:S(2)}) collective-permute-start(bf16[32,1280]{1,0:T(8,128)(2,1)} %param.5), channel_id=1, source_target_pairs={{0,8},{8,0},{16,24},{24,16},{1,9},{9,1},{17,25},{25,17},{2,10},{10... | collective-permute-start | bytes 245768 | tf_op jit(solution)/shard_map/ppermute | solution.py:42
  3.6 6.8 %collective-permute-start.1 = (bf16[32,1280]{1,0:T(8,128)(2,1)}, bf16[32,1280]{1,0:T(8,128)(2,1)S(1)}, u32[]{:S(2)}, u32[]{:S(2)}) collective-permute-start(bf16[32,1280]{1,0:T(8,128)(2,1)} %param.5), channel_id=1, source_target_pairs={{0,16},{8,24},{16,0},{24,8},{1,17},{9,25},{17,1},{25,9},{2,18},{10... | collective-permute-start | bytes 245768 | tf_op jit(solution)/shard_map/ppermute | solution.py:42
  5.2 5.7 %collective-permute-start.2 = (bf16[32,1280]{1,0:T(8,128)(2,1)}, bf16[32,1280]{1,0:T(8,128)(2,1)S(1)}, u32[]{:S(2)}, u32[]{:S(2)}) collective-permute-start(bf16[32,1280]{1,0:T(8,128)(2,1)} %param.5), channel_id=1, source_target_pairs={{0,24},{8,16},{16,8},{24,0},{1,25},{9,17},{17,9},{25,1},{2,26},{10... | collective-permute-start | bytes 245768 | tf_op jit(solution)/shard_map/ppermute | solution.py:42
  5.2 6.0 %collective-permute-start.3 = (bf16[32,1280]{1,0:T(8,128)(2,1)}, bf16[32,1280]{1,0:T(8,128)(2,1)S(1)}, u32[]{:S(2)}, u32[]{:S(2)}) collective-permute-start(bf16[32,1280]{1,0:T(8,128)(2,1)} %param.6), channel_id=1, source_target_pairs={{0,8},{8,0},{16,24},{24,16},{1,9},{9,1},{17,25},{25,17},{2,10},{10... | collective-permute-start | bytes 245768 | tf_op jit(solution)/shard_map/ppermute | solution.py:42
  7.1 4.7 %collective-permute-start.4 = (bf16[32,1280]{1,0:T(8,128)(2,1)}, bf16[32,1280]{1,0:T(8,128)(2,1)S(1)}, u32[]{:S(2)}, u32[]{:S(2)}) collective-permute-start(bf16[32,1280]{1,0:T(8,128)(2,1)} %param.6), channel_id=1, source_target_pairs={{0,16},{8,24},{16,0},{24,8},{1,17},{9,25},{17,1},{25,9},{2,18},{10... | collective-permute-start | bytes 245768 | tf_op jit(solution)/shard_map/ppermute | solution.py:42
  10.4 5.6 %collective-permute-start.5 = (bf16[32,1280]{1,0:T(8,128)(2,1)}, bf16[32,1280]{1,0:T(8,128)(2,1)S(1)}, u32[]{:S(2)}, u32[]{:S(2)}) collective-permute-start(bf16[32,1280]{1,0:T(8,128)(2,1)} %param.6), channel_id=1, source_target_pairs={{0,24},{8,16},{16,8},{24,0},{1,25},{9,17},{17,9},{25,1},{2,26},{10... | collective-permute-start | bytes 245768 | tf_op jit(solution)/shard_map/ppermute | solution.py:42
  16.3 4.4 %copy-start = (bf16[1280,4608]{1,0:T(8,128)(2,1)S(1)}, bf16[1280,4608]{1,0:T(8,128)(2,1)}, u32[]{:S(2)}) copy-start(bf16[1280,4608]{1,0:T(8,128)(2,1)} %refs_3_.3) | copy-start | bytes 35389444
  26.0 6.0 %collective-permute-start.12 = (bf16[2,64,2304]{2,1,0:T(8,128)(2,1)S(1)}, bf16[2,64,2304]{2,1,0:T(8,128)(2,1)S(1)}, u32[]{:S(2)}, u32[]{:S(2)}) collective-permute-start(bf16[2,64,2304]{2,1,0:T(8,128)(2,1)S(1)} %get-tuple-element.24), channel_id=1, source_target_pairs={{0,1},{1,0},{2,3},{3,2},{4,5},{5,4},{6,7},{7,6},{8,9},{9,8},{10,11... | collective-permute-start | bytes 1769480 | tf_op jit(solution)/shard_map/ppermute | solution.py:42
  31.4 2.3 %collective-permute-start.6 = (bf16[2,64,2304]{2,1,0:T(8,128)(2,1)S(1)}, bf16[2,64,2304]{2,1,0:T(8,128)(2,1)S(1)}, u32[]{:S(2)}, u32[]{:S(2)}) collective-permute-start(bf16[2,64,2304]{2,1,0:T(8,128)(2,1)S(1)} %get-tuple-element.18), channel_id=1, source_target_pairs={{0,1},{1,0},{2,3},{3,2},{4,5},{5,4},{6,7},{7,6},{8,9},{9,8},{10,11... | collective-permute-start | bytes 1769480 | tf_op jit(solution)/shard_map/ppermute | solution.py:42
  32.1 9.9 %collective-permute-start.13 = (bf16[2,32,2304]{2,1,0:T(8,128)(2,1)S(1)}, bf16[2,32,2304]{2,1,0:T(8,128)(2,1)S(1)}, u32[]{:S(2)}, u32[]{:S(2)}) collective-permute-start(bf16[2,32,2304]{2,1,0:T(8,128)(2,1)S(1)} %get-tuple-element.26), channel_id=1, source_target_pairs={{0,2},{1,3},{2,0},{3,1},{4,6},{5,7},{6,4},{7,5},{8,10},{9,11},{10,... | collective-permute-start | bytes 884744 | tf_op jit(solution)/shard_map/ppermute | solution.py:42
  33.9 16.7 %collective-permute-start.7 = (bf16[2,32,2304]{2,1,0:T(8,128)(2,1)S(1)}, bf16[2,32,2304]{2,1,0:T(8,128)(2,1)S(1)}, u32[]{:S(2)}, u32[]{:S(2)}) collective-permute-start(bf16[2,32,2304]{2,1,0:T(8,128)(2,1)S(1)} %get-tuple-element.20), channel_id=1, source_target_pairs={{0,2},{1,3},{2,0},{3,1},{4,6},{5,7},{6,4},{7,5},{8,10},{9,11},{10,... | collective-permute-start | bytes 884744 | tf_op jit(solution)/shard_map/ppermute | solution.py:42
  42.1 9.6 %collective-permute-start.14 = (bf16[2,16,2304]{2,1,0:T(8,128)(2,1)S(1)}, bf16[2,16,2304]{2,1,0:T(8,128)(2,1)S(1)}, u32[]{:S(2)}, u32[]{:S(2)}) collective-permute-start(bf16[2,16,2304]{2,1,0:T(8,128)(2,1)S(1)} %get-tuple-element.28), channel_id=1, source_target_pairs={{0,4},{1,5},{2,6},{3,7},{4,0},{5,1},{6,2},{7,3},{8,12},{9,13},{10,... | collective-permute-start | bytes 442376 | tf_op jit(solution)/shard_map/ppermute | solution.py:42
  50.6 12.6 %collective-permute-start.8 = (bf16[2,16,2304]{2,1,0:T(8,128)(2,1)S(1)}, bf16[2,16,2304]{2,1,0:T(8,128)(2,1)S(1)}, u32[]{:S(2)}, u32[]{:S(2)}) collective-permute-start(bf16[2,16,2304]{2,1,0:T(8,128)(2,1)S(1)} %get-tuple-element.22), channel_id=1, source_target_pairs={{0,4},{1,5},{2,6},{3,7},{4,0},{5,1},{6,2},{7,3},{8,12},{9,13},{10,... | collective-permute-start | bytes 442376 | tf_op jit(solution)/shard_map/ppermute | solution.py:42
  51.8 17.7 %collective-permute-start.15 = (bf16[2,16,2304]{2,1,0:T(8,128)(2,1)S(1)}, bf16[2,16,2304]{2,1,0:T(8,128)(2,1)S(1)}, u32[]{:S(2)}, u32[]{:S(2)}) collective-permute-start(bf16[2,16,2304]{2,1,0:T(8,128)(2,1)S(1)} %activate.3), channel_id=1, source_target_pairs={{0,4},{1,5},{2,6},{3,7},{4,0},{5,1},{6,2},{7,3},{8,12},{9,13},{10,... | collective-permute-start | bytes 442376 | tf_op jit(solution)/shard_map/ppermute | solution.py:42
  63.3 9.1 %collective-permute-start.9 = (bf16[2,16,2304]{2,1,0:T(8,128)(2,1)S(1)}, bf16[2,16,2304]{2,1,0:T(8,128)(2,1)S(1)}, u32[]{:S(2)}, u32[]{:S(2)}) collective-permute-start(bf16[2,16,2304]{2,1,0:T(8,128)(2,1)S(1)} %activate.2), channel_id=1, source_target_pairs={{0,4},{1,5},{2,6},{3,7},{4,0},{5,1},{6,2},{7,3},{8,12},{9,13},{10,... | collective-permute-start | bytes 442376 | tf_op jit(solution)/shard_map/ppermute | solution.py:42
  69.5 10.0 %collective-permute-start.16 = (bf16[2,32,2304]{2,1,0:T(8,128)(2,1)S(1)}, bf16[2,32,2304]{2,1,0:T(8,128)(2,1)S(1)}, u32[]{:S(2)}, u32[]{:S(2)}) collective-permute-start(bf16[2,32,2304]{2,1,0:T(8,128)(2,1)S(1)} %pad_maximum_fusion.3), channel_id=1, source_target_pairs={{0,2},{1,3},{2,0},{3,1},{4,6},{5,7},{6,4},{7,5},{8,10},{9,11},{10,... | collective-permute-start | bytes 884744 | tf_op jit(solution)/shard_map/ppermute | solution.py:42
  72.4 12.5 %collective-permute-start.10 = (bf16[2,32,2304]{2,1,0:T(8,128)(2,1)S(1)}, bf16[2,32,2304]{2,1,0:T(8,128)(2,1)S(1)}, u32[]{:S(2)}, u32[]{:S(2)}) collective-permute-start(bf16[2,32,2304]{2,1,0:T(8,128)(2,1)S(1)} %pad_maximum_fusion.2), channel_id=1, source_target_pairs={{0,2},{1,3},{2,0},{3,1},{4,6},{5,7},{6,4},{7,5},{8,10},{9,11},{10,... | collective-permute-start | bytes 884744 | tf_op jit(solution)/shard_map/ppermute | solution.py:42
  79.6 5.9 %collective-permute-start.17 = (bf16[2,64,2304]{2,1,0:T(8,128)(2,1)S(1)}, bf16[2,64,2304]{2,1,0:T(8,128)(2,1)S(1)}, u32[]{:S(2)}, u32[]{:S(2)}) collective-permute-start(bf16[2,64,2304]{2,1,0:T(8,128)(2,1)S(1)} %pad_maximum_fusion.1.refs_0_.refs_2_), channel_id=1, source_target_pairs={{0,1},{1,0},{2,3},{3,2},{4,5},{5,4},{6,7},{7,6},{8,9},{9,8},{10,11... | collective-permute-start | bytes 1769480 | tf_op jit(solution)/shard_map/ppermute | solution.py:42
  85.0 8.1 %collective-permute-start.11 = (bf16[2,64,2304]{2,1,0:T(8,128)(2,1)S(1)}, bf16[2,64,2304]{2,1,0:T(8,128)(2,1)S(1)}, u32[]{:S(2)}, u32[]{:S(2)}) collective-permute-start(bf16[2,64,2304]{2,1,0:T(8,128)(2,1)S(1)} %pad_maximum_fusion.refs_0_.refs_4_.refs_6_), channel_id=1, source_target_pairs={{0,1},{1,0},{2,3},{3,2},{4,5},{5,4},{6,7},{7,6},{8,9},{9,8},{10,11... | collective-permute-start | bytes 1769480 | tf_op jit(solution)/shard_map/ppermute | solution.py:42
  85.5 4.4 %copy-start.1 = (bf16[1280,4608]{1,0:T(8,128)(2,1)S(1)}, bf16[1280,4608]{1,0:T(8,128)(2,1)}, u32[]{:S(2)}) copy-start(bf16[1280,4608]{1,0:T(8,128)(2,1)} %refs_3_.3) | copy-start | bytes 35389444
  96.5 14.2 %collective-permute-start.18 = (bf16[32,1280]{1,0:T(8,128)(2,1)S(1)}, bf16[32,1280]{1,0:T(8,128)(2,1)S(1)}, u32[]{:S(2)}, u32[]{:S(2)}) collective-permute-start(bf16[32,1280]{1,0:T(8,128)(2,1)S(1)} %get-tuple-element.31), channel_id=1, source_target_pairs={{0,8},{8,0},{16,24},{24,16},{1,9},{9,1},{17,25},{25,17},{2,10},{10... | collective-permute-start | bytes 245768 | tf_op jit(solution)/shard_map/ppermute | solution.py:42
  97.1 13.6 %collective-permute-start.19 = (bf16[32,1280]{1,0:T(8,128)(2,1)S(1)}, bf16[32,1280]{1,0:T(8,128)(2,1)S(1)}, u32[]{:S(2)}, u32[]{:S(2)}) collective-permute-start(bf16[32,1280]{1,0:T(8,128)(2,1)S(1)} %get-tuple-element.33), channel_id=1, source_target_pairs={{0,16},{8,24},{16,0},{24,8},{1,17},{9,25},{17,1},{25,9},{2,18},{10... | collective-permute-start | bytes 245768 | tf_op jit(solution)/shard_map/ppermute | solution.py:42
  97.7 13.0 %collective-permute-start.20 = (bf16[32,1280]{1,0:T(8,128)(2,1)S(1)}, bf16[32,1280]{1,0:T(8,128)(2,1)S(1)}, u32[]{:S(2)}, u32[]{:S(2)}) collective-permute-start(bf16[32,1280]{1,0:T(8,128)(2,1)S(1)} %get-tuple-element.32), channel_id=1, source_target_pairs={{0,24},{8,16},{16,8},{24,0},{1,25},{9,17},{17,9},{25,1},{2,26},{10... | collective-permute-start | bytes 245768 | tf_op jit(solution)/shard_map/ppermute | solution.py:42

commit v2 on v0

v2 whole, which is shorter than its diff:
```python
import functools
import math

import jax
import jax.numpy as jnp
from jax import lax
from jax.experimental import pallas as pl
from jax.experimental.pallas import tpu as pltpu
from jax.sharding import PartitionSpec as P

BF16 = jnp.bfloat16
F32 = jnp.float32
GROUPS = 3
BLOCK = 512
VMEM_BYTES = 48 * 1024 * 1024
SMALL_BYTES = 16 * 1024 * 1024
SCALAR = pl.BlockSpec(memory_space=pltpu.SMEM)


def gelu_parts(preact):
    cumul = 0.5 * (1.0 + jax.scipy.special.erf(preact * (1.0 / math.sqrt(2.0))))
    density = jnp.exp(-0.5 * preact * preact) * (1.0 / math.sqrt(2.0 * math.pi))
    return (preact * cumul, cumul + preact * density)


def contract(left, right, left_dim, right_dim):
    return lax.dot_general(
        left,
        right,
        (((left_dim,), (right_dim,)), ((), ())),
        preferred_element_type=F32,
    )


def exchange(array, axis, size, step):
    return lax.ppermute(array, axis, [(i, i ^ step) for i in range(size)])


def whole(*shape):
    return pl.BlockSpec(shape, lambda step: (0,) * len(shape))


def params(size=VMEM_BYTES):
    return pltpu.CompilerParams(vmem_limit_bytes=size)


def cost(flops, size):
    return pl.CostEstimate(flops=flops, bytes_accessed=size, transcendentals=0)


def by_bit(rank_ref, bit, choose):
    side = (rank_ref[0] >> bit) & 1
    for value in range(2):
        pl.when(side == value)(functools.partial(choose, value))


def forward(rank, tokens, w_in, w_out, start, width):
    parts = len(tokens)
    rows, features = tokens[0].shape[1:]
    total = parts * rows
    half = total // 2
    first, steps = start // BLOCK, width // BLOCK

    def kernel(rank_ref, *refs):
        token_refs = refs[:parts]
        wi_ref, wo_ref, keep_ref, send_ref = refs[parts:]

        def rows_of(which):
            return jnp.concatenate([ref[which] for ref in token_refs], axis=0)

        sums = (
            contract(rows_of(0), wi_ref[...], 1, 0),
            contract(rows_of(1), wo_ref[...], 1, 1),
        )

        def choose(core):
            for which, value in enumerate(sums):
                halves = value[:half], value[half:]
                keep_ref[which] = halves[core]
                send_ref[which] = halves[1 - core].astype(BF16)

        by_bit(rank_ref, 0, choose)

    block = pl.BlockSpec((2, half, BLOCK), lambda i: (0, 0, i))
    return pl.pallas_call(
        kernel,
        grid=(steps,),
        out_shape=(
            jax.ShapeDtypeStruct((2, half, width), F32),
            jax.ShapeDtypeStruct((2, half, width), BF16),
        ),
        in_specs=[SCALAR]
        + [whole(2, rows, features)] * parts
        + [
            pl.BlockSpec((features, BLOCK), lambda i: (0, first + i)),
            pl.BlockSpec((BLOCK, features), lambda i: (first + i, 0)),
        ],
        out_specs=(block, block),
        compiler_params=params(),
        cost_estimate=cost(4 * total * features * width, 4 * features * width),
        name="forward",
    )(rank, *tokens, w_in, w_out)


def halve(rank, keep, received, bit):
    _, rows, width = keep.shape
    half = width // 2

    def kernel(rank_ref, keep_ref, received_ref, next_ref, send_ref):
        def choose(side):
            mine = slice(side * half, (side + 1) * half)
            other = slice((1 - side) * half, (2 - side) * half)
            next_ref[...] = keep_ref[:, :, mine] + received_ref[:, :, mine].astype(F32)
            send_ref[...] = (
                keep_ref[:, :, other] + received_ref[:, :, other].astype(F32)
            ).astype(BF16)

        by_bit(rank_ref, bit, choose)

    return pl.pallas_call(
        kernel,
        grid=(1,),
        out_shape=(
            jax.ShapeDtypeStruct((2, rows, half), F32),
            jax.ShapeDtypeStruct((2, rows, half), BF16),
        ),
        in_specs=[SCALAR] + [whole(2, rows, width)] * 2,
        out_specs=(whole(2, rows, half),) * 2,
        compiler_params=params(SMALL_BYTES),
        cost_estimate=cost(2 * rows * width, 12 * rows * width),
        name="halve",
    )(rank, keep, received)


def activate(keep, received):
    def kernel(keep_ref, received_ref, out_ref):
        value, slope = gelu_parts(keep_ref[0] + received_ref[0].astype(F32))
        grad = keep_ref[1] + received_ref[1].astype(F32)
        out_ref[0] = value.astype(BF16)
        out_ref[1] = (grad * slope).astype(BF16)

    return pl.pallas_call(
        kernel,
        grid=(1,),
        out_shape=jax.ShapeDtypeStruct(keep.shape, BF16),
        in_specs=[whole(*keep.shape)] * 2,
        out_specs=whole(*keep.shape),
        compiler_params=params(SMALL_BYTES),
        cost_estimate=cost(20 * keep.size, 8 * keep.size),
        name="activate",
    )(keep, received)


def join(rank, own, received, bit, axis):
    shape = list(own.shape)
    half = shape[axis]
    shape[axis] = 2 * half

    def kernel(rank_ref, own_ref, received_ref, out_ref):
        def choose(side):
            for place, source in ((side, own_ref), (1 - side, received_ref)):
                at = [slice(None)] * 3
                at[axis] = slice(place * half, (place + 1) * half)
                out_ref[tuple(at)] = source[...]

        by_bit(rank_ref, bit, choose)

    return pl.pallas_call(
        kernel,
        grid=(1,),
        out_shape=jax.ShapeDtypeStruct(shape, BF16),
        in_specs=[SCALAR] + [whole(*own.shape)] * 2,
        out_specs=whole(*shape),
        compiler_params=params(SMALL_BYTES),
        cost_estimate=cost(0, 8 * own.size),
        name="join",
    )(rank, own, received)


def reduce_and_activate(rank, keep, send, mp):
    bits = mp.bit_length() - 1
    for bit in range(1, bits):
        keep, send = halve(rank, keep, exchange(send, "mp", mp, 1 << (bit - 1)), bit)
    own = activate(keep, exchange(send, "mp", mp, 1 << (bits - 1)))
    for bit in range(bits - 1, -1, -1):
        own = join(rank, own, exchange(own, "mp", mp, 1 << bit), bit, 2 if bit else 1)
    return own


def input_grads(first_rows, other_rows, w_in, carried, start, width):
    rows, rest = first_rows.shape[1], other_rows.shape[1]
    features = w_in.shape[0]
    first, steps = start // BLOCK, width // BLOCK

    def kernel(*refs):
        own_ref, rest_ref, wi_ref = refs[:3]
        out_ref = refs[-1]
        step = pl.program_id(0)
        grad = jnp.concatenate([own_ref[0], rest_ref[0]], axis=0)
        value = contract(grad, wi_ref[...], 1, 1)

        @pl.when(step == 0)
        def _():
            out_ref[...] = value if carried is None else refs[3][...] + value

        @pl.when(step > 0)
        def _():
            out_ref[...] += value

    return pl.pallas_call(
        kernel,
        grid=(steps,),
        out_shape=jax.ShapeDtypeStruct((rows + rest, features), F32),
        in_specs=[
            pl.BlockSpec((1, rows, BLOCK), lambda i: (1, 0, first + i)),
            pl.BlockSpec((1, rest, BLOCK), lambda i: (1, 0, i)),
            pl.BlockSpec((features, BLOCK), lambda i: (0, first + i)),
        ]
        + ([] if carried is None else [whole(rows + rest, features)]),
        out_specs=whole(rows + rest, features),
        compiler_params=params(),
        cost_estimate=cost(
            2 * (rows + rest) * features * width, 2 * features * width
        ),
        name="input_grads",
    )(first_rows, other_rows, w_in, *([] if carried is None else [carried]))


def weight_grads(xt, gs, first_rows, others, factor):
    features, total = xt.shape
    hidden = first_rows.shape[2]
    rows, rest = first_rows.shape[1], others[0].shape[1]
    groups = len(others)
    steps = hidden // groups // BLOCK

    def kernel(xt_ref, gs_ref, act_ref, grad_ref, *refs):
        in_ref, out_ref = refs[-2:]
        step = pl.program_id(0)

        def work(rest_act_ref, rest_grad_ref):
            act = jnp.concatenate([act_ref[0], rest_act_ref[0]], axis=0)
            grad = jnp.concatenate([grad_ref[0], rest_grad_ref[0]], axis=0)
            turned = act.astype(F32).T.astype(BF16)
            in_ref[...] = (contract(xt_ref[...], grad, 1, 0) * factor).astype(BF16)
            out_ref[...] = (contract(turned, gs_ref[...], 1, 0) * factor).astype(BF16)

        for group in range(groups):
            here = (step >= group * steps) & (step < (group + 1) * steps)
            pl.when(here)(functools.partial(work, *refs[2 * group : 2 * group + 2]))

    def block(group, which):
        def place(i):
            return which, 0, jnp.clip(i - group * steps, 0, steps - 1)

        return pl.BlockSpec((1, rest, BLOCK), place)

    specs, operands = [], []
    for group, other in enumerate(others):
        specs += [block(group, 0), block(group, 1)]
        operands += [other, other]
    return pl.pallas_call(
        kernel,
        grid=(groups * steps,),
        out_shape=(
            jax.ShapeDtypeStruct((features, hidden), BF16),
            jax.ShapeDtypeStruct((hidden, features), BF16),
        ),
        in_specs=[
            whole(features, total),
            whole(total, features),
            pl.BlockSpec((1, rows, BLOCK), lambda i: (0, 0, i)),
            pl.BlockSpec((1, rows, BLOCK), lambda i: (1, 0, i)),
        ]
        + specs,
        out_specs=(
            pl.BlockSpec((features, BLOCK), lambda i: (0, i)),
            pl.BlockSpec((BLOCK, features), lambda i: (i, 0)),
        ),
        compiler_params=params(),
        cost_estimate=cost(4 * total * features * hidden, 4 * features * hidden),
        name="weight_grads",
    )(xt, gs, first_rows, first_rows, *operands)


def local(inputs, out_grads, w_in, w_out, dp, mp):
    hidden = w_in.shape[1]
    width = hidden // GROUPS
    rows = inputs.shape[0]
    total = rows * dp
    factor = 1.0 / math.sqrt(total)
    rank = lax.axis_index("mp").astype(jnp.int32).reshape(1)

    own = jnp.stack([inputs, out_grads])
    others = [exchange(own, "dp", dp, j) for j in range(1, dp)]

    keep, send = forward(rank, [own], w_in, w_out, 0, hidden)
    first_rows = reduce_and_activate(rank, keep, send, mp)
    other_rows = []
    for group in range(GROUPS):
        keep, send = forward(rank, others, w_in, w_out, group * width, width)
        other_rows.append(reduce_and_activate(rank, keep, send, mp))

    partial = None
    for group, other in enumerate(other_rows):
        partial = input_grads(first_rows, other, w_in, partial, group * width, width)
    in_total = partial[:rows]
    for j in range(1, dp):
        part = partial[j * rows : (j + 1) * rows].astype(BF16)
        in_total = in_total + exchange(part, "dp", dp, j).astype(F32)

    tokens = jnp.concatenate([own, *others], axis=1)
    unit = jnp.eye(total, dtype=BF16)
    xt = contract(tokens[0], unit, 0, 1).astype(BF16)
    grads = weight_grads(xt, tokens[1], first_rows, other_rows, factor)
    return (in_total, *grads)


def solution(mesh):
    sizes = dict(mesh.shape)
    return jax.shard_map(
        functools.partial(local, dp=sizes["dp"], mp=sizes["mp"]),
        mesh=mesh,
        in_specs=(P("dp", "mp"), P("dp", "mp"), P("mp", "dp"), P("dp", "mp")),
        out_specs=(P("dp", "mp"), P("mp", "dp"), P("dp", "mp")),
        check_vma=False,
    )
```

time: 196 us -> 114 us (0.58)
  waiting for transfers between devices: 107 us -> 26.1 us
  Pallas kernels: 0 us -> 52 us
  matrix products: 34.4 us -> 0.27 us
  starting transfers between devices: 0.08 us -> 32 us
  blocking collectives: 19.9 us -> 0 us
  local copies, waits for them, and re-layouts: 16.5 us -> 0.05 us
  between operations: 14 us -> 1.05 us
    psum x1 -> x0, waiting for transfers between devices: 107 us -> none  [local(): preact, grad_act = lax.psum((partial_pre, partial_grad), 'mp')]
    pallas_call x0 -> x32, Pallas kernels: none -> 52 us  [the longest x4 27.6 us: forward(): pl.pallas_call(kernel, grid=(steps,), out_shape=(jax.ShapeDtypeStruct((2,...]
    dot_general x5 -> x1, matrix products: 34.4 us -> 0.27 us  [contract(): lax.dot_general(left, right, (((left_dim,), (right_dim,)), ((), ())), pre...]
    ppermute x0 -> x30, starting transfers between devices: none -> 32 us  [exchange(): return lax.ppermute(array, axis, [(i, i ^ step) for i in range(size)])]
    ppermute x0 -> x30, waiting for transfers between devices: none -> 26.1 us  [exchange(): return lax.ppermute(array, axis, [(i, i ^ step) for i in range(size)])]
    all_gather x2 -> x0, blocking collectives: 19.9 us -> none  [the longest x1 11 us: local(): lax.all_gather(out_grads, 'dp', axis=0, tiled=True)]
    unnamed x5 -> x4, local copies, waits for them, and re-layouts: 16.5 us -> 0.01 us
    convert_element_type x1 -> x0, other arithmetic: 2.83 us -> none  [finish(): grad_preact = (grad_act * gelu_slope).astype(jnp.bfloat16)]
  transfers between devices with their start and end apart: 2 -> 30, of which waited for: 1 -> 12; matrix products, arithmetic and copies ran while one was open for 15% -> 0% of each run, Pallas kernels for 0% -> 42%
where the time goes in v2:
time: 114 us; the launch traced here: 113 us
  Pallas kernels  52 us (46%)
  starting transfers between devices  32 us (28%)
  waiting for transfers between devices  26.1 us (23%)
  other arithmetic  1.73 us (2%)
    ppermute x30, starting transfers between devices, exchange(): return lax.ppermute(array, axis, [(i, i ^ step) for i in range(size)])  32 us
    pallas_call x4, Pallas kernels, forward(): pl.pallas_call(kernel, grid=(steps,), out_shape=(jax.ShapeDtypeStruct((2,...  27.6 us
    ppermute x30, waiting for transfers between devices, exchange(): return lax.ppermute(array, axis, [(i, i ^ step) for i in range(size)])  26.1 us
    pallas_call x1, Pallas kernels, weight_grads(): pl.pallas_call(kernel, grid=(groups * steps,), out_shape=(jax.ShapeDtypeS...  11.7 us
    pallas_call x3, Pallas kernels, input_grads(): pl.pallas_call(kernel, grid=(steps,), out_shape=jax.ShapeDtypeStruct((row...  11.7 us
  transfers between devices with their start and end apart: 30, of which 12 were waited for; matrix products, arithmetic and copies ran while one was open for 0% of the time, Pallas kernels for 42%

profile of v2, /device:TPU:0, one launch (start us, length us, event | category | flops | bytes accessed | tf_op | source)
XLA Modules:
  0.0 113.1 jit_solution(1182857663576496024)
XLA Ops:
  0.6 0.9 pad_maximum_fusion.1.refs_0_
  1.6 3.0 %collective-permute-start.6 = (bf16[2,32,1280]{2,1,0:T(8,128)(2,1)S(1)}, bf16[2,32,1280]{2,1,0:T(8,128)(2,1)S(1)}, u32[]{:S(2)}, u32[]{:S(2)}) collective-permute-start(bf16[2,32,1280]{2,1,0:T(8,128)(2,1)S(1)} %pad_maximum_fusion.1.refs_0_), channel_id=1, source_target_pairs={{0,8},{8,0},{16,24},{24,16},{1,9},{9,1},{17,25},{25,17},{2,10},{10... | collective-permute-start | bytes 491528 | tf_op jit(solution)/shard_map/ppermute | solution.py:36
  4.6 1.5 %collective-permute-start.7 = (bf16[2,32,1280]{2,1,0:T(8,128)(2,1)S(1)}, bf16[2,32,1280]{2,1,0:T(8,128)(2,1)S(1)}, u32[]{:S(2)}, u32[]{:S(2)}) collective-permute-start(bf16[2,32,1280]{2,1,0:T(8,128)(2,1)S(1)} %pad_maximum_fusion.1.refs_0_), channel_id=1, source_target_pairs={{0,16},{8,24},{16,0},{24,8},{1,17},{9,25},{17,1},{25,9},{2,18},{10... | collective-permute-start | bytes 491528 | tf_op jit(solution)/shard_map/ppermute | solution.py:36
  6.1 12.6 %forward.4 = (f32[2,16,4608]{2,1,0:T(8,128)S(1)}, bf16[2,16,4608]{2,1,0:T(8,128)(2,1)S(1)}) custom-call(s32[1]{0:T(128)} %bitcast.rank_ref, bf16[2,32,1280]{2,1,0:T(8,128)(2,1)S(1)} %pad_maximum_fusion.1.refs_0_, bf16[1280,4608]{1,0:T(8,128)(2,1)} %refs_2_.7, bf16[4608,1280]{1,0:T(8,128)(2,1)} %refs_4_.5), custom_call_target="tpu_custom_call" | custom-call | flops 754974720 | bytes 23592960 | tf_op jit(solution)/shard_map/forward/pallas_call | solution.py:85
  18.7 0.1 collective-permute-start
  18.8 5.0 %forward.7 = (f32[2,48,1536]{2,1,0:T(8,128)S(1)}, bf16[2,48,1536]{2,1,0:T(8,128)(2,1)S(1)}) custom-call(s32[1]{0:T(128)} %bitcast.rank_ref, bf16[2,32,1280]{2,1,0:T(8,128)(2,1)S(1)} %collective-permute-done.6.refs_0_, bf16[2,32,1280]{2,1,0:T(8,128)(2,1)S(1)} %collective-permute-done.7.refs_1_, bf16[2,32,1280]{2,1,0:T(8,128)(2,1)S(1)} %collective-permute-done.8.refs_2_, ...), custom_call_target="tpu_custom_call" | custom-call | flops 754974720 | bytes 7864320 | tf_op jit(solution)/shard_map/forward/pallas_call | solution.py:85
  23.8 0.6 collective-permute-start.21
  24.4 5.0 %forward.6 = (f32[2,48,1536]{2,1,0:T(8,128)S(1)}, bf16[2,48,1536]{2,1,0:T(8,128)(2,1)S(1)}) custom-call(s32[1]{0:T(128)} %bitcast.rank_ref, bf16[2,32,1280]{2,1,0:T(8,128)(2,1)S(1)} %collective-permute-done.6.refs_0_, bf16[2,32,1280]{2,1,0:T(8,128)(2,1)S(1)} %collective-permute-done.7.refs_1_, bf16[2,32,1280]{2,1,0:T(8,128)(2,1)S(1)} %collective-permute-done.8.refs_2_, ...), custom_call_target="tpu_custom_call" | custom-call | flops 754974720 | bytes 7864320 | tf_op jit(solution)/shard_map/forward/pallas_call | solution.py:85
  29.4 0.1 collective-permute-start.15
  29.5 5.0 %forward.5 = (f32[2,48,1536]{2,1,0:T(8,128)S(1)}, bf16[2,48,1536]{2,1,0:T(8,128)(2,1)S(1)}) custom-call(s32[1]{0:T(128)} %bitcast.rank_ref, bf16[2,32,1280]{2,1,0:T(8,128)(2,1)S(1)} %collective-permute-done.6.refs_0_, bf16[2,32,1280]{2,1,0:T(8,128)(2,1)S(1)} %collective-permute-done.7.refs_1_, bf16[2,32,1280]{2,1,0:T(8,128)(2,1)S(1)} %collective-permute-done.8.refs_2_, ...), custom_call_target="tpu_custom_call" | custom-call | flops 754974720 | bytes 7864320 | tf_op jit(solution)/shard_map/forward/pallas_call | solution.py:85
  34.6 0.5 collective-permute-start.9
  35.2 2.1 %collective-permute-start.1 = (bf16[2,16,2304]{2,1,0:T(8,128)(2,1)S(1)}, bf16[2,16,2304]{2,1,0:T(8,128)(2,1)S(1)}, u32[]{:S(2)}, u32[]{:S(2)}) collective-permute-start(bf16[2,16,2304]{2,1,0:T(8,128)(2,1)S(1)} %get-tuple-element.32), channel_id=1, source_target_pairs={{0,2},{1,3},{2,0},{3,1},{4,6},{5,7},{6,4},{7,5},{8,10},{9,11},{10,... | collective-permute-start | bytes 442376 | tf_op jit(solution)/shard_map/ppermute | solution.py:36
  37.3 0.1 collective-permute-start.22
  37.5 2.1 %collective-permute-start.16 = (bf16[2,48,768]{2,1,0:T(8,128)(2,1)S(1)}, bf16[2,48,768]{2,1,0:T(8,128)(2,1)S(1)}, u32[]{:S(2)}, u32[]{:S(2)}) collective-permute-start(bf16[2,48,768]{2,1,0:T(8,128)(2,1)S(1)} %get-tuple-element.44), channel_id=1, source_target_pairs={{0,2},{1,3},{2,0},{3,1},{4,6},{5,7},{6,4},{7,5},{8,10},{9,11},{10,... | collective-permute-start | bytes 442376 | tf_op jit(solution)/shard_map/ppermute | solution.py:36
  39.6 0.1 collective-permute-start.10
  39.7 2.2 %collective-permute-done.1.received_ref = bf16[2,16,2304]{2,1,0:T(8,128)(2,1)S(1)} collective-permute-done((bf16[2,16,2304]{2,1,0:T(8,128)(2,1)S(1)}, bf16[2,16,2304]{2,1,0:T(8,128)(2,1)S(1)}, u32[]{:S(2)}, u32[]{:S(2)}) %collective-permute-start.1) | collective-permute-done | bytes 147488 | tf_op jit(solution)/shard_map/ppermute | solution.py:36
  42.0 3.1 %collective-permute-start.2 = (bf16[2,16,1152]{2,1,0:T(8,128)(2,1)S(1)}, bf16[2,16,1152]{2,1,0:T(8,128)(2,1)S(1)}, u32[]{:S(2)}, u32[]{:S(2)}) collective-permute-start(bf16[2,16,1152]{2,1,0:T(8,128)(2,1)S(1)} %get-tuple-element.34), channel_id=1, source_target_pairs={{0,4},{1,5},{2,6},{3,7},{4,0},{5,1},{6,2},{7,3},{8,12},{9,13},{10,... | collective-permute-start | bytes 221192 | tf_op jit(solution)/shard_map/ppermute | solution.py:36
  45.1 0.8 collective-permute-done.22.received_ref
  45.9 2.3 %collective-permute-start.23 = (bf16[2,48,384]{2,1,0:T(8,128)(2,1)S(1)}, bf16[2,48,384]{2,1,0:T(8,128)(2,1)S(1)}, u32[]{:S(2)}, u32[]{:S(2)}) collective-permute-start(bf16[2,48,384]{2,1,0:T(8,128)(2,1)S(1)} %get-tuple-element.52), channel_id=1, source_target_pairs={{0,4},{1,5},{2,6},{3,7},{4,0},{5,1},{6,2},{7,3},{8,12},{9,13},{10,... | collective-permute-start | bytes 221192 | tf_op jit(solution)/shard_map/ppermute | solution.py:36
  48.3 3.1 %collective-permute-done.16.received_ref = bf16[2,48,768]{2,1,0:T(8,128)(2,1)S(1)} collective-permute-done((bf16[2,48,768]{2,1,0:T(8,128)(2,1)S(1)}, bf16[2,48,768]{2,1,0:T(8,128)(2,1)S(1)}, u32[]{:S(2)}, u32[]{:S(2)}) %collective-permute-start.16) | collective-permute-done | bytes 147488 | tf_op jit(solution)/shard_map/ppermute | solution.py:36
  51.5 1.5 %collective-permute-start.17 = (bf16[2,48,384]{2,1,0:T(8,128)(2,1)S(1)}, bf16[2,48,384]{2,1,0:T(8,128)(2,1)S(1)}, u32[]{:S(2)}, u32[]{:S(2)}) collective-permute-start(bf16[2,48,384]{2,1,0:T(8,128)(2,1)S(1)} %get-tuple-element.46), channel_id=1, source_target_pairs={{0,4},{1,5},{2,6},{3,7},{4,0},{5,1},{6,2},{7,3},{8,12},{9,13},{10,... | collective-permute-start | bytes 221192 | tf_op jit(solution)/shard_map/ppermute | solution.py:36
  53.0 3.2 %collective-permute-start.3 = (bf16[2,16,1152]{2,1,0:T(8,128)(2,1)S(1)}, bf16[2,16,1152]{2,1,0:T(8,128)(2,1)S(1)}, u32[]{:S(2)}, u32[]{:S(2)}) collective-permute-start(bf16[2,16,1152]{2,1,0:T(8,128)(2,1)S(1)} %activate.4.own_ref), channel_id=1, source_target_pairs={{0,4},{1,5},{2,6},{3,7},{4,0},{5,1},{6,2},{7,3},{8,12},{9,13},{10,... | collective-permute-start | bytes 221192 | tf_op jit(solution)/shard_map/ppermute | solution.py:36
  56.2 0.1 collective-permute-start.11
  56.4 3.0 %collective-permute-start.24 = (bf16[2,48,384]{2,1,0:T(8,128)(2,1)S(1)}, bf16[2,48,384]{2,1,0:T(8,128)(2,1)S(1)}, u32[]{:S(2)}, u32[]{:S(2)}) collective-permute-start(bf16[2,48,384]{2,1,0:T(8,128)(2,1)S(1)} %activate.7.own_ref), channel_id=1, source_target_pairs={{0,4},{1,5},{2,6},{3,7},{4,0},{5,1},{6,2},{7,3},{8,12},{9,13},{10,... | collective-permute-start | bytes 221192 | tf_op jit(solution)/shard_map/ppermute | solution.py:36
  59.3 4.1 %collective-permute-done.17.received_ref = bf16[2,48,384]{2,1,0:T(8,128)(2,1)S(1)} collective-permute-done((bf16[2,48,384]{2,1,0:T(8,128)(2,1)S(1)}, bf16[2,48,384]{2,1,0:T(8,128)(2,1)S(1)}, u32[]{:S(2)}, u32[]{:S(2)}) %collective-permute-start.17) | collective-permute-done | bytes 73760 | tf_op jit(solution)/shard_map/ppermute | solution.py:36
  63.6 1.4 %collective-permute-done.3.received_ref = bf16[2,16,1152]{2,1,0:T(8,128)(2,1)S(1)} collective-permute-done((bf16[2,16,1152]{2,1,0:T(8,128)(2,1)S(1)}, bf16[2,16,1152]{2,1,0:T(8,128)(2,1)S(1)}, u32[]{:S(2)}, u32[]{:S(2)}) %collective-permute-start.3) | collective-permute-done | bytes 73760 | tf_op jit(solution)/shard_map/ppermute | solution.py:36
  65.0 2.6 %collective-permute-start.4 = (bf16[2,16,2304]{2,1,0:T(8,128)(2,1)S(1)}, bf16[2,16,2304]{2,1,0:T(8,128)(2,1)S(1)}, u32[]{:S(2)}, u32[]{:S(2)}) collective-permute-start(bf16[2,16,2304]{2,1,0:T(8,128)(2,1)S(1)} %join.12.own_ref), channel_id=1, source_target_pairs={{0,2},{1,3},{2,0},{3,1},{4,6},{5,7},{6,4},{7,5},{8,10},{9,11},{10,... | collective-permute-start | bytes 442376 | tf_op jit(solution)/shard_map/ppermute | solution.py:36
  67.6 0.6 collective-permute-done.11.received_ref
  68.3 0.9 collective-permute-start.12
  69.2 1.4 %collective-permute-done.24.received_ref = bf16[2,48,384]{2,1,0:T(8,128)(2,1)S(1)} collective-permute-done((bf16[2,48,384]{2,1,0:T(8,128)(2,1)S(1)}, bf16[2,48,384]{2,1,0:T(8,128)(2,1)S(1)}, u32[]{:S(2)}, u32[]{:S(2)}) %collective-permute-start.24) | collective-permute-done | bytes 73760 | tf_op jit(solution)/shard_map/ppermute | solution.py:36
  70.7 0.9 collective-permute-start.25
  71.6 1.0 collective-permute-done.18.received_ref
  72.6 0.2 collective-permute-start.19
  72.9 3.3 %collective-permute-done.4.received_ref = bf16[2,16,2304]{2,1,0:T(8,128)(2,1)S(1)} collective-permute-done((bf16[2,16,2304]{2,1,0:T(8,128)(2,1)S(1)}, bf16[2,16,2304]{2,1,0:T(8,128)(2,1)S(1)}, u32[]{:S(2)}, u32[]{:S(2)}) %collective-permute-start.4) | collective-permute-done | bytes 147488 | tf_op jit(solution)/shard_map/ppermute | solution.py:36
  76.2 0.1 collective-permute-start.5
  76.4 2.9 %collective-permute-done.25.received_ref = bf16[2,48,768]{2,1,0:T(8,128)(2,1)S(1)} collective-permute-done((bf16[2,48,768]{2,1,0:T(8,128)(2,1)S(1)}, bf16[2,48,768]{2,1,0:T(8,128)(2,1)S(1)}, u32[]{:S(2)}, u32[]{:S(2)}) %collective-permute-start.25) | collective-permute-done | bytes 147488 | tf_op jit(solution)/shard_map/ppermute | solution.py:36
  79.3 0.1 collective-permute-start.26
  79.4 3.1 %collective-permute-done.19.received_ref = bf16[2,48,768]{2,1,0:T(8,128)(2,1)S(1)} collective-permute-done((bf16[2,48,768]{2,1,0:T(8,128)(2,1)S(1)}, bf16[2,48,768]{2,1,0:T(8,128)(2,1)S(1)}, u32[]{:S(2)}, u32[]{:S(2)}) %collective-permute-start.19) | collective-permute-done | bytes 147488 | tf_op jit(solution)/shard_map/ppermute | solution.py:36
  82.6 2.1 %collective-permute-done.13.received_ref = bf16[2,48,768]{2,1,0:T(8,128)(2,1)S(1)} collective-permute-done((bf16[2,48,768]{2,1,0:T(8,128)(2,1)S(1)}, bf16[2,48,768]{2,1,0:T(8,128)(2,1)S(1)}, u32[]{:S(2)}, u32[]{:S(2)}) %collective-permute-start.13) | collective-permute-done | bytes 147488 | tf_op jit(solution)/shard_map/ppermute | solution.py:36
  84.8 0.3 convolution_convert_fusion.xt_ref
  85.3 3.9 %input_grads.3.refs_3_ = f32[128,1280]{1,0:T(8,128)S(1)} custom-call(bf16[2,32,4608]{2,1,0:T(8,128)(2,1)S(1)} %join.14.refs_0_.act_ref.grad_ref, bf16[2,96,1536]{2,1,0:T(8,128)(2,1)S(1)} %join.23.refs_1_.refs_0_, bf16[1280,4608]{1,0:T(8,128)(2,1)} %refs_2_.7), custom_call_target="tpu_custom_call" | custom-call | flops 503316480 | bytes 3932160 | tf_op jit(solution)/shard_map/input_grads/pallas_call | solution.py:210
  89.1 3.9 %input_grads.4.refs_3_ = f32[128,1280]{1,0:T(8,128)S(1)} custom-call(bf16[2,32,4608]{2,1,0:T(8,128)(2,1)S(1)} %join.14.refs_0_.act_ref.grad_ref, bf16[2,96,1536]{2,1,0:T(8,128)(2,1)S(1)} %join.20.refs_1_.refs_2_.refs_3_, bf16[1280,4608]{1,0:T(8,128)(2,1)} %refs_2_.7, f32[128,1280]{1,0:T(8,128)S(1)} %input_grads.3.refs_3_), custom_call_target="tpu_custom_call" | custom-call | flops 503316480 | bytes 3932160 | tf_op jit(solution)/shard_map/input_grads/pallas_call | solution.py:210
  93.1 3.9 %input_grads.5 = f32[128,1280]{1,0:T(8,128)S(1)} custom-call(bf16[2,32,4608]{2,1,0:T(8,128)(2,1)S(1)} %join.14.refs_0_.act_ref.grad_ref, bf16[2,96,1536]{2,1,0:T(8,128)(2,1)S(1)} %join.17.refs_1_.refs_4_.refs_5_, bf16[1280,4608]{1,0:T(8,128)(2,1)} %refs_2_.7, f32[128,1280]{1,0:T(8,128)S(1)} %input_grads.4.refs_3_), custom_call_target="tpu_custom_call" | custom-call | flops 503316480 | bytes 3932160 | tf_op jit(solution)/shard_map/input_grads/pallas_call | solution.py:210
  97.1 1.3 %collective-permute-start.27 = (bf16[32,1280]{1,0:T(8,128)(2,1)S(1)}, bf16[32,1280]{1,0:T(8,128)(2,1)S(1)}, u32[]{:S(2)}, u32[]{:S(2)}) collective-permute-start(bf16[32,1280]{1,0:T(8,128)(2,1)S(1)} %get-tuple-element.55), channel_id=1, source_target_pairs={{0,8},{8,0},{16,24},{24,16},{1,9},{9,1},{17,25},{25,17},{2,10},{10... | collective-permute-start | bytes 245768 | tf_op jit(solution)/shard_map/ppermute | solution.py:36
  98.5 1.5 %collective-permute-start.28 = (bf16[32,1280]{1,0:T(8,128)(2,1)S(1)}, bf16[32,1280]{1,0:T(8,128)(2,1)S(1)}, u32[]{:S(2)}, u32[]{:S(2)}) collective-permute-start(bf16[32,1280]{1,0:T(8,128)(2,1)S(1)} %get-tuple-element.57), channel_id=1, source_target_pairs={{0,16},{8,24},{16,0},{24,8},{1,17},{9,25},{17,1},{25,9},{2,18},{10... | collective-permute-start | bytes 245768 | tf_op jit(solution)/shard_map/ppermute | solution.py:36
  100.0 0.7 collective-permute-start.29
  100.7 11.7 %weight_grads.1 = (bf16[1280,4608]{1,0:T(8,128)(2,1)}, bf16[4608,1280]{1,0:T(8,128)(2,1)}) custom-call(bf16[1280,128]{1,0:T(8,128)(2,1)S(1)} %convolution_convert_fusion.xt_ref, bf16[128,1280]{1,0:T(8,128)(2,1)S(1)} %slice_bitcast_fusion.gs_ref, bf16[2,32,4608]{2,1,0:T(8,128)(2,1)S(1)} %join.14.refs_0_.act_ref.grad_ref, ...), custom_call_target="tpu_custom_call" | custom-call | flops 3019898880 | bytes 23592960 | tf_op jit(solution)/shard_map/weight_grads/pallas_call | solution.py:261
  112.4 0.7 fusion.1
  (55 shorter events, 1.4 us)
Async XLA Ops:
  1.6 17.2 %collective-permute-start.6 = (bf16[2,32,1280]{2,1,0:T(8,128)(2,1)S(1)}, bf16[2,32,1280]{2,1,0:T(8,128)(2,1)S(1)}, u32[]{:S(2)}, u32[]{:S(2)}) collective-permute-start(bf16[2,32,1280]{2,1,0:T(8,128)(2,1)S(1)} %pad_maximum_fusion.1.refs_0_), channel_id=1, source_target_pairs={{0,8},{8,0},{16,24},{24,16},{1,9},{9,1},{17,25},{25,17},{2,10},{10... | collective-permute-start | bytes 491528 | tf_op jit(solution)/shard_map/ppermute | solution.py:36
  4.6 14.2 %collective-permute-start.7 = (bf16[2,32,1280]{2,1,0:T(8,128)(2,1)S(1)}, bf16[2,32,1280]{2,1,0:T(8,128)(2,1)S(1)}, u32[]{:S(2)}, u32[]{:S(2)}) collective-permute-start(bf16[2,32,1280]{2,1,0:T(8,128)(2,1)S(1)} %pad_maximum_fusion.1.refs_0_), channel_id=1, source_target_pairs={{0,16},{8,24},{16,0},{24,8},{1,17},{9,25},{17,1},{25,9},{2,18},{10... | collective-permute-start | bytes 491528 | tf_op jit(solution)/shard_map/ppermute | solution.py:36
  6.1 12.7 %collective-permute-start.8 = (bf16[2,32,1280]{2,1,0:T(8,128)(2,1)S(1)}, bf16[2,32,1280]{2,1,0:T(8,128)(2,1)S(1)}, u32[]{:S(2)}, u32[]{:S(2)}) collective-permute-start(bf16[2,32,1280]{2,1,0:T(8,128)(2,1)S(1)} %pad_maximum_fusion.1.refs_0_), channel_id=1, source_target_pairs={{0,24},{8,16},{16,8},{24,0},{1,25},{9,17},{17,9},{25,1},{2,26},{10... | collective-permute-start | bytes 491528 | tf_op jit(solution)/shard_map/ppermute | solution.py:36
  18.7 16.4 %collective-permute-start = (bf16[2,16,4608]{2,1,0:T(8,128)(2,1)S(1)}, bf16[2,16,4608]{2,1,0:T(8,128)(2,1)S(1)}, u32[]{:S(2)}, u32[]{:S(2)}) collective-permute-start(bf16[2,16,4608]{2,1,0:T(8,128)(2,1)S(1)} %get-tuple-element.30), channel_id=1, source_target_pairs={{0,1},{1,0},{2,3},{3,2},{4,5},{5,4},{6,7},{7,6},{8,9},{9,8},{10,11... | collective-permute-start | bytes 884744 | tf_op jit(solution)/shard_map/ppermute | solution.py:36
  23.8 13.4 %collective-permute-start.21 = (bf16[2,48,1536]{2,1,0:T(8,128)(2,1)S(1)}, bf16[2,48,1536]{2,1,0:T(8,128)(2,1)S(1)}, u32[]{:S(2)}, u32[]{:S(2)}) collective-permute-start(bf16[2,48,1536]{2,1,0:T(8,128)(2,1)S(1)} %get-tuple-element.48), channel_id=1, source_target_pairs={{0,1},{1,0},{2,3},{3,2},{4,5},{5,4},{6,7},{7,6},{8,9},{9,8},{10,11... | collective-permute-start | bytes 884744 | tf_op jit(solution)/shard_map/ppermute | solution.py:36
  29.4 8.0 %collective-permute-start.15 = (bf16[2,48,1536]{2,1,0:T(8,128)(2,1)S(1)}, bf16[2,48,1536]{2,1,0:T(8,128)(2,1)S(1)}, u32[]{:S(2)}, u32[]{:S(2)}) collective-permute-start(bf16[2,48,1536]{2,1,0:T(8,128)(2,1)S(1)} %get-tuple-element.42), channel_id=1, source_target_pairs={{0,1},{1,0},{2,3},{3,2},{4,5},{5,4},{6,7},{7,6},{8,9},{9,8},{10,11... | collective-permute-start | bytes 884744 | tf_op jit(solution)/shard_map/ppermute | solution.py:36
  34.6 5.0 %collective-permute-start.9 = (bf16[2,48,1536]{2,1,0:T(8,128)(2,1)S(1)}, bf16[2,48,1536]{2,1,0:T(8,128)(2,1)S(1)}, u32[]{:S(2)}, u32[]{:S(2)}) collective-permute-start(bf16[2,48,1536]{2,1,0:T(8,128)(2,1)S(1)} %get-tuple-element.36), channel_id=1, source_target_pairs={{0,1},{1,0},{2,3},{3,2},{4,5},{5,4},{6,7},{7,6},{8,9},{9,8},{10,11... | collective-permute-start | bytes 884744 | tf_op jit(solution)/shard_map/ppermute | solution.py:36
  35.2 6.7 %collective-permute-start.1 = (bf16[2,16,2304]{2,1,0:T(8,128)(2,1)S(1)}, bf16[2,16,2304]{2,1,0:T(8,128)(2,1)S(1)}, u32[]{:S(2)}, u32[]{:S(2)}) collective-permute-start(bf16[2,16,2304]{2,1,0:T(8,128)(2,1)S(1)} %get-tuple-element.32), channel_id=1, source_target_pairs={{0,2},{1,3},{2,0},{3,1},{4,6},{5,7},{6,4},{7,5},{8,10},{9,11},{10,... | collective-permute-start | bytes 442376 | tf_op jit(solution)/shard_map/ppermute | solution.py:36
  37.3 8.5 %collective-permute-start.22 = (bf16[2,48,768]{2,1,0:T(8,128)(2,1)S(1)}, bf16[2,48,768]{2,1,0:T(8,128)(2,1)S(1)}, u32[]{:S(2)}, u32[]{:S(2)}) collective-permute-start(bf16[2,48,768]{2,1,0:T(8,128)(2,1)S(1)} %get-tuple-element.50), channel_id=1, source_target_pairs={{0,2},{1,3},{2,0},{3,1},{4,6},{5,7},{6,4},{7,5},{8,10},{9,11},{10,... | collective-permute-start | bytes 442376 | tf_op jit(solution)/shard_map/ppermute | solution.py:36
  37.5 13.9 %collective-permute-start.16 = (bf16[2,48,768]{2,1,0:T(8,128)(2,1)S(1)}, bf16[2,48,768]{2,1,0:T(8,128)(2,1)S(1)}, u32[]{:S(2)}, u32[]{:S(2)}) collective-permute-start(bf16[2,48,768]{2,1,0:T(8,128)(2,1)S(1)} %get-tuple-element.44), channel_id=1, source_target_pairs={{0,2},{1,3},{2,0},{3,1},{4,6},{5,7},{6,4},{7,5},{8,10},{9,11},{10,... | collective-permute-start | bytes 442376 | tf_op jit(solution)/shard_map/ppermute | solution.py:36
  39.6 16.5 %collective-permute-start.10 = (bf16[2,48,768]{2,1,0:T(8,128)(2,1)S(1)}, bf16[2,48,768]{2,1,0:T(8,128)(2,1)S(1)}, u32[]{:S(2)}, u32[]{:S(2)}) collective-permute-start(bf16[2,48,768]{2,1,0:T(8,128)(2,1)S(1)} %get-tuple-element.38), channel_id=1, source_target_pairs={{0,2},{1,3},{2,0},{3,1},{4,6},{5,7},{6,4},{7,5},{8,10},{9,11},{10,... | collective-permute-start | bytes 442376 | tf_op jit(solution)/shard_map/ppermute | solution.py:36
  42.0 11.0 %collective-permute-start.2 = (bf16[2,16,1152]{2,1,0:T(8,128)(2,1)S(1)}, bf16[2,16,1152]{2,1,0:T(8,128)(2,1)S(1)}, u32[]{:S(2)}, u32[]{:S(2)}) collective-permute-start(bf16[2,16,1152]{2,1,0:T(8,128)(2,1)S(1)} %get-tuple-element.34), channel_id=1, source_target_pairs={{0,4},{1,5},{2,6},{3,7},{4,0},{5,1},{6,2},{7,3},{8,12},{9,13},{10,... | collective-permute-start | bytes 221192 | tf_op jit(solution)/shard_map/ppermute | solution.py:36
  45.9 10.4 %collective-permute-start.23 = (bf16[2,48,384]{2,1,0:T(8,128)(2,1)S(1)}, bf16[2,48,384]{2,1,0:T(8,128)(2,1)S(1)}, u32[]{:S(2)}, u32[]{:S(2)}) collective-permute-start(bf16[2,48,384]{2,1,0:T(8,128)(2,1)S(1)} %get-tuple-element.52), channel_id=1, source_target_pairs={{0,4},{1,5},{2,6},{3,7},{4,0},{5,1},{6,2},{7,3},{8,12},{9,13},{10,... | collective-permute-start | bytes 221192 | tf_op jit(solution)/shard_map/ppermute | solution.py:36
  51.5 21.4 %copy-start = (bf16[32,1280]{1,0:T(8,128)(2,1)S(1)}, bf16[32,1280]{1,0:T(8,128)(2,1)}, u32[]{:S(2)}) copy-start(bf16[32,1280]{1,0:T(8,128)(2,1)} %param.5) | copy-start | bytes 245764
  51.5 21.4 %copy-start.1 = (bf16[32,1280]{1,0:T(8,128)(2,1)S(1)}, bf16[32,1280]{1,0:T(8,128)(2,1)}, u32[]{:S(2)}) copy-start(bf16[32,1280]{1,0:T(8,128)(2,1)} %param.4) | copy-start | bytes 245764
  51.5 11.9 %collective-permute-start.17 = (bf16[2,48,384]{2,1,0:T(8,128)(2,1)S(1)}, bf16[2,48,384]{2,1,0:T(8,128)(2,1)S(1)}, u32[]{:S(2)}, u32[]{:S(2)}) collective-permute-start(bf16[2,48,384]{2,1,0:T(8,128)(2,1)S(1)} %get-tuple-element.46), channel_id=1, source_target_pairs={{0,4},{1,5},{2,6},{3,7},{4,0},{5,1},{6,2},{7,3},{8,12},{9,13},{10,... | collective-permute-start | bytes 221192 | tf_op jit(solution)/shard_map/ppermute | solution.py:36
  53.0 12.0 %collective-permute-start.3 = (bf16[2,16,1152]{2,1,0:T(8,128)(2,1)S(1)}, bf16[2,16,1152]{2,1,0:T(8,128)(2,1)S(1)}, u32[]{:S(2)}, u32[]{:S(2)}) collective-permute-start(bf16[2,16,1152]{2,1,0:T(8,128)(2,1)S(1)} %activate.4.own_ref), channel_id=1, source_target_pairs={{0,4},{1,5},{2,6},{3,7},{4,0},{5,1},{6,2},{7,3},{8,12},{9,13},{10,... | collective-permute-start | bytes 221192 | tf_op jit(solution)/shard_map/ppermute | solution.py:36
  56.2 12.0 %collective-permute-start.11 = (bf16[2,48,384]{2,1,0:T(8,128)(2,1)S(1)}, bf16[2,48,384]{2,1,0:T(8,128)(2,1)S(1)}, u32[]{:S(2)}, u32[]{:S(2)}) collective-permute-start(bf16[2,48,384]{2,1,0:T(8,128)(2,1)S(1)} %get-tuple-element.40), channel_id=1, source_target_pairs={{0,4},{1,5},{2,6},{3,7},{4,0},{5,1},{6,2},{7,3},{8,12},{9,13},{10,... | collective-permute-start | bytes 221192 | tf_op jit(solution)/shard_map/ppermute | solution.py:36
  56.4 14.3 %collective-permute-start.24 = (bf16[2,48,384]{2,1,0:T(8,128)(2,1)S(1)}, bf16[2,48,384]{2,1,0:T(8,128)(2,1)S(1)}, u32[]{:S(2)}, u32[]{:S(2)}) collective-permute-start(bf16[2,48,384]{2,1,0:T(8,128)(2,1)S(1)} %activate.7.own_ref), channel_id=1, source_target_pairs={{0,4},{1,5},{2,6},{3,7},{4,0},{5,1},{6,2},{7,3},{8,12},{9,13},{10,... | collective-permute-start | bytes 221192 | tf_op jit(solution)/shard_map/ppermute | solution.py:36
  63.5 9.1 %collective-permute-start.18 = (bf16[2,48,384]{2,1,0:T(8,128)(2,1)S(1)}, bf16[2,48,384]{2,1,0:T(8,128)(2,1)S(1)}, u32[]{:S(2)}, u32[]{:S(2)}) collective-permute-start(bf16[2,48,384]{2,1,0:T(8,128)(2,1)S(1)} %activate.6.own_ref), channel_id=1, source_target_pairs={{0,4},{1,5},{2,6},{3,7},{4,0},{5,1},{6,2},{7,3},{8,12},{9,13},{10,... | collective-permute-start | bytes 221192 | tf_op jit(solution)/shard_map/ppermute | solution.py:36
  65.0 11.1 %collective-permute-start.4 = (bf16[2,16,2304]{2,1,0:T(8,128)(2,1)S(1)}, bf16[2,16,2304]{2,1,0:T(8,128)(2,1)S(1)}, u32[]{:S(2)}, u32[]{:S(2)}) collective-permute-start(bf16[2,16,2304]{2,1,0:T(8,128)(2,1)S(1)} %join.12.own_ref), channel_id=1, source_target_pairs={{0,2},{1,3},{2,0},{3,1},{4,6},{5,7},{6,4},{7,5},{8,10},{9,11},{10,... | collective-permute-start | bytes 442376 | tf_op jit(solution)/shard_map/ppermute | solution.py:36
  68.3 7.9 %collective-permute-start.12 = (bf16[2,48,384]{2,1,0:T(8,128)(2,1)S(1)}, bf16[2,48,384]{2,1,0:T(8,128)(2,1)S(1)}, u32[]{:S(2)}, u32[]{:S(2)}) collective-permute-start(bf16[2,48,384]{2,1,0:T(8,128)(2,1)S(1)} %activate.5.own_ref), channel_id=1, source_target_pairs={{0,4},{1,5},{2,6},{3,7},{4,0},{5,1},{6,2},{7,3},{8,12},{9,13},{10,... | collective-permute-start | bytes 221192 | tf_op jit(solution)/shard_map/ppermute | solution.py:36
  70.7 8.7 %collective-permute-start.25 = (bf16[2,48,768]{2,1,0:T(8,128)(2,1)S(1)}, bf16[2,48,768]{2,1,0:T(8,128)(2,1)S(1)}, u32[]{:S(2)}, u32[]{:S(2)}) collective-permute-start(bf16[2,48,768]{2,1,0:T(8,128)(2,1)S(1)} %join.21.own_ref), channel_id=1, source_target_pairs={{0,2},{1,3},{2,0},{3,1},{4,6},{5,7},{6,4},{7,5},{8,10},{9,11},{10,... | collective-permute-start | bytes 442376 | tf_op jit(solution)/shard_map/ppermute | solution.py:36
  72.6 9.8 %collective-permute-start.19 = (bf16[2,48,768]{2,1,0:T(8,128)(2,1)S(1)}, bf16[2,48,768]{2,1,0:T(8,128)(2,1)S(1)}, u32[]{:S(2)}, u32[]{:S(2)}) collective-permute-start(bf16[2,48,768]{2,1,0:T(8,128)(2,1)S(1)} %join.18.own_ref), channel_id=1, source_target_pairs={{0,2},{1,3},{2,0},{3,1},{4,6},{5,7},{6,4},{7,5},{8,10},{9,11},{10,... | collective-permute-start | bytes 442376 | tf_op jit(solution)/shard_map/ppermute | solution.py:36
  76.2 8.9 %collective-permute-start.5 = (bf16[2,16,4608]{2,1,0:T(8,128)(2,1)S(1)}, bf16[2,16,4608]{2,1,0:T(8,128)(2,1)S(1)}, u32[]{:S(2)}, u32[]{:S(2)}) collective-permute-start(bf16[2,16,4608]{2,1,0:T(8,128)(2,1)S(1)} %join.13.own_ref), channel_id=1, source_target_pairs={{0,1},{1,0},{2,3},{3,2},{4,5},{5,4},{6,7},{7,6},{8,9},{9,8},{10,11... | collective-permute-start | bytes 884744 | tf_op jit(solution)/shard_map/ppermute | solution.py:36
  76.3 8.4 %collective-permute-start.13 = (bf16[2,48,768]{2,1,0:T(8,128)(2,1)S(1)}, bf16[2,48,768]{2,1,0:T(8,128)(2,1)S(1)}, u32[]{:S(2)}, u32[]{:S(2)}) collective-permute-start(bf16[2,48,768]{2,1,0:T(8,128)(2,1)S(1)} %join.15.own_ref), channel_id=1, source_target_pairs={{0,2},{1,3},{2,0},{3,1},{4,6},{5,7},{6,4},{7,5},{8,10},{9,11},{10,... | collective-permute-start | bytes 442376 | tf_op jit(solution)/shard_map/ppermute | solution.py:36
  79.3 5.8 %collective-permute-start.26 = (bf16[2,48,1536]{2,1,0:T(8,128)(2,1)S(1)}, bf16[2,48,1536]{2,1,0:T(8,128)(2,1)S(1)}, u32[]{:S(2)}, u32[]{:S(2)}) collective-permute-start(bf16[2,48,1536]{2,1,0:T(8,128)(2,1)S(1)} %join.22.own_ref), channel_id=1, source_target_pairs={{0,1},{1,0},{2,3},{3,2},{4,5},{5,4},{6,7},{7,6},{8,9},{9,8},{10,11... | collective-permute-start | bytes 884744 | tf_op jit(solution)/shard_map/ppermute | solution.py:36
  82.5 2.7 %collective-permute-start.20 = (bf16[2,48,1536]{2,1,0:T(8,128)(2,1)S(1)}, bf16[2,48,1536]{2,1,0:T(8,128)(2,1)S(1)}, u32[]{:S(2)}, u32[]{:S(2)}) collective-permute-start(bf16[2,48,1536]{2,1,0:T(8,128)(2,1)S(1)} %join.19.own_ref), channel_id=1, source_target_pairs={{0,1},{1,0},{2,3},{3,2},{4,5},{5,4},{6,7},{7,6},{8,9},{9,8},{10,11... | collective-permute-start | bytes 884744 | tf_op jit(solution)/shard_map/ppermute | solution.py:36
  84.7 8.4 %collective-permute-start.14 = (bf16[2,48,1536]{2,1,0:T(8,128)(2,1)S(1)}, bf16[2,48,1536]{2,1,0:T(8,128)(2,1)S(1)}, u32[]{:S(2)}, u32[]{:S(2)}) collective-permute-start(bf16[2,48,1536]{2,1,0:T(8,128)(2,1)S(1)} %join.16.own_ref), channel_id=1, source_target_pairs={{0,1},{1,0},{2,3},{3,2},{4,5},{5,4},{6,7},{7,6},{8,9},{9,8},{10,11... | collective-permute-start | bytes 884744 | tf_op jit(solution)/shard_map/ppermute | solution.py:36
  97.1 15.3 %collective-permute-start.27 = (bf16[32,1280]{1,0:T(8,128)(2,1)S(1)}, bf16[32,1280]{1,0:T(8,128)(2,1)S(1)}, u32[]{:S(2)}, u32[]{:S(2)}) collective-permute-start(bf16[32,1280]{1,0:T(8,128)(2,1)S(1)} %get-tuple-element.55), channel_id=1, source_target_pairs={{0,8},{8,0},{16,24},{24,16},{1,9},{9,1},{17,25},{25,17},{2,10},{10... | collective-permute-start | bytes 245768 | tf_op jit(solution)/shard_map/ppermute | solution.py:36
  98.5 13.9 %collective-permute-start.28 = (bf16[32,1280]{1,0:T(8,128)(2,1)S(1)}, bf16[32,1280]{1,0:T(8,128)(2,1)S(1)}, u32[]{:S(2)}, u32[]{:S(2)}) collective-permute-start(bf16[32,1280]{1,0:T(8,128)(2,1)S(1)} %get-tuple-element.57), channel_id=1, source_target_pairs={{0,16},{8,24},{16,0},{24,8},{1,17},{9,25},{17,1},{25,9},{2,18},{10... | collective-permute-start | bytes 245768 | tf_op jit(solution)/shard_map/ppermute | solution.py:36
  100.0 12.4 %collective-permute-start.29 = (bf16[32,1280]{1,0:T(8,128)(2,1)S(1)}, bf16[32,1280]{1,0:T(8,128)(2,1)S(1)}, u32[]{:S(2)}, u32[]{:S(2)}) collective-permute-start(bf16[32,1280]{1,0:T(8,128)(2,1)S(1)} %get-tuple-element.56), channel_id=1, source_target_pairs={{0,24},{8,16},{16,8},{24,0},{1,25},{9,17},{17,9},{25,1},{2,26},{10... | collective-permute-start | bytes 245768 | tf_op jit(solution)/shard_map/ppermute | solution.py:36

commit v3 on v2

v3 whole, which is shorter than its diff:
```python
import functools
import math

import jax
import jax.numpy as jnp
from jax import lax
from jax.experimental import pallas as pl
from jax.experimental.pallas import tpu as pltpu
from jax.sharding import PartitionSpec as P

BF16 = jnp.bfloat16
F32 = jnp.float32
GROUPS = 3
BLOCK = 512
SHARE = 1
VMEM_BYTES = 48 * 1024 * 1024
SMALL_BYTES = 16 * 1024 * 1024
SCALAR = pl.BlockSpec(memory_space=pltpu.SMEM)
ANY = pl.BlockSpec(memory_space=pl.ANY)


def gelu_parts(preact):
    cumul = 0.5 * (1.0 + jax.scipy.special.erf(preact * (1.0 / math.sqrt(2.0))))
    density = jnp.exp(-0.5 * preact * preact) * (1.0 / math.sqrt(2.0 * math.pi))
    return (preact * cumul, cumul + preact * density)


def contract(left, right, left_dim, right_dim):
    return lax.dot_general(
        left,
        right,
        (((left_dim,), (right_dim,)), ((), ())),
        preferred_element_type=F32,
    )


def exchange(array, axis, size, step):
    return lax.ppermute(array, axis, [(i, i ^ step) for i in range(size)])


def whole(*shape):
    return pl.BlockSpec(shape, lambda step: (0,) * len(shape))


def params(size=VMEM_BYTES):
    return pltpu.CompilerParams(vmem_limit_bytes=size)


def cost(flops, size):
    return pl.CostEstimate(
        flops=flops // SHARE, bytes_accessed=size // SHARE, transcendentals=0
    )


def by_bit(rank_ref, bit, choose):
    side = (rank_ref[0] >> bit) & 1
    for value in range(2):
        pl.when(side == value)(functools.partial(choose, value))


def forward(rank, tokens, w_in, w_out, start, width, after=()):
    parts = len(tokens)
    rows, features = tokens[0].shape[1:]
    total = parts * rows
    half = total // 2
    first, steps = start // BLOCK, width // BLOCK

    def kernel(rank_ref, *refs):
        token_refs = refs[:parts]
        wi_ref, wo_ref = refs[parts : parts + 2]
        keep_ref, send_ref = refs[-2:]

        def rows_of(which):
            return jnp.concatenate([ref[which] for ref in token_refs], axis=0)

        sums = (
            contract(rows_of(0), wi_ref[...], 1, 0),
            contract(wo_ref[...], rows_of(1), 1, 1).T,
        )

        def choose(core):
            for which, value in enumerate(sums):
                halves = value[:half], value[half:]
                keep_ref[which] = halves[core]
                send_ref[which] = halves[1 - core].astype(BF16)

        by_bit(rank_ref, 0, choose)

    block = pl.BlockSpec((2, half, BLOCK), lambda i: (0, 0, i))
    return pl.pallas_call(
        kernel,
        grid=(steps,),
        out_shape=(
            jax.ShapeDtypeStruct((2, half, width), F32),
            jax.ShapeDtypeStruct((2, half, width), BF16),
        ),
        in_specs=[SCALAR]
        + [whole(2, rows, features)] * parts
        + [
            pl.BlockSpec((features, BLOCK), lambda i: (0, first + i)),
            pl.BlockSpec((BLOCK, features), lambda i: (first + i, 0)),
        ]
        + [ANY] * len(after),
        out_specs=(block, block),
        compiler_params=params(),
        cost_estimate=cost(4 * total * features * width, 4 * features * width),
        name="forward",
    )(rank, *tokens, w_in, w_out, *after)


def halve(rank, keep, received, bit, after=()):
    _, rows, width = keep.shape
    half = width // 2

    def kernel(rank_ref, keep_ref, received_ref, *rest):
        next_ref, send_ref = rest[-2:]

        def choose(side):
            mine = slice(side * half, (side + 1) * half)
            other = slice((1 - side) * half, (2 - side) * half)
            next_ref[...] = keep_ref[:, :, mine] + received_ref[:, :, mine].astype(F32)
            send_ref[...] = (
                keep_ref[:, :, other] + received_ref[:, :, other].astype(F32)
            ).astype(BF16)

        by_bit(rank_ref, bit, choose)

    return pl.pallas_call(
        kernel,
        grid=(1,),
        out_shape=(
            jax.ShapeDtypeStruct((2, rows, half), F32),
            jax.ShapeDtypeStruct((2, rows, half), BF16),
        ),
        in_specs=[SCALAR] + [whole(2, rows, width)] * 2 + [ANY] * len(after),
        out_specs=(whole(2, rows, half),) * 2,
        compiler_params=params(SMALL_BYTES),
        cost_estimate=cost(2 * rows * width, 12 * rows * width),
        name="halve",
    )(rank, keep, received, *after)


def activate(keep, received, after=()):
    def kernel(keep_ref, received_ref, *rest):
        out_ref = rest[-1]
        value, slope = gelu_parts(keep_ref[0] + received_ref[0].astype(F32))
        grad = keep_ref[1] + received_ref[1].astype(F32)
        out_ref[0] = value.astype(BF16)
        out_ref[1] = (grad * slope).astype(BF16)

    return pl.pallas_call(
        kernel,
        grid=(1,),
        out_shape=jax.ShapeDtypeStruct(keep.shape, BF16),
        in_specs=[whole(*keep.shape)] * 2 + [ANY] * len(after),
        out_specs=whole(*keep.shape),
        compiler_params=params(SMALL_BYTES),
        cost_estimate=cost(20 * keep.size, 8 * keep.size),
        name="activate",
    )(keep, received, *after)


def relay(array, after):
    def kernel(in_ref, *rest):
        rest[-1][...] = in_ref[...]

    return pl.pallas_call(
        kernel,
        grid=(1,),
        out_shape=jax.ShapeDtypeStruct(array.shape, array.dtype),
        in_specs=[whole(*array.shape)] + [ANY] * len(after),
        out_specs=whole(*array.shape),
        compiler_params=params(SMALL_BYTES),
        cost_estimate=cost(0, 4 * array.size),
        name="relay",
    )(array, *after)


def join(rank, own, received, bit, axis, after=()):
    shape = list(own.shape)
    half = shape[axis]
    shape[axis] = 2 * half

    def kernel(rank_ref, own_ref, received_ref, *rest):
        out_ref = rest[-1]

        def choose(side):
            for place, source in ((side, own_ref), (1 - side, received_ref)):
                at = [slice(None)] * 3
                at[axis] = slice(place * half, (place + 1) * half)
                out_ref[tuple(at)] = source[...]

        by_bit(rank_ref, bit, choose)

    return pl.pallas_call(
        kernel,
        grid=(1,),
        out_shape=jax.ShapeDtypeStruct(shape, BF16),
        in_specs=[SCALAR] + [whole(*own.shape)] * 2 + [ANY] * len(after),
        out_specs=whole(*shape),
        compiler_params=params(SMALL_BYTES),
        cost_estimate=cost(0, 8 * own.size),
        name="join",
    )(rank, own, received, *after)


class Chunk:
    def __init__(self, rank, mp):
        self.rank, self.mp, self.bits = rank, mp, mp.bit_length() - 1
        self.keep, self.send, self.level = None, None, 0

    def advance(self, after):
        level, self.level = self.level, self.level + 1
        bit = level if level < self.bits else 2 * self.bits - 1 - level
        received = exchange(self.send, "mp", self.mp, 1 << bit)
        if level < self.bits - 1:
            self.keep, self.send = halve(self.rank, self.keep, received, bit + 1, after)
        elif level == self.bits - 1:
            self.send = activate(self.keep, received, after)
        else:
            axis = 2 if bit else 1
            self.send = join(self.rank, self.send, received, bit, axis, after)


def input_grads(
    first_rows, offset, other_rows, w_in, carried, start, width, last
):
    rows, rest = first_rows.shape[1], other_rows.shape[1]
    features = w_in.shape[0]
    first, steps = start // BLOCK, width // BLOCK
    shift = offset // BLOCK
    shape = (features, rows + rest)

    def kernel(*refs):
        own_ref, rest_ref, wi_ref = refs[:3]
        out_ref, sum_ref = refs[-2:]
        step = pl.program_id(0)
        grad = jnp.concatenate([own_ref[0], rest_ref[0]], axis=0)
        value = contract(wi_ref[...], grad, 1, 1)

        @pl.when(step == 0)
        def _():
            sum_ref[...] = value if carried is None else refs[3][...] + value

        @pl.when(step > 0)
        def _():
            sum_ref[...] += value

        @pl.when(step == steps - 1)
        def _():
            out_ref[...] = sum_ref[...].T if last else sum_ref[...]

    out = shape[::-1] if last else shape
    return pl.pallas_call(
        kernel,
        grid=(steps,),
        out_shape=jax.ShapeDtypeStruct(out, F32),
        in_specs=[
            pl.BlockSpec((1, rows, BLOCK), lambda i: (1, 0, shift + i)),
            pl.BlockSpec((1, rest, BLOCK), lambda i: (1, 0, i)),
            pl.BlockSpec((features, BLOCK), lambda i: (0, first + i)),
        ]
        + ([] if carried is None else [whole(*shape)]),
        out_specs=whole(*out),
        scratch_shapes=[pltpu.VMEM(shape, F32)],
        compiler_params=params(),
        cost_estimate=cost(
            2 * (rows + rest) * features * width, 2 * features * width
        ),
        name="input_grads",
    )(first_rows, other_rows, w_in, *([] if carried is None else [carried]))


def weight_grads(xt, gs, firsts, others, factor):
    features, total = xt.shape
    hidden = sum(part.shape[2] for part in firsts)

    def spans(arrays):
        end, found = 0, []
        for array in arrays:
            start, end = end, end + array.shape[2] // BLOCK
            found.append((array, start, end))
        return found

    first_spans, other_spans = spans(firsts), spans(others)
    cuts = sorted({end for _, _, end in first_spans + other_spans} | {0})

    def kernel(xt_ref, gs_ref, *refs):
        in_ref, out_ref = refs[-2:]
        step = pl.program_id(0)
        pairs = list(zip(refs[0:-2:2], refs[1:-2:2]))

        def work(first, other):
            (act_a, grad_a), (act_b, grad_b) = first, other
            act = jnp.concatenate([act_a[0], act_b[0]], axis=0)
            grad = jnp.concatenate([grad_a[0], grad_b[0]], axis=0)
            turned = act.astype(F32).T.astype(BF16)
            in_ref[...] = (contract(xt_ref[...], grad, 1, 0) * factor).astype(BF16)
            out_ref[...] = (contract(turned, gs_ref[...], 1, 0) * factor).astype(BF16)

        def holder(found, at, base):
            for index, (_, start, end) in enumerate(found):
                if start <= at < end:
                    return pairs[base + index]

        for low, high in zip(cuts[:-1], cuts[1:]):
            first = holder(first_spans, low, 0)
            other = holder(other_spans, low, len(firsts))
            here = (step >= low) & (step < high)
            pl.when(here)(functools.partial(work, first, other))

    def block(rows, start, end, which):
        def place(i):
            return which, 0, jnp.clip(i - start, 0, end - start - 1)

        return pl.BlockSpec((1, rows, BLOCK), place)

    specs, operands = [], []
    for array, start, end in first_spans + other_spans:
        specs += [block(array.shape[1], start, end, which) for which in range(2)]
        operands += [array, array]
    return pl.pallas_call(
        kernel,
        grid=(hidden // BLOCK,),
        out_shape=(
            jax.ShapeDtypeStruct((features, hidden), BF16),
            jax.ShapeDtypeStruct((hidden, features), BF16),
        ),
        in_specs=[whole(features, total), whole(total, features)] + specs,
        out_specs=(
            pl.BlockSpec((features, BLOCK), lambda i: (0, i)),
            pl.BlockSpec((BLOCK, features), lambda i: (i, 0)),
        ),
        compiler_params=params(),
        cost_estimate=cost(4 * total * features * hidden, 4 * features * hidden),
        name="weight_grads",
    )(xt, gs, *operands)


def local(inputs, out_grads, w_in, w_out, dp, mp):
    hidden = w_in.shape[1]
    width = hidden // GROUPS
    rows = inputs.shape[0]
    total = rows * dp
    factor = 1.0 / math.sqrt(total)
    rank = lax.axis_index("mp").astype(jnp.int32).reshape(1)

    own = jnp.stack([inputs, out_grads])
    others = [exchange(own, "dp", dp, j) for j in range(1, dp)]

    plans = [([own], 0, width), ([own], width, hidden - width)]
    plans += [(others, group * width, width) for group in range(GROUPS)]
    chunks = [Chunk(rank, mp) for _ in plans]
    levels = 2 * chunks[0].bits
    partial, after = None, []

    for slot in range(len(chunks) + levels):
        if slot < len(chunks):
            tokens, start, size = plans[slot]
            chunk = chunks[slot]
            chunk.keep, chunk.send = forward(
                rank, tokens, w_in, w_out, start, size, after
            )
            after = [chunk.send]
        for chunk in chunks[max(0, slot - levels) : slot]:
            early = slot < len(chunks)
            chunk.advance(after if early or chunk is chunks[-1] else [])
            after = [chunk.send] if early else after
        if 1 <= slot < len(chunks):
            chunks[slot].send = relay(chunks[slot].send, after)
            after = [chunks[slot].send]
        group = slot - levels - 2
        if group >= 0:
            first, offset = (0, 0) if group == 0 else (1, (group - 1) * width)
            partial = input_grads(
                chunks[first].send,
                offset,
                chunks[2 + group].send,
                w_in,
                partial,
                group * width,
                width,
                group == GROUPS - 1,
            )
            after = [partial]
    firsts = [chunk.send for chunk in chunks[:2]]
    finals = [chunk.send for chunk in chunks[2:]]

    in_total = partial[:rows]
    for j in range(1, dp):
        part = partial[j * rows : (j + 1) * rows].astype(BF16)
        in_total = in_total + exchange(part, "dp", dp, j).astype(F32)

    tokens = jnp.concatenate([own, *others], axis=1)
    unit = jnp.eye(total, dtype=BF16)
    xt = contract(tokens[0], unit, 0, 1).astype(BF16)
    grads = weight_grads(xt, tokens[1], firsts, finals, factor)
    return (in_total, *grads)


def solution(mesh):
    sizes = dict(mesh.shape)
    return jax.shard_map(
        functools.partial(local, dp=sizes["dp"], mp=sizes["mp"]),
        mesh=mesh,
        in_specs=(P("dp", "mp"), P("dp", "mp"), P("mp", "dp"), P("dp", "mp")),
        out_specs=(P("dp", "mp"), P("mp", "dp"), P("dp", "mp")),
        check_vma=False,
    )
```

time: 114 us -> 115 us (level)
  Pallas kernels: 52 us -> 53.3 us
    pallas_call x4 -> x5, Pallas kernels: 27.6 us -> 28.7 us  [forward(): pl.pallas_call(kernel, grid=(steps,), out_shape=(jax.ShapeDtypeStruct((2,...]
    ppermute x30 -> x36, starting transfers between devices: 32 us -> 31.3 us  [exchange(): return lax.ppermute(array, axis, [(i, i ^ step) for i in range(size)])]
    ppermute x30 -> x36, waiting for transfers between devices: 26.1 us -> 26.4 us  [exchange(): return lax.ppermute(array, axis, [(i, i ^ step) for i in range(size)])]
    pallas_call x4 -> x8, Pallas kernels: 23.4 us -> 23.6 us  [the longest x3 11.8 us: input_grads(): pl.pallas_call(kernel, grid=(steps,), out_shape=jax.ShapeDtypeStruct(out,...]
  transfers between devices with their start and end apart: 30 -> 36, of which waited for: 12 -> 10; matrix products, arithmetic and copies ran while one was open for 0% -> 0% of each run, Pallas kernels for 42% -> 38%
where the time goes in v3:
time: 115 us; the launch traced here: 114 us
  Pallas kernels  53.3 us (46%)
  starting transfers between devices  31.3 us (27%)
  waiting for transfers between devices  26.4 us (23%)
  other arithmetic  1.73 us (2%)
  between operations  1.2 us (1%)
    ppermute x36, starting transfers between devices, exchange(): return lax.ppermute(array, axis, [(i, i ^ step) for i in range(size)])  31.3 us
    pallas_call x5, Pallas kernels, forward(): pl.pallas_call(kernel, grid=(steps,), out_shape=(jax.ShapeDtypeStruct((2,...  28.7 us
    ppermute x36, waiting for transfers between devices, exchange(): return lax.ppermute(array, axis, [(i, i ^ step) for i in range(size)])  26.4 us
    pallas_call x3, Pallas kernels, input_grads(): pl.pallas_call(kernel, grid=(steps,), out_shape=jax.ShapeDtypeStruct(out,...  11.8 us
    pallas_call x1, Pallas kernels, weight_grads(): pl.pallas_call(kernel, grid=(hidden // BLOCK,), out_shape=(jax.ShapeDtype...  11.7 us
  transfers between devices with their start and end apart: 36, of which 10 were waited for; matrix products, arithmetic and copies ran while one was open for 0% of the time, Pallas kernels for 38%

profile of v3, /device:TPU:0, one launch (start us, length us, event | category | flops | bytes accessed | tf_op | source)
XLA Modules:
  0.0 114.3 jit_solution(15771737156304109207)
XLA Ops:
  0.6 0.9 pad_maximum_fusion.1.refs_0_
  1.6 5.0 %forward.5 = (f32[2,16,1536]{2,1,0:T(8,128)S(1)}, bf16[2,16,1536]{2,1,0:T(8,128)(2,1)S(1)}) custom-call(s32[1]{0:T(128)} %bitcast.rank_ref, bf16[2,32,1280]{2,1,0:T(8,128)(2,1)S(1)} %pad_maximum_fusion.1.refs_0_, bf16[1280,4608]{1,0:T(8,128)(2,1)} %refs_2_.9, bf16[4608,1280]{1,0:T(8,128)(2,1)} %refs_4_.5), custom_call_target="tpu_custom_call" | custom-call | flops 251658240 | bytes 7864320 | tf_op jit(solution)/shard_map/forward/pallas_call | solution.py:90
  6.6 0.5 collective-permute-start
  7.1 3.5 %collective-permute-start.5 = (bf16[2,32,1280]{2,1,0:T(8,128)(2,1)S(1)}, bf16[2,32,1280]{2,1,0:T(8,128)(2,1)S(1)}, u32[]{:S(2)}, u32[]{:S(2)}) collective-permute-start(bf16[2,32,1280]{2,1,0:T(8,128)(2,1)S(1)} %pad_maximum_fusion.1.refs_0_), channel_id=1, source_target_pairs={{0,24},{8,16},{16,8},{24,0},{1,25},{9,17},{17,9},{25,1},{2,26},{10... | collective-permute-start | bytes 491528 | tf_op jit(solution)/shard_map/ppermute | solution.py:38
  10.6 0.5 collective-permute-start.4
  11.1 0.1 collective-permute-start.3
  11.3 8.6 %forward.6 = (f32[2,16,3072]{2,1,0:T(8,128)S(1)}, bf16[2,16,3072]{2,1,0:T(8,128)(2,1)S(1)}) custom-call(s32[1]{0:T(128)} %bitcast.rank_ref, bf16[2,32,1280]{2,1,0:T(8,128)(2,1)S(1)} %pad_maximum_fusion.1.refs_0_, bf16[1280,4608]{1,0:T(8,128)(2,1)} %refs_2_.9, bf16[4608,1280]{1,0:T(8,128)(2,1)} %refs_4_.5, bf16[2,16,1536]{2,1,0:T(8,128)(2,1)S(1)} %get-tuple-element.35.refs_3_), custom_call_target="tpu_custom_call" | custom-call | flops 503316480 | bytes 15728640 | tf_op jit(solution)/shard_map/forward/pallas_call | solution.py:90
  20.0 2.0 %collective-permute-start.2 = (bf16[2,16,768]{2,1,0:T(8,128)(2,1)S(1)}, bf16[2,16,768]{2,1,0:T(8,128)(2,1)S(1)}, u32[]{:S(2)}, u32[]{:S(2)}) collective-permute-start(bf16[2,16,768]{2,1,0:T(8,128)(2,1)S(1)} %get-tuple-element.39.rest_0_), channel_id=1, source_target_pairs={{0,2},{1,3},{2,0},{3,1},{4,6},{5,7},{6,4},{7,5},{8,10},{9,11},{10,... | collective-permute-start | bytes 147464 | tf_op jit(solution)/shard_map/ppermute | solution.py:38
  22.1 5.0 %forward.7 = (f32[2,48,1536]{2,1,0:T(8,128)S(1)}, bf16[2,48,1536]{2,1,0:T(8,128)(2,1)S(1)}) custom-call(s32[1]{0:T(128)} %bitcast.rank_ref, bf16[2,32,1280]{2,1,0:T(8,128)(2,1)S(1)} %collective-permute-done.3.refs_0_, bf16[2,32,1280]{2,1,0:T(8,128)(2,1)S(1)} %collective-permute-done.4.refs_1_, bf16[2,32,1280]{2,1,0:T(8,128)(2,1)S(1)} %collective-permute-done.5.refs_2_, ...), custom_call_target="tpu_custom_call" | custom-call | flops 754974720 | bytes 7864320 | tf_op jit(solution)/shard_map/forward/pallas_call | solution.py:90
  27.3 0.3 collective-permute-start.10
  27.6 0.3 collective-permute-start.6
  27.8 2.8 %collective-permute-start.7 = (bf16[2,16,384]{2,1,0:T(8,128)(2,1)S(1)}, bf16[2,16,384]{2,1,0:T(8,128)(2,1)S(1)}, u32[]{:S(2)}, u32[]{:S(2)}) collective-permute-start(bf16[2,16,384]{2,1,0:T(8,128)(2,1)S(1)} %get-tuple-element.42.rest_0_), channel_id=1, source_target_pairs={{0,4},{1,5},{2,6},{3,7},{4,0},{5,1},{6,2},{7,3},{8,12},{9,13},{10,... | collective-permute-start | bytes 73736 | tf_op jit(solution)/shard_map/ppermute | solution.py:38
  30.6 5.0 %forward.8 = (f32[2,48,1536]{2,1,0:T(8,128)S(1)}, bf16[2,48,1536]{2,1,0:T(8,128)(2,1)S(1)}) custom-call(s32[1]{0:T(128)} %bitcast.rank_ref, bf16[2,32,1280]{2,1,0:T(8,128)(2,1)S(1)} %collective-permute-done.3.refs_0_, bf16[2,32,1280]{2,1,0:T(8,128)(2,1)S(1)} %collective-permute-done.4.refs_1_, bf16[2,32,1280]{2,1,0:T(8,128)(2,1)S(1)} %collective-permute-done.5.refs_2_, ...), custom_call_target="tpu_custom_call" | custom-call | flops 754974720 | bytes 7864320 | tf_op jit(solution)/shard_map/forward/pallas_call | solution.py:90
  35.9 1.6 %collective-permute-start.15 = (bf16[2,48,768]{2,1,0:T(8,128)(2,1)S(1)}, bf16[2,48,768]{2,1,0:T(8,128)(2,1)S(1)}, u32[]{:S(2)}, u32[]{:S(2)}) collective-permute-start(bf16[2,48,768]{2,1,0:T(8,128)(2,1)S(1)} %get-tuple-element.50.rest_0_), channel_id=1, source_target_pairs={{0,2},{1,3},{2,0},{3,1},{4,6},{5,7},{6,4},{7,5},{8,10},{9,11},{10,... | collective-permute-start | bytes 442376 | tf_op jit(solution)/shard_map/ppermute | solution.py:38
  37.6 0.3 collective-permute-start.9
  37.9 2.6 %collective-permute-start.8 = (bf16[2,16,768]{2,1,0:T(8,128)(2,1)S(1)}, bf16[2,16,768]{2,1,0:T(8,128)(2,1)S(1)}, u32[]{:S(2)}, u32[]{:S(2)}) collective-permute-start(bf16[2,16,768]{2,1,0:T(8,128)(2,1)S(1)} %get-tuple-element.48.rest_0_), channel_id=1, source_target_pairs={{0,4},{1,5},{2,6},{3,7},{4,0},{5,1},{6,2},{7,3},{8,12},{9,13},{10,... | collective-permute-start | bytes 147464 | tf_op jit(solution)/shard_map/ppermute | solution.py:38
  40.5 5.0 %forward.9 = (f32[2,48,1536]{2,1,0:T(8,128)S(1)}, bf16[2,48,1536]{2,1,0:T(8,128)(2,1)S(1)}) custom-call(s32[1]{0:T(128)} %bitcast.rank_ref, bf16[2,32,1280]{2,1,0:T(8,128)(2,1)S(1)} %collective-permute-done.3.refs_0_, bf16[2,32,1280]{2,1,0:T(8,128)(2,1)S(1)} %collective-permute-done.4.refs_1_, bf16[2,32,1280]{2,1,0:T(8,128)(2,1)S(1)} %collective-permute-done.5.refs_2_, ...), custom_call_target="tpu_custom_call" | custom-call | flops 754974720 | bytes 7864320 | tf_op jit(solution)/shard_map/forward/pallas_call | solution.py:90
  45.9 0.7 collective-permute-start.23
  46.6 0.8 collective-permute-done.16.received_ref
  47.5 1.2 %collective-permute-start.17 = (bf16[2,48,768]{2,1,0:T(8,128)(2,1)S(1)}, bf16[2,48,768]{2,1,0:T(8,128)(2,1)S(1)}, u32[]{:S(2)}, u32[]{:S(2)}) collective-permute-start(bf16[2,48,768]{2,1,0:T(8,128)(2,1)S(1)} %get-tuple-element.58), channel_id=1, source_target_pairs={{0,2},{1,3},{2,0},{3,1},{4,6},{5,7},{6,4},{7,5},{8,10},{9,11},{10,... | collective-permute-start | bytes 442376 | tf_op jit(solution)/shard_map/ppermute | solution.py:38
  48.7 4.3 %collective-permute-done.23.received_ref = bf16[2,48,384]{2,1,0:T(8,128)(2,1)S(1)} collective-permute-done((bf16[2,48,384]{2,1,0:T(8,128)(2,1)S(1)}, bf16[2,48,384]{2,1,0:T(8,128)(2,1)S(1)}, u32[]{:S(2)}, u32[]{:S(2)}) %collective-permute-start.23) | collective-permute-done | bytes 73760 | tf_op jit(solution)/shard_map/ppermute | solution.py:38
  53.2 6.6 %collective-permute-done.24.received_ref = bf16[2,48,384]{2,1,0:T(8,128)(2,1)S(1)} collective-permute-done((bf16[2,48,384]{2,1,0:T(8,128)(2,1)S(1)}, bf16[2,48,384]{2,1,0:T(8,128)(2,1)S(1)}, u32[]{:S(2)}, u32[]{:S(2)}) %collective-permute-start.24) | collective-permute-done | bytes 73760 | tf_op jit(solution)/shard_map/ppermute | solution.py:38
  59.8 0.2 collective-permute-start.25
  60.0 0.2 collective-permute-start.29
  60.3 2.8 %collective-permute-start.18 = (bf16[2,48,384]{2,1,0:T(8,128)(2,1)S(1)}, bf16[2,48,384]{2,1,0:T(8,128)(2,1)S(1)}, u32[]{:S(2)}, u32[]{:S(2)}) collective-permute-start(bf16[2,48,384]{2,1,0:T(8,128)(2,1)S(1)} %get-tuple-element.60), channel_id=1, source_target_pairs={{0,4},{1,5},{2,6},{3,7},{4,0},{5,1},{6,2},{7,3},{8,12},{9,13},{10,... | collective-permute-start | bytes 221192 | tf_op jit(solution)/shard_map/ppermute | solution.py:38
  63.2 5.3 %collective-permute-done.29.received_ref = bf16[2,48,384]{2,1,0:T(8,128)(2,1)S(1)} collective-permute-done((bf16[2,48,384]{2,1,0:T(8,128)(2,1)S(1)}, bf16[2,48,384]{2,1,0:T(8,128)(2,1)S(1)}, u32[]{:S(2)}, u32[]{:S(2)}) %collective-permute-start.29) | collective-permute-done | bytes 73760 | tf_op jit(solution)/shard_map/ppermute | solution.py:38
  68.5 0.3 collective-permute-start.30
  68.8 2.8 %collective-permute-done.18.received_ref = bf16[2,48,384]{2,1,0:T(8,128)(2,1)S(1)} collective-permute-done((bf16[2,48,384]{2,1,0:T(8,128)(2,1)S(1)}, bf16[2,48,384]{2,1,0:T(8,128)(2,1)S(1)}, u32[]{:S(2)}, u32[]{:S(2)}) %collective-permute-start.18) | collective-permute-done | bytes 73760 | tf_op jit(solution)/shard_map/ppermute | solution.py:38
  71.7 2.4 %collective-permute-start.21 = (bf16[2,16,768]{2,1,0:T(8,128)(2,1)S(1)}, bf16[2,16,768]{2,1,0:T(8,128)(2,1)S(1)}, u32[]{:S(2)}, u32[]{:S(2)}) collective-permute-start(bf16[2,16,768]{2,1,0:T(8,128)(2,1)S(1)} %join.15.rest_0_.own_ref), channel_id=1, source_target_pairs={{0,2},{1,3},{2,0},{3,1},{4,6},{5,7},{6,4},{7,5},{8,10},{9,11},{10,... | collective-permute-start | bytes 147464 | tf_op jit(solution)/shard_map/ppermute | solution.py:38
  74.2 0.6 collective-permute-start.11
  74.8 1.4 %collective-permute-done.21.received_ref = bf16[2,16,768]{2,1,0:T(8,128)(2,1)S(1)} collective-permute-done((bf16[2,16,768]{2,1,0:T(8,128)(2,1)S(1)}, bf16[2,16,768]{2,1,0:T(8,128)(2,1)S(1)}, u32[]{:S(2)}, u32[]{:S(2)}) %collective-permute-start.21) | collective-permute-done | bytes 49184 | tf_op jit(solution)/shard_map/ppermute | solution.py:38
  76.3 2.5 %collective-permute-start.31 = (bf16[2,48,768]{2,1,0:T(8,128)(2,1)S(1)}, bf16[2,48,768]{2,1,0:T(8,128)(2,1)S(1)}, u32[]{:S(2)}, u32[]{:S(2)}) collective-permute-start(bf16[2,48,768]{2,1,0:T(8,128)(2,1)S(1)} %join.26.own_ref), channel_id=1, source_target_pairs={{0,2},{1,3},{2,0},{3,1},{4,6},{5,7},{6,4},{7,5},{8,10},{9,11},{10,... | collective-permute-start | bytes 442376 | tf_op jit(solution)/shard_map/ppermute | solution.py:38
  78.8 0.1 collective-permute-start.20
  79.0 1.1 collective-permute-done.11.received_ref
  80.1 1.0 collective-permute-start.12
  81.1 2.4 %collective-permute-done.31.received_ref = bf16[2,48,768]{2,1,0:T(8,128)(2,1)S(1)} collective-permute-done((bf16[2,48,768]{2,1,0:T(8,128)(2,1)S(1)}, bf16[2,48,768]{2,1,0:T(8,128)(2,1)S(1)}, u32[]{:S(2)}, u32[]{:S(2)}) %collective-permute-start.31) | collective-permute-done | bytes 147488 | tf_op jit(solution)/shard_map/ppermute | solution.py:38
  83.7 3.8 %input_grads.3.rest_0_.refs_3_ = f32[1280,128]{1,0:T(8,128)S(1)} custom-call(bf16[2,32,1536]{2,1,0:T(8,128)(2,1)S(1)} %join.21.refs_0_.refs_1_, bf16[2,96,1536]{2,1,0:T(8,128)(2,1)S(1)} %join.24.refs_1_.refs_4_.refs_5_, bf16[1280,4608]{1,0:T(8,128)(2,1)} %refs_2_.9), custom_call_target="tpu_custom_call" | custom-call | flops 503316480 | bytes 3932160 | tf_op jit(solution)/shard_map/input_grads/pallas_call | solution.py:254
  87.6 0.5 collective-permute-start.27
  88.1 0.4 collective-permute-done.12.received_ref
  88.7 0.3 convolution_convert_fusion.xt_ref
  88.9 1.1 %collective-permute-done.13.received_ref = bf16[2,16,3072]{2,1,0:T(8,128)(2,1)S(1)} collective-permute-done((bf16[2,16,3072]{2,1,0:T(8,128)(2,1)S(1)}, bf16[2,16,3072]{2,1,0:T(8,128)(2,1)S(1)}, u32[]{:S(2)}, u32[]{:S(2)}) %collective-permute-start.13) | collective-permute-done | bytes 196640 | tf_op jit(solution)/shard_map/ppermute | solution.py:38
  90.2 3.9 %input_grads.4.rest_0_.refs_3_ = f32[1280,128]{1,0:T(8,128)S(1)} custom-call(bf16[2,32,3072]{2,1,0:T(8,128)(2,1)S(1)} %join.18.refs_0_.refs_2_.refs_3_, bf16[2,96,1536]{2,1,0:T(8,128)(2,1)S(1)} %join.28.refs_1_.refs_6_.refs_7_, bf16[1280,4608]{1,0:T(8,128)(2,1)} %refs_2_.9, f32[1280,128]{1,0:T(8,128)S(1)} %input_grads.3.rest_0_.refs_3_), custom_call_target="tpu_custom_call" | custom-call | flops 503316480 | bytes 3932160 | tf_op jit(solution)/shard_map/input_grads/pallas_call | solution.py:254
  94.1 4.1 %input_grads.5 = f32[128,1280]{1,0:T(8,128)S(1)} custom-call(bf16[2,32,3072]{2,1,0:T(8,128)(2,1)S(1)} %join.18.refs_0_.refs_2_.refs_3_, bf16[2,96,1536]{2,1,0:T(8,128)(2,1)S(1)} %join.29.refs_1_.refs_8_.refs_9_, bf16[1280,4608]{1,0:T(8,128)(2,1)} %refs_2_.9, f32[1280,128]{1,0:T(8,128)S(1)} %input_grads.4.rest_0_.refs_3_), custom_call_target="tpu_custom_call" | custom-call | flops 503316480 | bytes 3932160 | tf_op jit(solution)/shard_map/input_grads/pallas_call | solution.py:254
  98.3 1.6 %collective-permute-start.33 = (bf16[32,1280]{1,0:T(8,128)(2,1)S(1)}, bf16[32,1280]{1,0:T(8,128)(2,1)S(1)}, u32[]{:S(2)}, u32[]{:S(2)}) collective-permute-start(bf16[32,1280]{1,0:T(8,128)(2,1)S(1)} %get-tuple-element.67), channel_id=1, source_target_pairs={{0,8},{8,0},{16,24},{24,16},{1,9},{9,1},{17,25},{25,17},{2,10},{10... | collective-permute-start | bytes 245768 | tf_op jit(solution)/shard_map/ppermute | solution.py:38
  99.9 1.5 %collective-permute-start.35 = (bf16[32,1280]{1,0:T(8,128)(2,1)S(1)}, bf16[32,1280]{1,0:T(8,128)(2,1)S(1)}, u32[]{:S(2)}, u32[]{:S(2)}) collective-permute-start(bf16[32,1280]{1,0:T(8,128)(2,1)S(1)} %get-tuple-element.68), channel_id=1, source_target_pairs={{0,24},{8,16},{16,8},{24,0},{1,25},{9,17},{17,9},{25,1},{2,26},{10... | collective-permute-start | bytes 245768 | tf_op jit(solution)/shard_map/ppermute | solution.py:38
  101.4 0.5 collective-permute-start.34
  101.9 11.7 %weight_grads.1 = (bf16[1280,4608]{1,0:T(8,128)(2,1)}, bf16[4608,1280]{1,0:T(8,128)(2,1)}) custom-call(bf16[1280,128]{1,0:T(8,128)(2,1)S(1)} %convolution_convert_fusion.xt_ref, bf16[128,1280]{1,0:T(8,128)(2,1)S(1)} %slice_bitcast_fusion.gs_ref, bf16[2,32,1536]{2,1,0:T(8,128)(2,1)S(1)} %join.21.refs_0_.refs_1_, ...), custom_call_target="tpu_custom_call" | custom-call | flops 3019898880 | bytes 23592960 | tf_op jit(solution)/shard_map/weight_grads/pallas_call | solution.py:322
  113.6 0.7 fusion.1
  (78 shorter events, 1.9 us)
Async XLA Ops:
  6.6 13.3 %collective-permute-start = (bf16[2,16,1536]{2,1,0:T(8,128)(2,1)S(1)}, bf16[2,16,1536]{2,1,0:T(8,128)(2,1)S(1)}, u32[]{:S(2)}, u32[]{:S(2)}) collective-permute-start(bf16[2,16,1536]{2,1,0:T(8,128)(2,1)S(1)} %get-tuple-element.35.refs_3_), channel_id=1, source_target_pairs={{0,1},{1,0},{2,3},{3,2},{4,5},{5,4},{6,7},{7,6},{8,9},{9,8},{10,11... | collective-permute-start | bytes 294920 | tf_op jit(solution)/shard_map/ppermute | solution.py:38
  7.1 15.0 %collective-permute-start.5 = (bf16[2,32,1280]{2,1,0:T(8,128)(2,1)S(1)}, bf16[2,32,1280]{2,1,0:T(8,128)(2,1)S(1)}, u32[]{:S(2)}, u32[]{:S(2)}) collective-permute-start(bf16[2,32,1280]{2,1,0:T(8,128)(2,1)S(1)} %pad_maximum_fusion.1.refs_0_), channel_id=1, source_target_pairs={{0,24},{8,16},{16,8},{24,0},{1,25},{9,17},{17,9},{25,1},{2,26},{10... | collective-permute-start | bytes 491528 | tf_op jit(solution)/shard_map/ppermute | solution.py:38
  10.6 11.5 %collective-permute-start.4 = (bf16[2,32,1280]{2,1,0:T(8,128)(2,1)S(1)}, bf16[2,32,1280]{2,1,0:T(8,128)(2,1)S(1)}, u32[]{:S(2)}, u32[]{:S(2)}) collective-permute-start(bf16[2,32,1280]{2,1,0:T(8,128)(2,1)S(1)} %pad_maximum_fusion.1.refs_0_), channel_id=1, source_target_pairs={{0,16},{8,24},{16,0},{24,8},{1,17},{9,25},{17,1},{25,9},{2,18},{10... | collective-permute-start | bytes 491528 | tf_op jit(solution)/shard_map/ppermute | solution.py:38
  11.1 11.0 %collective-permute-start.3 = (bf16[2,32,1280]{2,1,0:T(8,128)(2,1)S(1)}, bf16[2,32,1280]{2,1,0:T(8,128)(2,1)S(1)}, u32[]{:S(2)}, u32[]{:S(2)}) collective-permute-start(bf16[2,32,1280]{2,1,0:T(8,128)(2,1)S(1)} %pad_maximum_fusion.1.refs_0_), channel_id=1, source_target_pairs={{0,8},{8,0},{16,24},{24,16},{1,9},{9,1},{17,25},{25,17},{2,10},{10... | collective-permute-start | bytes 491528 | tf_op jit(solution)/shard_map/ppermute | solution.py:38
  20.0 7.2 %collective-permute-start.1 = (bf16[2,16,3072]{2,1,0:T(8,128)(2,1)S(1)}, bf16[2,16,3072]{2,1,0:T(8,128)(2,1)S(1)}, u32[]{:S(2)}, u32[]{:S(2)}) collective-permute-start(bf16[2,16,3072]{2,1,0:T(8,128)(2,1)S(1)} %relay.4.refs_5_), channel_id=1, source_target_pairs={{0,1},{1,0},{2,3},{3,2},{4,5},{5,4},{6,7},{7,6},{8,9},{9,8},{10,11... | collective-permute-start | bytes 589832 | tf_op jit(solution)/shard_map/ppermute | solution.py:38
  20.0 7.1 %collective-permute-start.2 = (bf16[2,16,768]{2,1,0:T(8,128)(2,1)S(1)}, bf16[2,16,768]{2,1,0:T(8,128)(2,1)S(1)}, u32[]{:S(2)}, u32[]{:S(2)}) collective-permute-start(bf16[2,16,768]{2,1,0:T(8,128)(2,1)S(1)} %get-tuple-element.39.rest_0_), channel_id=1, source_target_pairs={{0,2},{1,3},{2,0},{3,1},{4,6},{5,7},{6,4},{7,5},{8,10},{9,11},{10,... | collective-permute-start | bytes 147464 | tf_op jit(solution)/shard_map/ppermute | solution.py:38
  27.3 8.4 %collective-permute-start.10 = (bf16[2,48,1536]{2,1,0:T(8,128)(2,1)S(1)}, bf16[2,48,1536]{2,1,0:T(8,128)(2,1)S(1)}, u32[]{:S(2)}, u32[]{:S(2)}) collective-permute-start(bf16[2,48,1536]{2,1,0:T(8,128)(2,1)S(1)} %relay.5.refs_5_), channel_id=1, source_target_pairs={{0,1},{1,0},{2,3},{3,2},{4,5},{5,4},{6,7},{7,6},{8,9},{9,8},{10,11... | collective-permute-start | bytes 884744 | tf_op jit(solution)/shard_map/ppermute | solution.py:38
  27.6 8.1 %collective-permute-start.6 = (bf16[2,16,1536]{2,1,0:T(8,128)(2,1)S(1)}, bf16[2,16,1536]{2,1,0:T(8,128)(2,1)S(1)}, u32[]{:S(2)}, u32[]{:S(2)}) collective-permute-start(bf16[2,16,1536]{2,1,0:T(8,128)(2,1)S(1)} %get-tuple-element.44.rest_0_), channel_id=1, source_target_pairs={{0,2},{1,3},{2,0},{3,1},{4,6},{5,7},{6,4},{7,5},{8,10},{9,11},{10,... | collective-permute-start | bytes 294920 | tf_op jit(solution)/shard_map/ppermute | solution.py:38
  27.8 7.8 %collective-permute-start.7 = (bf16[2,16,384]{2,1,0:T(8,128)(2,1)S(1)}, bf16[2,16,384]{2,1,0:T(8,128)(2,1)S(1)}, u32[]{:S(2)}, u32[]{:S(2)}) collective-permute-start(bf16[2,16,384]{2,1,0:T(8,128)(2,1)S(1)} %get-tuple-element.42.rest_0_), channel_id=1, source_target_pairs={{0,4},{1,5},{2,6},{3,7},{4,0},{5,1},{6,2},{7,3},{8,12},{9,13},{10,... | collective-permute-start | bytes 73736 | tf_op jit(solution)/shard_map/ppermute | solution.py:38
  35.8 9.8 %collective-permute-start.14 = (bf16[2,48,1536]{2,1,0:T(8,128)(2,1)S(1)}, bf16[2,48,1536]{2,1,0:T(8,128)(2,1)S(1)}, u32[]{:S(2)}, u32[]{:S(2)}) collective-permute-start(bf16[2,48,1536]{2,1,0:T(8,128)(2,1)S(1)} %relay.6.refs_5_), channel_id=1, source_target_pairs={{0,1},{1,0},{2,3},{3,2},{4,5},{5,4},{6,7},{7,6},{8,9},{9,8},{10,11... | collective-permute-start | bytes 884744 | tf_op jit(solution)/shard_map/ppermute | solution.py:38
  35.9 9.7 %collective-permute-start.15 = (bf16[2,48,768]{2,1,0:T(8,128)(2,1)S(1)}, bf16[2,48,768]{2,1,0:T(8,128)(2,1)S(1)}, u32[]{:S(2)}, u32[]{:S(2)}) collective-permute-start(bf16[2,48,768]{2,1,0:T(8,128)(2,1)S(1)} %get-tuple-element.50.rest_0_), channel_id=1, source_target_pairs={{0,2},{1,3},{2,0},{3,1},{4,6},{5,7},{6,4},{7,5},{8,10},{9,11},{10,... | collective-permute-start | bytes 442376 | tf_op jit(solution)/shard_map/ppermute | solution.py:38
  37.6 8.0 %collective-permute-start.9 = (bf16[2,16,384]{2,1,0:T(8,128)(2,1)S(1)}, bf16[2,16,384]{2,1,0:T(8,128)(2,1)S(1)}, u32[]{:S(2)}, u32[]{:S(2)}) collective-permute-start(bf16[2,16,384]{2,1,0:T(8,128)(2,1)S(1)} %activate.5.rest_0_.own_ref), channel_id=1, source_target_pairs={{0,4},{1,5},{2,6},{3,7},{4,0},{5,1},{6,2},{7,3},{8,12},{9,13},{10,... | collective-permute-start | bytes 73736 | tf_op jit(solution)/shard_map/ppermute | solution.py:38
  37.9 7.7 %collective-permute-start.8 = (bf16[2,16,768]{2,1,0:T(8,128)(2,1)S(1)}, bf16[2,16,768]{2,1,0:T(8,128)(2,1)S(1)}, u32[]{:S(2)}, u32[]{:S(2)}) collective-permute-start(bf16[2,16,768]{2,1,0:T(8,128)(2,1)S(1)} %get-tuple-element.48.rest_0_), channel_id=1, source_target_pairs={{0,4},{1,5},{2,6},{3,7},{4,0},{5,1},{6,2},{7,3},{8,12},{9,13},{10,... | collective-permute-start | bytes 147464 | tf_op jit(solution)/shard_map/ppermute | solution.py:38
  45.8 1.6 %collective-permute-start.16 = (bf16[2,48,1536]{2,1,0:T(8,128)(2,1)S(1)}, bf16[2,48,1536]{2,1,0:T(8,128)(2,1)S(1)}, u32[]{:S(2)}, u32[]{:S(2)}) collective-permute-start(bf16[2,48,1536]{2,1,0:T(8,128)(2,1)S(1)} %relay.7.rest_0_), channel_id=1, source_target_pairs={{0,1},{1,0},{2,3},{3,2},{4,5},{5,4},{6,7},{7,6},{8,9},{9,8},{10,11... | collective-permute-start | bytes 884744 | tf_op jit(solution)/shard_map/ppermute | solution.py:38
  45.9 7.2 %collective-permute-start.23 = (bf16[2,48,384]{2,1,0:T(8,128)(2,1)S(1)}, bf16[2,48,384]{2,1,0:T(8,128)(2,1)S(1)}, u32[]{:S(2)}, u32[]{:S(2)}) collective-permute-start(bf16[2,48,384]{2,1,0:T(8,128)(2,1)S(1)} %get-tuple-element.55.rest_0_), channel_id=1, source_target_pairs={{0,4},{1,5},{2,6},{3,7},{4,0},{5,1},{6,2},{7,3},{8,12},{9,13},{10,... | collective-permute-start | bytes 221192 | tf_op jit(solution)/shard_map/ppermute | solution.py:38
  46.6 13.4 %collective-permute-start.28 = (bf16[2,48,768]{2,1,0:T(8,128)(2,1)S(1)}, bf16[2,48,768]{2,1,0:T(8,128)(2,1)S(1)}, u32[]{:S(2)}, u32[]{:S(2)}) collective-permute-start(bf16[2,48,768]{2,1,0:T(8,128)(2,1)S(1)} %get-tuple-element.56.rest_0_), channel_id=1, source_target_pairs={{0,2},{1,3},{2,0},{3,1},{4,6},{5,7},{6,4},{7,5},{8,10},{9,11},{10,... | collective-permute-start | bytes 442376 | tf_op jit(solution)/shard_map/ppermute | solution.py:38
  47.5 12.8 %collective-permute-start.17 = (bf16[2,48,768]{2,1,0:T(8,128)(2,1)S(1)}, bf16[2,48,768]{2,1,0:T(8,128)(2,1)S(1)}, u32[]{:S(2)}, u32[]{:S(2)}) collective-permute-start(bf16[2,48,768]{2,1,0:T(8,128)(2,1)S(1)} %get-tuple-element.58), channel_id=1, source_target_pairs={{0,2},{1,3},{2,0},{3,1},{4,6},{5,7},{6,4},{7,5},{8,10},{9,11},{10,... | collective-permute-start | bytes 442376 | tf_op jit(solution)/shard_map/ppermute | solution.py:38
  53.1 6.7 %collective-permute-start.24 = (bf16[2,48,384]{2,1,0:T(8,128)(2,1)S(1)}, bf16[2,48,384]{2,1,0:T(8,128)(2,1)S(1)}, u32[]{:S(2)}, u32[]{:S(2)}) collective-permute-start(bf16[2,48,384]{2,1,0:T(8,128)(2,1)S(1)} %activate.8.own_ref), channel_id=1, source_target_pairs={{0,4},{1,5},{2,6},{3,7},{4,0},{5,1},{6,2},{7,3},{8,12},{9,13},{10,... | collective-permute-start | bytes 221192 | tf_op jit(solution)/shard_map/ppermute | solution.py:38
  59.8 14.3 %collective-permute-start.25 = (bf16[2,48,768]{2,1,0:T(8,128)(2,1)S(1)}, bf16[2,48,768]{2,1,0:T(8,128)(2,1)S(1)}, u32[]{:S(2)}, u32[]{:S(2)}) collective-permute-start(bf16[2,48,768]{2,1,0:T(8,128)(2,1)S(1)} %join.22.own_ref), channel_id=1, source_target_pairs={{0,2},{1,3},{2,0},{3,1},{4,6},{5,7},{6,4},{7,5},{8,10},{9,11},{10,... | collective-permute-start | bytes 442376 | tf_op jit(solution)/shard_map/ppermute | solution.py:38
  60.0 8.4 %collective-permute-start.29 = (bf16[2,48,384]{2,1,0:T(8,128)(2,1)S(1)}, bf16[2,48,384]{2,1,0:T(8,128)(2,1)S(1)}, u32[]{:S(2)}, u32[]{:S(2)}) collective-permute-start(bf16[2,48,384]{2,1,0:T(8,128)(2,1)S(1)} %get-tuple-element.64), channel_id=1, source_target_pairs={{0,4},{1,5},{2,6},{3,7},{4,0},{5,1},{6,2},{7,3},{8,12},{9,13},{10,... | collective-permute-start | bytes 221192 | tf_op jit(solution)/shard_map/ppermute | solution.py:38
  60.3 18.6 %copy-start = (bf16[32,1280]{1,0:T(8,128)(2,1)S(1)}, bf16[32,1280]{1,0:T(8,128)(2,1)}, u32[]{:S(2)}) copy-start(bf16[32,1280]{1,0:T(8,128)(2,1)} %param.5) | copy-start | bytes 245764
  60.3 18.6 %copy-start.1 = (bf16[32,1280]{1,0:T(8,128)(2,1)S(1)}, bf16[32,1280]{1,0:T(8,128)(2,1)}, u32[]{:S(2)}) copy-start(bf16[32,1280]{1,0:T(8,128)(2,1)} %param.4) | copy-start | bytes 245764
  60.3 11.2 %collective-permute-start.18 = (bf16[2,48,384]{2,1,0:T(8,128)(2,1)S(1)}, bf16[2,48,384]{2,1,0:T(8,128)(2,1)S(1)}, u32[]{:S(2)}, u32[]{:S(2)}) collective-permute-start(bf16[2,48,384]{2,1,0:T(8,128)(2,1)S(1)} %get-tuple-element.60), channel_id=1, source_target_pairs={{0,4},{1,5},{2,6},{3,7},{4,0},{5,1},{6,2},{7,3},{8,12},{9,13},{10,... | collective-permute-start | bytes 221192 | tf_op jit(solution)/shard_map/ppermute | solution.py:38
  68.5 7.8 %collective-permute-start.30 = (bf16[2,48,384]{2,1,0:T(8,128)(2,1)S(1)}, bf16[2,48,384]{2,1,0:T(8,128)(2,1)S(1)}, u32[]{:S(2)}, u32[]{:S(2)}) collective-permute-start(bf16[2,48,384]{2,1,0:T(8,128)(2,1)S(1)} %activate.9.own_ref), channel_id=1, source_target_pairs={{0,4},{1,5},{2,6},{3,7},{4,0},{5,1},{6,2},{7,3},{8,12},{9,13},{10,... | collective-permute-start | bytes 221192 | tf_op jit(solution)/shard_map/ppermute | solution.py:38
  71.6 7.2 %collective-permute-start.19 = (bf16[2,48,384]{2,1,0:T(8,128)(2,1)S(1)}, bf16[2,48,384]{2,1,0:T(8,128)(2,1)S(1)}, u32[]{:S(2)}, u32[]{:S(2)}) collective-permute-start(bf16[2,48,384]{2,1,0:T(8,128)(2,1)S(1)} %activate.7.own_ref), channel_id=1, source_target_pairs={{0,4},{1,5},{2,6},{3,7},{4,0},{5,1},{6,2},{7,3},{8,12},{9,13},{10,... | collective-permute-start | bytes 221192 | tf_op jit(solution)/shard_map/ppermute | solution.py:38
  71.7 4.5 %collective-permute-start.21 = (bf16[2,16,768]{2,1,0:T(8,128)(2,1)S(1)}, bf16[2,16,768]{2,1,0:T(8,128)(2,1)S(1)}, u32[]{:S(2)}, u32[]{:S(2)}) collective-permute-start(bf16[2,16,768]{2,1,0:T(8,128)(2,1)S(1)} %join.15.rest_0_.own_ref), channel_id=1, source_target_pairs={{0,2},{1,3},{2,0},{3,1},{4,6},{5,7},{6,4},{7,5},{8,10},{9,11},{10,... | collective-permute-start | bytes 147464 | tf_op jit(solution)/shard_map/ppermute | solution.py:38
  74.2 9.4 %collective-permute-start.26 = (bf16[2,48,1536]{2,1,0:T(8,128)(2,1)S(1)}, bf16[2,48,1536]{2,1,0:T(8,128)(2,1)S(1)}, u32[]{:S(2)}, u32[]{:S(2)}) collective-permute-start(bf16[2,48,1536]{2,1,0:T(8,128)(2,1)S(1)} %join.23.own_ref), channel_id=1, source_target_pairs={{0,1},{1,0},{2,3},{3,2},{4,5},{5,4},{6,7},{7,6},{8,9},{9,8},{10,11... | collective-permute-start | bytes 884744 | tf_op jit(solution)/shard_map/ppermute | solution.py:38
  74.2 5.8 %collective-permute-start.11 = (bf16[2,16,768]{2,1,0:T(8,128)(2,1)S(1)}, bf16[2,16,768]{2,1,0:T(8,128)(2,1)S(1)}, u32[]{:S(2)}, u32[]{:S(2)}) collective-permute-start(bf16[2,16,768]{2,1,0:T(8,128)(2,1)S(1)} %activate.6.own_ref.rest_0_), channel_id=1, source_target_pairs={{0,4},{1,5},{2,6},{3,7},{4,0},{5,1},{6,2},{7,3},{8,12},{9,13},{10,... | collective-permute-start | bytes 147464 | tf_op jit(solution)/shard_map/ppermute | solution.py:38
  76.2 4.9 %collective-permute-start.22 = (bf16[2,16,1536]{2,1,0:T(8,128)(2,1)S(1)}, bf16[2,16,1536]{2,1,0:T(8,128)(2,1)S(1)}, u32[]{:S(2)}, u32[]{:S(2)}) collective-permute-start(bf16[2,16,1536]{2,1,0:T(8,128)(2,1)S(1)} %join.20.own_ref), channel_id=1, source_target_pairs={{0,1},{1,0},{2,3},{3,2},{4,5},{5,4},{6,7},{7,6},{8,9},{9,8},{10,11... | collective-permute-start | bytes 294920 | tf_op jit(solution)/shard_map/ppermute | solution.py:38
  76.3 7.2 %collective-permute-start.31 = (bf16[2,48,768]{2,1,0:T(8,128)(2,1)S(1)}, bf16[2,48,768]{2,1,0:T(8,128)(2,1)S(1)}, u32[]{:S(2)}, u32[]{:S(2)}) collective-permute-start(bf16[2,48,768]{2,1,0:T(8,128)(2,1)S(1)} %join.26.own_ref), channel_id=1, source_target_pairs={{0,2},{1,3},{2,0},{3,1},{4,6},{5,7},{6,4},{7,5},{8,10},{9,11},{10,... | collective-permute-start | bytes 442376 | tf_op jit(solution)/shard_map/ppermute | solution.py:38
  78.8 8.7 %collective-permute-start.20 = (bf16[2,48,768]{2,1,0:T(8,128)(2,1)S(1)}, bf16[2,48,768]{2,1,0:T(8,128)(2,1)S(1)}, u32[]{:S(2)}, u32[]{:S(2)}) collective-permute-start(bf16[2,48,768]{2,1,0:T(8,128)(2,1)S(1)} %join.19.own_ref), channel_id=1, source_target_pairs={{0,2},{1,3},{2,0},{3,1},{4,6},{5,7},{6,4},{7,5},{8,10},{9,11},{10,... | collective-permute-start | bytes 442376 | tf_op jit(solution)/shard_map/ppermute | solution.py:38
  80.1 8.5 %collective-permute-start.12 = (bf16[2,16,1536]{2,1,0:T(8,128)(2,1)S(1)}, bf16[2,16,1536]{2,1,0:T(8,128)(2,1)S(1)}, u32[]{:S(2)}, u32[]{:S(2)}) collective-permute-start(bf16[2,16,1536]{2,1,0:T(8,128)(2,1)S(1)} %join.16.own_ref), channel_id=1, source_target_pairs={{0,2},{1,3},{2,0},{3,1},{4,6},{5,7},{6,4},{7,5},{8,10},{9,11},{10,... | collective-permute-start | bytes 294920 | tf_op jit(solution)/shard_map/ppermute | solution.py:38
  83.5 6.6 %collective-permute-start.32 = (bf16[2,48,1536]{2,1,0:T(8,128)(2,1)S(1)}, bf16[2,48,1536]{2,1,0:T(8,128)(2,1)S(1)}, u32[]{:S(2)}, u32[]{:S(2)}) collective-permute-start(bf16[2,48,1536]{2,1,0:T(8,128)(2,1)S(1)} %join.27.own_ref), channel_id=1, source_target_pairs={{0,1},{1,0},{2,3},{3,2},{4,5},{5,4},{6,7},{7,6},{8,9},{9,8},{10,11... | collective-permute-start | bytes 884744 | tf_op jit(solution)/shard_map/ppermute | solution.py:38
  87.6 6.5 %collective-permute-start.27 = (bf16[2,48,1536]{2,1,0:T(8,128)(2,1)S(1)}, bf16[2,48,1536]{2,1,0:T(8,128)(2,1)S(1)}, u32[]{:S(2)}, u32[]{:S(2)}) collective-permute-start(bf16[2,48,1536]{2,1,0:T(8,128)(2,1)S(1)} %join.25.own_ref), channel_id=1, source_target_pairs={{0,1},{1,0},{2,3},{3,2},{4,5},{5,4},{6,7},{7,6},{8,9},{9,8},{10,11... | collective-permute-start | bytes 884744 | tf_op jit(solution)/shard_map/ppermute | solution.py:38
  88.6 1.5 %collective-permute-start.13 = (bf16[2,16,3072]{2,1,0:T(8,128)(2,1)S(1)}, bf16[2,16,3072]{2,1,0:T(8,128)(2,1)S(1)}, u32[]{:S(2)}, u32[]{:S(2)}) collective-permute-start(bf16[2,16,3072]{2,1,0:T(8,128)(2,1)S(1)} %join.17.own_ref), channel_id=1, source_target_pairs={{0,1},{1,0},{2,3},{3,2},{4,5},{5,4},{6,7},{7,6},{8,9},{9,8},{10,11... | collective-permute-start | bytes 589832 | tf_op jit(solution)/shard_map/ppermute | solution.py:38
  98.3 15.3 %collective-permute-start.33 = (bf16[32,1280]{1,0:T(8,128)(2,1)S(1)}, bf16[32,1280]{1,0:T(8,128)(2,1)S(1)}, u32[]{:S(2)}, u32[]{:S(2)}) collective-permute-start(bf16[32,1280]{1,0:T(8,128)(2,1)S(1)} %get-tuple-element.67), channel_id=1, source_target_pairs={{0,8},{8,0},{16,24},{24,16},{1,9},{9,1},{17,25},{25,17},{2,10},{10... | collective-permute-start | bytes 245768 | tf_op jit(solution)/shard_map/ppermute | solution.py:38
  99.9 13.7 %collective-permute-start.35 = (bf16[32,1280]{1,0:T(8,128)(2,1)S(1)}, bf16[32,1280]{1,0:T(8,128)(2,1)S(1)}, u32[]{:S(2)}, u32[]{:S(2)}) collective-permute-start(bf16[32,1280]{1,0:T(8,128)(2,1)S(1)} %get-tuple-element.68), channel_id=1, source_target_pairs={{0,24},{8,16},{16,8},{24,0},{1,25},{9,17},{17,9},{25,1},{2,26},{10... | collective-permute-start | bytes 245768 | tf_op jit(solution)/shard_map/ppermute | solution.py:38
  101.4 12.2 %collective-permute-start.34 = (bf16[32,1280]{1,0:T(8,128)(2,1)S(1)}, bf16[32,1280]{1,0:T(8,128)(2,1)S(1)}, u32[]{:S(2)}, u32[]{:S(2)}) collective-permute-start(bf16[32,1280]{1,0:T(8,128)(2,1)S(1)} %get-tuple-element.69), channel_id=1, source_target_pairs={{0,16},{8,24},{16,0},{24,8},{1,17},{9,25},{17,1},{25,9},{2,18},{10... | collective-permute-start | bytes 245768 | tf_op jit(solution)/shard_map/ppermute | solution.py:38

commit v4 on v0

v4 whole, which is shorter than its diff:
```python
import functools
import math

import jax
import jax.numpy as jnp
from jax import lax
from jax.experimental import pallas as pl
from jax.experimental.pallas import tpu as pltpu
from jax.sharding import PartitionSpec as P

BF16 = jnp.bfloat16
F32 = jnp.float32
LOAD_BYTES = 38 * 1024 * 1024
CHUNKS = 4
PIECE = 384
VMEM_BYTES = 40 * 1024 * 1024
SMALL_BYTES = 16 * 1024 * 1024
SCALAR = pl.BlockSpec(memory_space=pltpu.SMEM)
ANY = pl.BlockSpec(memory_space=pl.ANY)
HBM = pl.BlockSpec(memory_space=pltpu.HBM)
VMEM = pl.BlockSpec(memory_space=pltpu.VMEM)


def gelu_parts(preact):
    cumul = 0.5 * (1.0 + jax.scipy.special.erf(preact * (1.0 / math.sqrt(2.0))))
    density = jnp.exp(-0.5 * preact * preact) * (1.0 / math.sqrt(2.0 * math.pi))
    return (preact * cumul, cumul + preact * density)


def contract(left, right, left_dim, right_dim):
    return lax.dot_general(
        left,
        right,
        (((left_dim,), (right_dim,)), ((), ())),
        preferred_element_type=F32,
    )


def exchange(array, axis, size, step):
    return lax.ppermute(array, axis, [(i, i ^ step) for i in range(size)])


def partner_step(level):
    return (1, 2, 6)[level] if level < 3 else 1 << level


def whole(*shape):
    return pl.BlockSpec(shape, lambda step: (0,) * len(shape))


def params(size=VMEM_BYTES):
    return pltpu.CompilerParams(vmem_limit_bytes=size)


def cost(flops, size):
    return pl.CostEstimate(
        flops=flops, bytes_accessed=size, transcendentals=0
    )


def by_side(rank_ref, level, choose):
    rank = rank_ref[0]
    side = (rank >> level) & 1
    if level == 1:
        side ^= (rank >> 2) & 1
    for value in range(2):
        pl.when(side == value)(functools.partial(choose, value))


def load(*weights):
    count = len(weights)

    def kernel(*refs):
        sources, targets, done = refs[:count], refs[count : 2 * count], refs[-1]
        copies = [
            pltpu.make_async_copy(source, target, done.at[index])
            for index, (source, target) in enumerate(zip(sources, targets))
        ]
        for copy in copies:
            copy.start()
        for copy in copies:
            copy.wait()

    return pl.pallas_call(
        kernel,
        out_shape=tuple(jax.ShapeDtypeStruct(w.shape, w.dtype) for w in weights),
        in_specs=[HBM] * count,
        out_specs=(VMEM,) * count,
        scratch_shapes=[pltpu.SemaphoreType.DMA((count,))],
        compiler_params=params(LOAD_BYTES),
        cost_estimate=cost(0, 4 * sum(w.size for w in weights)),
        name="load",
    )(*weights)


def pieces(start, width):
    return [(at, at + PIECE) for at in range(start, start + width, PIECE)]


def forward(rank, tokens, w_in, w_out, start, width, after=()):
    parts = len(tokens)
    rows, features = tokens[0].shape[1:]
    total = parts * rows
    half = total // 2

    def kernel(rank_ref, *refs):
        token_refs = refs[:parts]
        wi_ref, wo_ref = refs[parts : parts + 2]
        keep_ref, send_ref = refs[-2:]

        def rows_of(which):
            return jnp.concatenate([ref[which] for ref in token_refs], axis=0)

        for low, high in pieces(start, width):
            at = slice(low - start, high - start)
            sums = (
                contract(rows_of(0), wi_ref[:, low:high], 1, 0),
                contract(rows_of(1), wo_ref[low:high, :], 1, 1),
            )

            def choose(core, at=at, sums=sums):
                for which, value in enumerate(sums):
                    halves = value[:half], value[half:]
                    keep_ref[which, :, at] = halves[core]
                    send_ref[which, :, at] = halves[1 - core].astype(BF16)

            by_side(rank_ref, 0, choose)

    return pl.pallas_call(
        kernel,
        grid=(1,),
        out_shape=(
            jax.ShapeDtypeStruct((2, half, width), F32),
            jax.ShapeDtypeStruct((2, half, width), BF16),
        ),
        in_specs=[SCALAR]
        + [whole(2, rows, features)] * parts
        + [VMEM, VMEM]
        + [ANY] * len(after),
        out_specs=(whole(2, half, width),) * 2,
        compiler_params=params(SMALL_BYTES),
        cost_estimate=cost(4 * total * features * width, 4 * features * width),
        name="forward",
    )(rank, *tokens, w_in, w_out, *after)


def halve(rank, keep, received, level, after=()):
    _, rows, width = keep.shape
    half = rows // 2

    def kernel(rank_ref, keep_ref, received_ref, *rest):
        next_ref, send_ref = rest[-2:]

        def choose(side):
            mine = slice(side * half, (side + 1) * half)
            other = slice((1 - side) * half, (2 - side) * half)
            next_ref[...] = keep_ref[:, mine] + received_ref[:, mine].astype(F32)
            send_ref[...] = (
                keep_ref[:, other] + received_ref[:, other].astype(F32)
            ).astype(BF16)

        by_side(rank_ref, level, choose)

    return pl.pallas_call(
        kernel,
        grid=(1,),
        out_shape=(
            jax.ShapeDtypeStruct((2, half, width), F32),
            jax.ShapeDtypeStruct((2, half, width), BF16),
        ),
        in_specs=[SCALAR] + [whole(2, rows, width)] * 2 + [ANY] * len(after),
        out_specs=(whole(2, half, width),) * 2,
        compiler_params=params(SMALL_BYTES),
        cost_estimate=cost(2 * rows * width, 12 * rows * width),
        name="halve",
    )(rank, keep, received, *after)


def activate(keep, received, after=()):
    def kernel(keep_ref, received_ref, *rest):
        out_ref = rest[-1]
        value, slope = gelu_parts(keep_ref[0] + received_ref[0].astype(F32))
        grad = keep_ref[1] + received_ref[1].astype(F32)
        out_ref[0] = value.astype(BF16)
        out_ref[1] = (grad * slope).astype(BF16)

    return pl.pallas_call(
        kernel,
        grid=(1,),
        out_shape=jax.ShapeDtypeStruct(keep.shape, BF16),
        in_specs=[whole(*keep.shape)] * 2 + [ANY] * len(after),
        out_specs=whole(*keep.shape),
        compiler_params=params(SMALL_BYTES),
        cost_estimate=cost(20 * keep.size, 8 * keep.size),
        name="activate",
    )(keep, received, *after)


def relay(array, after):
    def kernel(in_ref, *rest):
        rest[-1][...] = in_ref[...]

    return pl.pallas_call(
        kernel,
        grid=(1,),
        out_shape=jax.ShapeDtypeStruct(array.shape, array.dtype),
        in_specs=[whole(*array.shape)] + [ANY] * len(after),
        out_specs=whole(*array.shape),
        compiler_params=params(SMALL_BYTES),
        cost_estimate=cost(0, 4 * array.size),
        name="relay",
    )(array, *after)


def join(rank, own, received, level, after=()):
    _, half, width = own.shape

    def kernel(rank_ref, own_ref, received_ref, *rest):
        out_ref = rest[-1]

        def choose(side):
            out_ref[:, side * half : (side + 1) * half] = own_ref[...]
            out_ref[:, (1 - side) * half : (2 - side) * half] = received_ref[...]

        by_side(rank_ref, level, choose)

    return pl.pallas_call(
        kernel,
        grid=(1,),
        out_shape=jax.ShapeDtypeStruct((2, 2 * half, width), BF16),
        in_specs=[SCALAR] + [whole(2, half, width)] * 2 + [ANY] * len(after),
        out_specs=whole(2, 2 * half, width),
        compiler_params=params(SMALL_BYTES),
        cost_estimate=cost(0, 8 * own.size),
        name="join",
    )(rank, own, received, *after)


class Chunk:
    def __init__(self, rank, mp, keep, send):
        self.rank, self.mp, self.levels = rank, mp, mp.bit_length() - 1
        self.keep, self.send, self.done = keep, send, 0

    def advance(self, after=()):
        index, self.done = self.done, self.done + 1
        level = min(index, 2 * self.levels - 1 - index)
        received = exchange(self.send, "mp", self.mp, partner_step(level))
        if index < self.levels - 1:
            self.keep, self.send = halve(
                self.rank, self.keep, received, level + 1, after
            )
        elif index == self.levels - 1:
            self.send = activate(self.keep, received, after)
        else:
            self.send = join(self.rank, self.send, received, level, after)
        return self.send

    def reach(self, done):
        while self.done < done:
            self.advance()


def input_grads(grads, w_in, carried, start):
    _, total, width = grads.shape
    features = w_in.shape[0]
    before = [] if carried is None else [carried]

    def kernel(grad_ref, wi_ref, *refs):
        value = refs[0][...] if before else 0.0
        for low, high in pieces(start, width):
            block = grad_ref[1, :, low - start : high - start]
            value = value + contract(block, wi_ref[:, low:high], 1, 1)
        refs[-1][...] = value

    return pl.pallas_call(
        kernel,
        grid=(1,),
        out_shape=jax.ShapeDtypeStruct((total, features), F32),
        in_specs=[whole(2, total, width), VMEM] + [whole(total, features)] * len(before),
        out_specs=whole(total, features),
        compiler_params=params(SMALL_BYTES),
        cost_estimate=cost(2 * total * features * width, 2 * features * width),
        name="input_grads",
    )(grads, w_in, *before)


def weight_grads(xt, gs, finals, factor):
    features, total = xt.shape
    width = finals[0].shape[2]
    hidden = width * len(finals)

    def kernel(xt_ref, gs_ref, *refs):
        in_ref, out_ref = refs[-2:]
        step = pl.program_id(0)

        def work(final_ref):
            for low, high in pieces(0, width):
                act, grad = final_ref[0, :, low:high], final_ref[1, :, low:high]
                turned = act.astype(F32).T.astype(BF16)
                in_ref[:, low:high] = (contract(xt_ref[...], grad, 1, 0) * factor).astype(BF16)
                out_ref[low:high, :] = (contract(turned, gs_ref[...], 1, 0) * factor).astype(BF16)

        for index in range(len(finals)):
            pl.when(step == index)(functools.partial(work, refs[index]))

    return pl.pallas_call(
        kernel,
        grid=(len(finals),),
        out_shape=(
            jax.ShapeDtypeStruct((features, hidden), BF16),
            jax.ShapeDtypeStruct((hidden, features), BF16),
        ),
        in_specs=[whole(features, total), whole(total, features)]
        + [whole(2, total, width)] * len(finals),
        out_specs=(
            pl.BlockSpec((features, width), lambda i: (0, i)),
            pl.BlockSpec((width, features), lambda i: (i, 0)),
        ),
        compiler_params=params(),
        cost_estimate=cost(4 * total * features * hidden, 4 * features * hidden),
        name="weight_grads",
    )(xt, gs, *finals)


def local(inputs, out_grads, w_in, w_out, dp, mp):
    hidden = w_in.shape[1]
    rows = inputs.shape[0]
    total = rows * dp
    factor = 1.0 / math.sqrt(total)
    rank = lax.axis_index("mp").astype(jnp.int32).reshape(1)
    width = hidden // CHUNKS
    starts = [index * width for index in range(CHUNKS)]

    own = jnp.stack([inputs, out_grads])
    parts = [own] + [exchange(own, "dp", dp, j) for j in range(1, dp)]

    w_in, w_out = load(w_in, w_out)

    chunks, after = [], []
    for start in starts:
        keep, send = forward(rank, parts, w_in, w_out, start, width, after)
        after = [send]
        for chunk in chunks[::-1]:
            after = [chunk.advance(after)]
        if chunks:
            after = [relay(send, after)]
            send = after[0]
        chunks.append(Chunk(rank, mp, keep, send))

    steps = 2 * chunks[0].levels
    partials, partial = [], None
    for index, (start, chunk) in enumerate(zip(starts, chunks)):
        chunk.reach(steps - 2)
        chunk.advance(partials[index - 2 : index - 1] if index > 1 else [])
        chunk.advance(partials[index - 1 :])
        partial = input_grads(chunk.send, w_in, partial, start)
        partials.append(partial)
    finals = [chunk.send for chunk in chunks]

    in_total = partial[:rows]
    for j in range(1, dp):
        part = partial[j * rows : (j + 1) * rows].astype(BF16)
        in_total = in_total + exchange(part, "dp", dp, j).astype(F32)

    tokens = jnp.concatenate(parts, axis=1)
    unit = jnp.eye(total, dtype=BF16)
    xt = contract(tokens[0], unit, 0, 1).astype(BF16)
    return (in_total, *weight_grads(xt, tokens[1], finals, factor))


def solution(mesh):
    sizes = dict(mesh.shape)
    return jax.shard_map(
        functools.partial(local, dp=sizes["dp"], mp=sizes["mp"]),
        mesh=mesh,
        in_specs=(P("dp", "mp"), P("dp", "mp"), P("mp", "dp"), P("dp", "mp")),
        out_specs=(P("dp", "mp"), P("mp", "dp"), P("dp", "mp")),
        check_vma=False,
    )
```

time: 196 us -> 102 us (0.52)
  waiting for transfers between devices: 107 us -> 25.3 us
  Pallas kernels: 0 us -> 36.1 us
  matrix products: 34.4 us -> 0.27 us
  starting transfers between devices: 0.08 us -> 32.9 us
  blocking collectives: 19.9 us -> 0 us
  between operations: 14 us -> 1.15 us
  local copies, waits for them, and re-layouts: 16.5 us -> 4.41 us
    psum x1 -> x0, waiting for transfers between devices: 107 us -> none  [local(): preact, grad_act = lax.psum((partial_pre, partial_grad), 'mp')]
    pallas_call x0 -> x37, Pallas kernels: none -> 36.1 us  [the longest x1 12.2 us: load(): pl.pallas_call(kernel, out_shape=tuple((jax.ShapeDtypeStruct(w.shape, w.d...]
    dot_general x5 -> x1, matrix products: 34.4 us -> 0.27 us  [contract(): lax.dot_general(left, right, (((left_dim,), (right_dim,)), ((), ())), pre...]
    ppermute x0 -> x30, starting transfers between devices: none -> 32.9 us  [exchange(): return lax.ppermute(array, axis, [(i, i ^ step) for i in range(size)])]
    ppermute x0 -> x30, waiting for transfers between devices: none -> 25.3 us  [exchange(): return lax.ppermute(array, axis, [(i, i ^ step) for i in range(size)])]
    all_gather x2 -> x0, blocking collectives: 19.9 us -> none  [the longest x1 11 us: local(): lax.all_gather(out_grads, 'dp', axis=0, tiled=True)]
    unnamed x5 -> x12, local copies, waits for them, and re-layouts: 16.5 us -> 4.37 us
    convert_element_type x1 -> x0, other arithmetic: 2.83 us -> none  [finish(): grad_preact = (grad_act * gelu_slope).astype(jnp.bfloat16)]
  transfers between devices with their start and end apart: 2 -> 30, of which waited for: 1 -> 11; matrix products, arithmetic and copies ran while one was open for 15% -> 0% of each run, Pallas kernels for 0% -> 32%
where the time goes in v4:
time: 102 us
  Pallas kernels  36.1 us (35%)
  starting transfers between devices  32.9 us (32%)
  waiting for transfers between devices  25.3 us (25%)
  local copies, waits for them, and re-layouts  4.41 us (4%)
  other arithmetic  1.74 us (2%)
  between operations  1.15 us (1%)
    ppermute x30, starting transfers between devices, exchange(): return lax.ppermute(array, axis, [(i, i ^ step) for i in range(size)])  32.9 us
    ppermute x30, waiting for transfers between devices, exchange(): return lax.ppermute(array, axis, [(i, i ^ step) for i in range(size)])  25.3 us
    pallas_call x1, Pallas kernels, load(): pl.pallas_call(kernel, out_shape=tuple((jax.ShapeDtypeStruct(w.shape, w.d...  12.2 us
    pallas_call x1, Pallas kernels, weight_grads(): pl.pallas_call(kernel, grid=(len(finals),), out_shape=(jax.ShapeDtypeStru...  10.3 us
    pallas_call x4, Pallas kernels, forward(): pl.pallas_call(kernel, grid=(1,), out_shape=(jax.ShapeDtypeStruct((2, hal...  8.4 us
    unnamed x12, local copies, waits for them, and re-layouts  4.37 us
    pallas_call x4, Pallas kernels, input_grads(): pl.pallas_call(kernel, grid=(1,), out_shape=jax.ShapeDtypeStruct((total,...  3.88 us
  transfers between devices with their start and end apart: 30, of which 11 were waited for; matrix products, arithmetic and copies ran while one was open for 0% of the time, Pallas kernels for 32%

profile of v4, /device:TPU:0, one launch (start us, length us, event | category | flops | bytes accessed | tf_op | source)
XLA Modules:
  0.0 101.8 jit_solution(1732908699669686525)
XLA Ops:
  0.6 0.9 pad_maximum_fusion.1.refs_0_
  1.6 3.0 %collective-permute-start = (bf16[2,32,1280]{2,1,0:T(8,128)(2,1)S(1)}, bf16[2,32,1280]{2,1,0:T(8,128)(2,1)S(1)}, u32[]{:S(2)}, u32[]{:S(2)}) collective-permute-start(bf16[2,32,1280]{2,1,0:T(8,128)(2,1)S(1)} %pad_maximum_fusion.1.refs_0_), channel_id=1, source_target_pairs={{0,8},{8,0},{16,24},{24,16},{1,9},{9,1},{17,25},{25,17},{2,10},{10... | collective-permute-start | bytes 491528 | tf_op jit(solution)/shard_map/ppermute | solution.py:40
  4.6 1.5 %collective-permute-start.1 = (bf16[2,32,1280]{2,1,0:T(8,128)(2,1)S(1)}, bf16[2,32,1280]{2,1,0:T(8,128)(2,1)S(1)}, u32[]{:S(2)}, u32[]{:S(2)}) collective-permute-start(bf16[2,32,1280]{2,1,0:T(8,128)(2,1)S(1)} %pad_maximum_fusion.1.refs_0_), channel_id=1, source_target_pairs={{0,16},{8,24},{16,0},{24,8},{1,17},{9,25},{17,1},{25,9},{2,18},{10... | collective-permute-start | bytes 491528 | tf_op jit(solution)/shard_map/ppermute | solution.py:40
  6.1 12.2 %load.1 = (bf16[1280,4608]{1,0:T(8,128)(2,1)S(1)}, bf16[4608,1280]{1,0:T(8,128)(2,1)}) custom-call(bf16[1280,4608]{1,0:T(8,128)(2,1)} %refs_0_.1, bf16[4608,1280]{1,0:T(8,128)(2,1)} %refs_1_.1), custom_call_target="tpu_custom_call" | custom-call | bytes 47185920 | tf_op jit(solution)/shard_map/load/pallas_call | solution.py:84
  18.4 4.3 %copy-done = bf16[4608,1280]{1,0:T(8,128)(2,1)S(1)} copy-done((bf16[4608,1280]{1,0:T(8,128)(2,1)S(1)}, bf16[4608,1280]{1,0:T(8,128)(2,1)}, u32[]{:S(2)}) %copy-start) | copy-done | bytes 11796504
  22.8 2.1 %forward.4 = (f32[2,64,1152]{2,1,0:T(8,128)S(1)}, bf16[2,64,1152]{2,1,0:T(8,128)(2,1)S(1)}) custom-call(s32[1]{0:T(128)} %bitcast.rank_ref, bf16[2,32,1280]{2,1,0:T(8,128)(2,1)S(1)} %pad_maximum_fusion.1.refs_0_, bf16[2,32,1280]{2,1,0:T(8,128)(2,1)S(1)} %collective-permute-done.refs_1_, bf16[2,32,1280]{2,1,0:T(8,128)(2,1)S(1)} %collective-permute-done.1.refs_2_, ...), custom_call_target="tpu_custom_call" | custom-call | flops 754974720 | bytes 5898240 | tf_op jit(solution)/shard_map/forward/pallas_call | solution.py:129
  25.0 2.1 %forward.5 = (f32[2,64,1152]{2,1,0:T(8,128)S(1)}, bf16[2,64,1152]{2,1,0:T(8,128)(2,1)S(1)}) custom-call(s32[1]{0:T(128)} %bitcast.rank_ref, bf16[2,32,1280]{2,1,0:T(8,128)(2,1)S(1)} %pad_maximum_fusion.1.refs_0_, bf16[2,32,1280]{2,1,0:T(8,128)(2,1)S(1)} %collective-permute-done.refs_1_, bf16[2,32,1280]{2,1,0:T(8,128)(2,1)S(1)} %collective-permute-done.1.refs_2_, ...), custom_call_target="tpu_custom_call" | custom-call | flops 754974720 | bytes 5898240 | tf_op jit(solution)/shard_map/forward/pallas_call | solution.py:129
  27.2 0.6 collective-permute-start.5
  27.8 2.0 %collective-permute-start.4 = (bf16[2,32,1152]{2,1,0:T(8,128)(2,1)S(1)}, bf16[2,32,1152]{2,1,0:T(8,128)(2,1)S(1)}, u32[]{:S(2)}, u32[]{:S(2)}) collective-permute-start(bf16[2,32,1152]{2,1,0:T(8,128)(2,1)S(1)} %get-tuple-element.36.rest_0_), channel_id=1, source_target_pairs={{0,2},{1,3},{2,0},{3,1},{4,6},{5,7},{6,4},{7,5},{8,10},{9,11},{10,... | collective-permute-start | bytes 442376 | tf_op jit(solution)/shard_map/ppermute | solution.py:40
  29.9 2.1 %forward.6 = (f32[2,64,1152]{2,1,0:T(8,128)S(1)}, bf16[2,64,1152]{2,1,0:T(8,128)(2,1)S(1)}) custom-call(s32[1]{0:T(128)} %bitcast.rank_ref, bf16[2,32,1280]{2,1,0:T(8,128)(2,1)S(1)} %pad_maximum_fusion.1.refs_0_, bf16[2,32,1280]{2,1,0:T(8,128)(2,1)S(1)} %collective-permute-done.refs_1_, bf16[2,32,1280]{2,1,0:T(8,128)(2,1)S(1)} %collective-permute-done.1.refs_2_, ...), custom_call_target="tpu_custom_call" | custom-call | flops 754974720 | bytes 5898240 | tf_op jit(solution)/shard_map/forward/pallas_call | solution.py:129
  32.0 0.1 halve.9
  32.1 1.9 %collective-permute-done.4.received_ref = bf16[2,32,1152]{2,1,0:T(8,128)(2,1)S(1)} collective-permute-done((bf16[2,32,1152]{2,1,0:T(8,128)(2,1)S(1)}, bf16[2,32,1152]{2,1,0:T(8,128)(2,1)S(1)}, u32[]{:S(2)}, u32[]{:S(2)}) %collective-permute-start.4) | collective-permute-done | bytes 147488 | tf_op jit(solution)/shard_map/ppermute | solution.py:40
  34.1 1.8 %collective-permute-start.7 = (bf16[2,32,1152]{2,1,0:T(8,128)(2,1)S(1)}, bf16[2,32,1152]{2,1,0:T(8,128)(2,1)S(1)}, u32[]{:S(2)}, u32[]{:S(2)}) collective-permute-start(bf16[2,32,1152]{2,1,0:T(8,128)(2,1)S(1)} %get-tuple-element.40.rest_0_), channel_id=1, source_target_pairs={{0,2},{1,3},{2,0},{3,1},{4,6},{5,7},{6,4},{7,5},{8,10},{9,11},{10,... | collective-permute-start | bytes 442376 | tf_op jit(solution)/shard_map/ppermute | solution.py:40
  35.9 2.5 %collective-permute-start.6 = (bf16[2,16,1152]{2,1,0:T(8,128)(2,1)S(1)}, bf16[2,16,1152]{2,1,0:T(8,128)(2,1)S(1)}, u32[]{:S(2)}, u32[]{:S(2)}) collective-permute-start(bf16[2,16,1152]{2,1,0:T(8,128)(2,1)S(1)} %get-tuple-element.41.rest_0_), channel_id=1, source_target_pairs={{0,6},{1,7},{2,4},{3,5},{4,2},{5,3},{6,0},{7,1},{8,14},{9,15},{10,... | collective-permute-start | bytes 221192 | tf_op jit(solution)/shard_map/ppermute | solution.py:40
  38.4 2.1 %forward.7 = (f32[2,64,1152]{2,1,0:T(8,128)S(1)}, bf16[2,64,1152]{2,1,0:T(8,128)(2,1)S(1)}) custom-call(s32[1]{0:T(128)} %bitcast.rank_ref, bf16[2,32,1280]{2,1,0:T(8,128)(2,1)S(1)} %pad_maximum_fusion.1.refs_0_, bf16[2,32,1280]{2,1,0:T(8,128)(2,1)S(1)} %collective-permute-done.refs_1_, bf16[2,32,1280]{2,1,0:T(8,128)(2,1)S(1)} %collective-permute-done.1.refs_2_, ...), custom_call_target="tpu_custom_call" | custom-call | flops 754974720 | bytes 5898240 | tf_op jit(solution)/shard_map/forward/pallas_call | solution.py:129
  40.5 0.1 halve.11
  40.6 3.5 %collective-permute-done.6.received_ref = bf16[2,16,1152]{2,1,0:T(8,128)(2,1)S(1)} collective-permute-done((bf16[2,16,1152]{2,1,0:T(8,128)(2,1)S(1)}, bf16[2,16,1152]{2,1,0:T(8,128)(2,1)S(1)}, u32[]{:S(2)}, u32[]{:S(2)}) %collective-permute-start.6) | collective-permute-done | bytes 73760 | tf_op jit(solution)/shard_map/ppermute | solution.py:40
  44.3 1.7 %collective-permute-start.14 = (bf16[2,16,1152]{2,1,0:T(8,128)(2,1)S(1)}, bf16[2,16,1152]{2,1,0:T(8,128)(2,1)S(1)}, u32[]{:S(2)}, u32[]{:S(2)}) collective-permute-start(bf16[2,16,1152]{2,1,0:T(8,128)(2,1)S(1)} %get-tuple-element.48.rest_0_), channel_id=1, source_target_pairs={{0,6},{1,7},{2,4},{3,5},{4,2},{5,3},{6,0},{7,1},{8,14},{9,15},{10,... | collective-permute-start | bytes 221192 | tf_op jit(solution)/shard_map/ppermute | solution.py:40
  46.1 2.1 %collective-permute-start.10 = (bf16[2,32,1152]{2,1,0:T(8,128)(2,1)S(1)}, bf16[2,32,1152]{2,1,0:T(8,128)(2,1)S(1)}, u32[]{:S(2)}, u32[]{:S(2)}) collective-permute-start(bf16[2,32,1152]{2,1,0:T(8,128)(2,1)S(1)} %get-tuple-element.50), channel_id=1, source_target_pairs={{0,2},{1,3},{2,0},{3,1},{4,6},{5,7},{6,4},{7,5},{8,10},{9,11},{10,... | collective-permute-start | bytes 442376 | tf_op jit(solution)/shard_map/ppermute | solution.py:40
  48.1 2.2 %collective-permute-start.18 = (bf16[2,16,1152]{2,1,0:T(8,128)(2,1)S(1)}, bf16[2,16,1152]{2,1,0:T(8,128)(2,1)S(1)}, u32[]{:S(2)}, u32[]{:S(2)}) collective-permute-start(bf16[2,16,1152]{2,1,0:T(8,128)(2,1)S(1)} %activate.4.rest_0_.own_ref), channel_id=1, source_target_pairs={{0,6},{1,7},{2,4},{3,5},{4,2},{5,3},{6,0},{7,1},{8,14},{9,15},{10,... | collective-permute-start | bytes 221192 | tf_op jit(solution)/shard_map/ppermute | solution.py:40
  50.3 0.9 collective-permute-done.14.received_ref
  51.3 1.7 %collective-permute-start.15 = (bf16[2,16,1152]{2,1,0:T(8,128)(2,1)S(1)}, bf16[2,16,1152]{2,1,0:T(8,128)(2,1)S(1)}, u32[]{:S(2)}, u32[]{:S(2)}) collective-permute-start(bf16[2,16,1152]{2,1,0:T(8,128)(2,1)S(1)} %activate.6.own_ref), channel_id=1, source_target_pairs={{0,6},{1,7},{2,4},{3,5},{4,2},{5,3},{6,0},{7,1},{8,14},{9,15},{10,... | collective-permute-start | bytes 221192 | tf_op jit(solution)/shard_map/ppermute | solution.py:40
  53.0 6.1 %collective-permute-done.18.received_ref = bf16[2,16,1152]{2,1,0:T(8,128)(2,1)S(1)} collective-permute-done((bf16[2,16,1152]{2,1,0:T(8,128)(2,1)S(1)}, bf16[2,16,1152]{2,1,0:T(8,128)(2,1)S(1)}, u32[]{:S(2)}, u32[]{:S(2)}) %collective-permute-start.18) | collective-permute-done | bytes 73760 | tf_op jit(solution)/shard_map/ppermute | solution.py:40
  59.2 1.0 %collective-permute-done.15.received_ref = bf16[2,16,1152]{2,1,0:T(8,128)(2,1)S(1)} collective-permute-done((bf16[2,16,1152]{2,1,0:T(8,128)(2,1)S(1)}, bf16[2,16,1152]{2,1,0:T(8,128)(2,1)S(1)}, u32[]{:S(2)}, u32[]{:S(2)}) %collective-permute-start.15) | collective-permute-done | bytes 73760 | tf_op jit(solution)/shard_map/ppermute | solution.py:40
  60.3 1.1 %collective-permute-start.16 = (bf16[2,32,1152]{2,1,0:T(8,128)(2,1)S(1)}, bf16[2,32,1152]{2,1,0:T(8,128)(2,1)S(1)}, u32[]{:S(2)}, u32[]{:S(2)}) collective-permute-start(bf16[2,32,1152]{2,1,0:T(8,128)(2,1)S(1)} %join.13.own_ref), channel_id=1, source_target_pairs={{0,2},{1,3},{2,0},{3,1},{4,6},{5,7},{6,4},{7,5},{8,10},{9,11},{10,... | collective-permute-start | bytes 442376 | tf_op jit(solution)/shard_map/ppermute | solution.py:40
  61.4 1.7 %collective-permute-start.23 = (bf16[2,16,1152]{2,1,0:T(8,128)(2,1)S(1)}, bf16[2,16,1152]{2,1,0:T(8,128)(2,1)S(1)}, u32[]{:S(2)}, u32[]{:S(2)}) collective-permute-start(bf16[2,16,1152]{2,1,0:T(8,128)(2,1)S(1)} %get-tuple-element.56), channel_id=1, source_target_pairs={{0,6},{1,7},{2,4},{3,5},{4,2},{5,3},{6,0},{7,1},{8,14},{9,15},{10,... | collective-permute-start | bytes 221192 | tf_op jit(solution)/shard_map/ppermute | solution.py:40
  63.1 2.3 %collective-permute-start.11 = (bf16[2,16,1152]{2,1,0:T(8,128)(2,1)S(1)}, bf16[2,16,1152]{2,1,0:T(8,128)(2,1)S(1)}, u32[]{:S(2)}, u32[]{:S(2)}) collective-permute-start(bf16[2,16,1152]{2,1,0:T(8,128)(2,1)S(1)} %get-tuple-element.52), channel_id=1, source_target_pairs={{0,6},{1,7},{2,4},{3,5},{4,2},{5,3},{6,0},{7,1},{8,14},{9,15},{10,... | collective-permute-start | bytes 221192 | tf_op jit(solution)/shard_map/ppermute | solution.py:40
  65.4 4.3 %collective-permute-done.23.received_ref = bf16[2,16,1152]{2,1,0:T(8,128)(2,1)S(1)} collective-permute-done((bf16[2,16,1152]{2,1,0:T(8,128)(2,1)S(1)}, bf16[2,16,1152]{2,1,0:T(8,128)(2,1)S(1)}, u32[]{:S(2)}, u32[]{:S(2)}) %collective-permute-start.23) | collective-permute-done | bytes 73760 | tf_op jit(solution)/shard_map/ppermute | solution.py:40
  69.8 2.2 %collective-permute-start.24 = (bf16[2,16,1152]{2,1,0:T(8,128)(2,1)S(1)}, bf16[2,16,1152]{2,1,0:T(8,128)(2,1)S(1)}, u32[]{:S(2)}, u32[]{:S(2)}) collective-permute-start(bf16[2,16,1152]{2,1,0:T(8,128)(2,1)S(1)} %activate.7.own_ref), channel_id=1, source_target_pairs={{0,6},{1,7},{2,4},{3,5},{4,2},{5,3},{6,0},{7,1},{8,14},{9,15},{10,... | collective-permute-start | bytes 221192 | tf_op jit(solution)/shard_map/ppermute | solution.py:40
  72.1 1.7 %collective-permute-start.12 = (bf16[2,16,1152]{2,1,0:T(8,128)(2,1)S(1)}, bf16[2,16,1152]{2,1,0:T(8,128)(2,1)S(1)}, u32[]{:S(2)}, u32[]{:S(2)}) collective-permute-start(bf16[2,16,1152]{2,1,0:T(8,128)(2,1)S(1)} %activate.5.own_ref), channel_id=1, source_target_pairs={{0,6},{1,7},{2,4},{3,5},{4,2},{5,3},{6,0},{7,1},{8,14},{9,15},{10,... | collective-permute-start | bytes 221192 | tf_op jit(solution)/shard_map/ppermute | solution.py:40
  73.9 0.5 collective-permute-start.17
  74.5 1.5 %collective-permute-done.24.received_ref = bf16[2,16,1152]{2,1,0:T(8,128)(2,1)S(1)} collective-permute-done((bf16[2,16,1152]{2,1,0:T(8,128)(2,1)S(1)}, bf16[2,16,1152]{2,1,0:T(8,128)(2,1)S(1)}, u32[]{:S(2)}, u32[]{:S(2)}) %collective-permute-start.24) | collective-permute-done | bytes 73760 | tf_op jit(solution)/shard_map/ppermute | solution.py:40
  76.1 2.8 %collective-permute-done.12.received_ref = bf16[2,16,1152]{2,1,0:T(8,128)(2,1)S(1)} collective-permute-done((bf16[2,16,1152]{2,1,0:T(8,128)(2,1)S(1)}, bf16[2,16,1152]{2,1,0:T(8,128)(2,1)S(1)}, u32[]{:S(2)}, u32[]{:S(2)}) %collective-permute-start.12) | collective-permute-done | bytes 73760 | tf_op jit(solution)/shard_map/ppermute | solution.py:40
  79.2 1.0 input_grads.4.rest_0_.refs_0_
  80.2 2.6 %collective-permute-done.25.received_ref = bf16[2,32,1152]{2,1,0:T(8,128)(2,1)S(1)} collective-permute-done((bf16[2,32,1152]{2,1,0:T(8,128)(2,1)S(1)}, bf16[2,32,1152]{2,1,0:T(8,128)(2,1)S(1)}, u32[]{:S(2)}, u32[]{:S(2)}) %collective-permute-start.25) | collective-permute-done | bytes 147488 | tf_op jit(solution)/shard_map/ppermute | solution.py:40
  82.9 1.0 input_grads.5.rest_0_.refs_0_
  83.9 0.4 collective-permute-done.13.received_ref
  84.3 0.1 collective-permute-start.21
  84.5 0.3 convolution_convert_fusion.xt_ref
  84.9 1.0 input_grads.6.rest_0_.refs_0_
  85.8 0.2 collective-permute-done.21.received_ref
  86.0 0.2 join.23.grad_ref.refs_3_
  86.2 1.0 input_grads.7
  87.3 2.5 %collective-permute-start.29 = (bf16[32,1280]{1,0:T(8,128)(2,1)S(1)}, bf16[32,1280]{1,0:T(8,128)(2,1)S(1)}, u32[]{:S(2)}, u32[]{:S(2)}) collective-permute-start(bf16[32,1280]{1,0:T(8,128)(2,1)S(1)} %get-tuple-element.60), channel_id=1, source_target_pairs={{0,24},{8,16},{16,8},{24,0},{1,25},{9,17},{17,9},{25,1},{2,26},{10... | collective-permute-start | bytes 245768 | tf_op jit(solution)/shard_map/ppermute | solution.py:40
  89.8 0.5 collective-permute-start.28
  90.3 0.5 collective-permute-start.27
  90.8 10.3 %weight_grads.1 = (bf16[1280,4608]{1,0:T(8,128)(2,1)}, bf16[4608,1280]{1,0:T(8,128)(2,1)}) custom-call(bf16[1280,128]{1,0:T(8,128)(2,1)S(1)} %convolution_convert_fusion.xt_ref, bf16[128,1280]{1,0:T(8,128)(2,1)S(1)} %slice_bitcast_fusion.gs_ref, bf16[2,128,1152]{2,1,0:T(8,128)(2,1)S(1)} %join.17.grad_ref.refs_0_, ...), custom_call_target="tpu_custom_call" | custom-call | flops 3019898880 | bytes 23592960 | tf_op jit(solution)/shard_map/weight_grads/pallas_call | solution.py:306
  101.1 0.7 fusion.1
  (69 shorter events, 1.7 us)
Async XLA Ops:
  1.6 16.8 %collective-permute-start = (bf16[2,32,1280]{2,1,0:T(8,128)(2,1)S(1)}, bf16[2,32,1280]{2,1,0:T(8,128)(2,1)S(1)}, u32[]{:S(2)}, u32[]{:S(2)}) collective-permute-start(bf16[2,32,1280]{2,1,0:T(8,128)(2,1)S(1)} %pad_maximum_fusion.1.refs_0_), channel_id=1, source_target_pairs={{0,8},{8,0},{16,24},{24,16},{1,9},{9,1},{17,25},{25,17},{2,10},{10... | collective-permute-start | bytes 491528 | tf_op jit(solution)/shard_map/ppermute | solution.py:40
  4.6 13.8 %collective-permute-start.1 = (bf16[2,32,1280]{2,1,0:T(8,128)(2,1)S(1)}, bf16[2,32,1280]{2,1,0:T(8,128)(2,1)S(1)}, u32[]{:S(2)}, u32[]{:S(2)}) collective-permute-start(bf16[2,32,1280]{2,1,0:T(8,128)(2,1)S(1)} %pad_maximum_fusion.1.refs_0_), channel_id=1, source_target_pairs={{0,16},{8,24},{16,0},{24,8},{1,17},{9,25},{17,1},{25,9},{2,18},{10... | collective-permute-start | bytes 491528 | tf_op jit(solution)/shard_map/ppermute | solution.py:40
  6.1 12.3 %collective-permute-start.2 = (bf16[2,32,1280]{2,1,0:T(8,128)(2,1)S(1)}, bf16[2,32,1280]{2,1,0:T(8,128)(2,1)S(1)}, u32[]{:S(2)}, u32[]{:S(2)}) collective-permute-start(bf16[2,32,1280]{2,1,0:T(8,128)(2,1)S(1)} %pad_maximum_fusion.1.refs_0_), channel_id=1, source_target_pairs={{0,24},{8,16},{16,8},{24,0},{1,25},{9,17},{17,9},{25,1},{2,26},{10... | collective-permute-start | bytes 491528 | tf_op jit(solution)/shard_map/ppermute | solution.py:40
  18.4 4.4 %copy-start = (bf16[4608,1280]{1,0:T(8,128)(2,1)S(1)}, bf16[4608,1280]{1,0:T(8,128)(2,1)}, u32[]{:S(2)}) copy-start(bf16[4608,1280]{1,0:T(8,128)(2,1)} %get-tuple-element.32.refs_5_) | copy-start | bytes 35389444
  24.9 5.0 %slice-start = ((s8[11796480]{0:T(1024)(128)(4,1)}), s8[4194304]{0:T(1024)(128)(4,1)S(1)}, s32[]{:S(2)}) async-start(s8[11796480]{0:T(1024)(128)(4,1)} %bitcast.8), calls=%async_computation | async-start | bytes 8388608
  24.9 5.0 %slice-start.1 = ((s8[11796480]{0:T(1024)(128)(4,1)}), s8[4194304]{0:T(1024)(128)(4,1)S(1)}, s32[]{:S(2)}) async-start(s8[11796480]{0:T(1024)(128)(4,1)} %bitcast.8), calls=%async_computation.1 | async-start | bytes 8388608
  24.9 5.0 %slice-start.2 = ((s8[11796480]{0:T(1024)(128)(4,1)}), s8[3407872]{0:T(1024)(128)(4,1)S(1)}, s32[]{:S(2)}) async-start(s8[11796480]{0:T(1024)(128)(4,1)} %bitcast.8), calls=%async_computation.2 | async-start | bytes 6815744
  24.9 2.2 %collective-permute-start.3 = (bf16[2,64,1152]{2,1,0:T(8,128)(2,1)S(1)}, bf16[2,64,1152]{2,1,0:T(8,128)(2,1)S(1)}, u32[]{:S(2)}, u32[]{:S(2)}) collective-permute-start(bf16[2,64,1152]{2,1,0:T(8,128)(2,1)S(1)} %get-tuple-element.33.refs_6_), channel_id=1, source_target_pairs={{0,1},{1,0},{2,3},{3,2},{4,5},{5,4},{6,7},{7,6},{8,9},{9,8},{10,11... | collective-permute-start | bytes 884744 | tf_op jit(solution)/shard_map/ppermute | solution.py:40
  27.2 4.8 %collective-permute-start.5 = (bf16[2,64,1152]{2,1,0:T(8,128)(2,1)S(1)}, bf16[2,64,1152]{2,1,0:T(8,128)(2,1)S(1)}, u32[]{:S(2)}, u32[]{:S(2)}) collective-permute-start(bf16[2,64,1152]{2,1,0:T(8,128)(2,1)S(1)} %relay.3.refs_6_), channel_id=1, source_target_pairs={{0,1},{1,0},{2,3},{3,2},{4,5},{5,4},{6,7},{7,6},{8,9},{9,8},{10,11... | collective-permute-start | bytes 884744 | tf_op jit(solution)/shard_map/ppermute | solution.py:40
  27.8 6.1 %collective-permute-start.4 = (bf16[2,32,1152]{2,1,0:T(8,128)(2,1)S(1)}, bf16[2,32,1152]{2,1,0:T(8,128)(2,1)S(1)}, u32[]{:S(2)}, u32[]{:S(2)}) collective-permute-start(bf16[2,32,1152]{2,1,0:T(8,128)(2,1)S(1)} %get-tuple-element.36.rest_0_), channel_id=1, source_target_pairs={{0,2},{1,3},{2,0},{3,1},{4,6},{5,7},{6,4},{7,5},{8,10},{9,11},{10,... | collective-permute-start | bytes 442376 | tf_op jit(solution)/shard_map/ppermute | solution.py:40
  34.0 6.5 %collective-permute-start.8 = (bf16[2,64,1152]{2,1,0:T(8,128)(2,1)S(1)}, bf16[2,64,1152]{2,1,0:T(8,128)(2,1)S(1)}, u32[]{:S(2)}, u32[]{:S(2)}) collective-permute-start(bf16[2,64,1152]{2,1,0:T(8,128)(2,1)S(1)} %relay.4.refs_6_), channel_id=1, source_target_pairs={{0,1},{1,0},{2,3},{3,2},{4,5},{5,4},{6,7},{7,6},{8,9},{9,8},{10,11... | collective-permute-start | bytes 884744 | tf_op jit(solution)/shard_map/ppermute | solution.py:40
  34.1 6.5 %collective-permute-start.7 = (bf16[2,32,1152]{2,1,0:T(8,128)(2,1)S(1)}, bf16[2,32,1152]{2,1,0:T(8,128)(2,1)S(1)}, u32[]{:S(2)}, u32[]{:S(2)}) collective-permute-start(bf16[2,32,1152]{2,1,0:T(8,128)(2,1)S(1)} %get-tuple-element.40.rest_0_), channel_id=1, source_target_pairs={{0,2},{1,3},{2,0},{3,1},{4,6},{5,7},{6,4},{7,5},{8,10},{9,11},{10,... | collective-permute-start | bytes 442376 | tf_op jit(solution)/shard_map/ppermute | solution.py:40
  35.9 8.2 %collective-permute-start.6 = (bf16[2,16,1152]{2,1,0:T(8,128)(2,1)S(1)}, bf16[2,16,1152]{2,1,0:T(8,128)(2,1)S(1)}, u32[]{:S(2)}, u32[]{:S(2)}) collective-permute-start(bf16[2,16,1152]{2,1,0:T(8,128)(2,1)S(1)} %get-tuple-element.41.rest_0_), channel_id=1, source_target_pairs={{0,6},{1,7},{2,4},{3,5},{4,2},{5,3},{6,0},{7,1},{8,14},{9,15},{10,... | collective-permute-start | bytes 221192 | tf_op jit(solution)/shard_map/ppermute | solution.py:40
  44.2 1.8 %collective-permute-start.9 = (bf16[2,64,1152]{2,1,0:T(8,128)(2,1)S(1)}, bf16[2,64,1152]{2,1,0:T(8,128)(2,1)S(1)}, u32[]{:S(2)}, u32[]{:S(2)}) collective-permute-start(bf16[2,64,1152]{2,1,0:T(8,128)(2,1)S(1)} %relay.5), channel_id=1, source_target_pairs={{0,1},{1,0},{2,3},{3,2},{4,5},{5,4},{6,7},{7,6},{8,9},{9,8},{10,11... | collective-permute-start | bytes 884744 | tf_op jit(solution)/shard_map/ppermute | solution.py:40
  44.3 6.9 %collective-permute-start.14 = (bf16[2,16,1152]{2,1,0:T(8,128)(2,1)S(1)}, bf16[2,16,1152]{2,1,0:T(8,128)(2,1)S(1)}, u32[]{:S(2)}, u32[]{:S(2)}) collective-permute-start(bf16[2,16,1152]{2,1,0:T(8,128)(2,1)S(1)} %get-tuple-element.48.rest_0_), channel_id=1, source_target_pairs={{0,6},{1,7},{2,4},{3,5},{4,2},{5,3},{6,0},{7,1},{8,14},{9,15},{10,... | collective-permute-start | bytes 221192 | tf_op jit(solution)/shard_map/ppermute | solution.py:40
  46.0 15.3 %collective-permute-start.22 = (bf16[2,32,1152]{2,1,0:T(8,128)(2,1)S(1)}, bf16[2,32,1152]{2,1,0:T(8,128)(2,1)S(1)}, u32[]{:S(2)}, u32[]{:S(2)}) collective-permute-start(bf16[2,32,1152]{2,1,0:T(8,128)(2,1)S(1)} %get-tuple-element.47.rest_0_), channel_id=1, source_target_pairs={{0,2},{1,3},{2,0},{3,1},{4,6},{5,7},{6,4},{7,5},{8,10},{9,11},{10,... | collective-permute-start | bytes 442376 | tf_op jit(solution)/shard_map/ppermute | solution.py:40
  46.1 17.0 %collective-permute-start.10 = (bf16[2,32,1152]{2,1,0:T(8,128)(2,1)S(1)}, bf16[2,32,1152]{2,1,0:T(8,128)(2,1)S(1)}, u32[]{:S(2)}, u32[]{:S(2)}) collective-permute-start(bf16[2,32,1152]{2,1,0:T(8,128)(2,1)S(1)} %get-tuple-element.50), channel_id=1, source_target_pairs={{0,2},{1,3},{2,0},{3,1},{4,6},{5,7},{6,4},{7,5},{8,10},{9,11},{10,... | collective-permute-start | bytes 442376 | tf_op jit(solution)/shard_map/ppermute | solution.py:40
  48.1 11.0 %collective-permute-start.18 = (bf16[2,16,1152]{2,1,0:T(8,128)(2,1)S(1)}, bf16[2,16,1152]{2,1,0:T(8,128)(2,1)S(1)}, u32[]{:S(2)}, u32[]{:S(2)}) collective-permute-start(bf16[2,16,1152]{2,1,0:T(8,128)(2,1)S(1)} %activate.4.rest_0_.own_ref), channel_id=1, source_target_pairs={{0,6},{1,7},{2,4},{3,5},{4,2},{5,3},{6,0},{7,1},{8,14},{9,15},{10,... | collective-permute-start | bytes 221192 | tf_op jit(solution)/shard_map/ppermute | solution.py:40
  51.3 9.0 %collective-permute-start.15 = (bf16[2,16,1152]{2,1,0:T(8,128)(2,1)S(1)}, bf16[2,16,1152]{2,1,0:T(8,128)(2,1)S(1)}, u32[]{:S(2)}, u32[]{:S(2)}) collective-permute-start(bf16[2,16,1152]{2,1,0:T(8,128)(2,1)S(1)} %activate.6.own_ref), channel_id=1, source_target_pairs={{0,6},{1,7},{2,4},{3,5},{4,2},{5,3},{6,0},{7,1},{8,14},{9,15},{10,... | collective-permute-start | bytes 221192 | tf_op jit(solution)/shard_map/ppermute | solution.py:40
  59.1 14.6 %collective-permute-start.19 = (bf16[2,32,1152]{2,1,0:T(8,128)(2,1)S(1)}, bf16[2,32,1152]{2,1,0:T(8,128)(2,1)S(1)}, u32[]{:S(2)}, u32[]{:S(2)}) collective-permute-start(bf16[2,32,1152]{2,1,0:T(8,128)(2,1)S(1)} %join.15.own_ref), channel_id=1, source_target_pairs={{0,2},{1,3},{2,0},{3,1},{4,6},{5,7},{6,4},{7,5},{8,10},{9,11},{10,... | collective-permute-start | bytes 442376 | tf_op jit(solution)/shard_map/ppermute | solution.py:40
  60.3 13.6 %collective-permute-start.16 = (bf16[2,32,1152]{2,1,0:T(8,128)(2,1)S(1)}, bf16[2,32,1152]{2,1,0:T(8,128)(2,1)S(1)}, u32[]{:S(2)}, u32[]{:S(2)}) collective-permute-start(bf16[2,32,1152]{2,1,0:T(8,128)(2,1)S(1)} %join.13.own_ref), channel_id=1, source_target_pairs={{0,2},{1,3},{2,0},{3,1},{4,6},{5,7},{6,4},{7,5},{8,10},{9,11},{10,... | collective-permute-start | bytes 442376 | tf_op jit(solution)/shard_map/ppermute | solution.py:40
  61.4 8.3 %collective-permute-start.23 = (bf16[2,16,1152]{2,1,0:T(8,128)(2,1)S(1)}, bf16[2,16,1152]{2,1,0:T(8,128)(2,1)S(1)}, u32[]{:S(2)}, u32[]{:S(2)}) collective-permute-start(bf16[2,16,1152]{2,1,0:T(8,128)(2,1)S(1)} %get-tuple-element.56), channel_id=1, source_target_pairs={{0,6},{1,7},{2,4},{3,5},{4,2},{5,3},{6,0},{7,1},{8,14},{9,15},{10,... | collective-permute-start | bytes 221192 | tf_op jit(solution)/shard_map/ppermute | solution.py:40
  63.0 16.0 %copy-start.1 = (bf16[32,1280]{1,0:T(8,128)(2,1)S(1)}, bf16[32,1280]{1,0:T(8,128)(2,1)}, u32[]{:S(2)}) copy-start(bf16[32,1280]{1,0:T(8,128)(2,1)} %param.5) | copy-start | bytes 245764
  63.0 16.0 %copy-start.2 = (bf16[32,1280]{1,0:T(8,128)(2,1)S(1)}, bf16[32,1280]{1,0:T(8,128)(2,1)}, u32[]{:S(2)}) copy-start(bf16[32,1280]{1,0:T(8,128)(2,1)} %param.4) | copy-start | bytes 245764
  63.1 8.9 %collective-permute-start.11 = (bf16[2,16,1152]{2,1,0:T(8,128)(2,1)S(1)}, bf16[2,16,1152]{2,1,0:T(8,128)(2,1)S(1)}, u32[]{:S(2)}, u32[]{:S(2)}) collective-permute-start(bf16[2,16,1152]{2,1,0:T(8,128)(2,1)S(1)} %get-tuple-element.52), channel_id=1, source_target_pairs={{0,6},{1,7},{2,4},{3,5},{4,2},{5,3},{6,0},{7,1},{8,14},{9,15},{10,... | collective-permute-start | bytes 221192 | tf_op jit(solution)/shard_map/ppermute | solution.py:40
  69.8 6.2 %collective-permute-start.24 = (bf16[2,16,1152]{2,1,0:T(8,128)(2,1)S(1)}, bf16[2,16,1152]{2,1,0:T(8,128)(2,1)S(1)}, u32[]{:S(2)}, u32[]{:S(2)}) collective-permute-start(bf16[2,16,1152]{2,1,0:T(8,128)(2,1)S(1)} %activate.7.own_ref), channel_id=1, source_target_pairs={{0,6},{1,7},{2,4},{3,5},{4,2},{5,3},{6,0},{7,1},{8,14},{9,15},{10,... | collective-permute-start | bytes 221192 | tf_op jit(solution)/shard_map/ppermute | solution.py:40
  72.1 6.9 %collective-permute-start.12 = (bf16[2,16,1152]{2,1,0:T(8,128)(2,1)S(1)}, bf16[2,16,1152]{2,1,0:T(8,128)(2,1)S(1)}, u32[]{:S(2)}, u32[]{:S(2)}) collective-permute-start(bf16[2,16,1152]{2,1,0:T(8,128)(2,1)S(1)} %activate.5.own_ref), channel_id=1, source_target_pairs={{0,6},{1,7},{2,4},{3,5},{4,2},{5,3},{6,0},{7,1},{8,14},{9,15},{10,... | collective-permute-start | bytes 221192 | tf_op jit(solution)/shard_map/ppermute | solution.py:40
  73.8 5.3 %collective-permute-start.20 = (bf16[2,64,1152]{2,1,0:T(8,128)(2,1)S(1)}, bf16[2,64,1152]{2,1,0:T(8,128)(2,1)S(1)}, u32[]{:S(2)}, u32[]{:S(2)}) collective-permute-start(bf16[2,64,1152]{2,1,0:T(8,128)(2,1)S(1)} %join.16.own_ref), channel_id=1, source_target_pairs={{0,1},{1,0},{2,3},{3,2},{4,5},{5,4},{6,7},{7,6},{8,9},{9,8},{10,11... | collective-permute-start | bytes 884744 | tf_op jit(solution)/shard_map/ppermute | solution.py:40
  73.9 8.9 %collective-permute-start.17 = (bf16[2,64,1152]{2,1,0:T(8,128)(2,1)S(1)}, bf16[2,64,1152]{2,1,0:T(8,128)(2,1)S(1)}, u32[]{:S(2)}, u32[]{:S(2)}) collective-permute-start(bf16[2,64,1152]{2,1,0:T(8,128)(2,1)S(1)} %join.14.own_ref), channel_id=1, source_target_pairs={{0,1},{1,0},{2,3},{3,2},{4,5},{5,4},{6,7},{7,6},{8,9},{9,8},{10,11... | collective-permute-start | bytes 884744 | tf_op jit(solution)/shard_map/ppermute | solution.py:40
  76.0 6.7 %collective-permute-start.25 = (bf16[2,32,1152]{2,1,0:T(8,128)(2,1)S(1)}, bf16[2,32,1152]{2,1,0:T(8,128)(2,1)S(1)}, u32[]{:S(2)}, u32[]{:S(2)}) collective-permute-start(bf16[2,32,1152]{2,1,0:T(8,128)(2,1)S(1)} %join.20.own_ref), channel_id=1, source_target_pairs={{0,2},{1,3},{2,0},{3,1},{4,6},{5,7},{6,4},{7,5},{8,10},{9,11},{10,... | collective-permute-start | bytes 442376 | tf_op jit(solution)/shard_map/ppermute | solution.py:40
  79.0 5.4 %collective-permute-start.13 = (bf16[2,32,1152]{2,1,0:T(8,128)(2,1)S(1)}, bf16[2,32,1152]{2,1,0:T(8,128)(2,1)S(1)}, u32[]{:S(2)}, u32[]{:S(2)}) collective-permute-start(bf16[2,32,1152]{2,1,0:T(8,128)(2,1)S(1)} %join.12.own_ref), channel_id=1, source_target_pairs={{0,2},{1,3},{2,0},{3,1},{4,6},{5,7},{6,4},{7,5},{8,10},{9,11},{10,... | collective-permute-start | bytes 442376 | tf_op jit(solution)/shard_map/ppermute | solution.py:40
  82.8 2.0 %collective-permute-start.26 = (bf16[2,64,1152]{2,1,0:T(8,128)(2,1)S(1)}, bf16[2,64,1152]{2,1,0:T(8,128)(2,1)S(1)}, u32[]{:S(2)}, u32[]{:S(2)}) collective-permute-start(bf16[2,64,1152]{2,1,0:T(8,128)(2,1)S(1)} %join.21.own_ref), channel_id=1, source_target_pairs={{0,1},{1,0},{2,3},{3,2},{4,5},{5,4},{6,7},{7,6},{8,9},{9,8},{10,11... | collective-permute-start | bytes 884744 | tf_op jit(solution)/shard_map/ppermute | solution.py:40
  84.3 1.6 %collective-permute-start.21 = (bf16[2,64,1152]{2,1,0:T(8,128)(2,1)S(1)}, bf16[2,64,1152]{2,1,0:T(8,128)(2,1)S(1)}, u32[]{:S(2)}, u32[]{:S(2)}) collective-permute-start(bf16[2,64,1152]{2,1,0:T(8,128)(2,1)S(1)} %join.19.own_ref), channel_id=1, source_target_pairs={{0,1},{1,0},{2,3},{3,2},{4,5},{5,4},{6,7},{7,6},{8,9},{9,8},{10,11... | collective-permute-start | bytes 884744 | tf_op jit(solution)/shard_map/ppermute | solution.py:40
  87.3 13.9 %collective-permute-start.29 = (bf16[32,1280]{1,0:T(8,128)(2,1)S(1)}, bf16[32,1280]{1,0:T(8,128)(2,1)S(1)}, u32[]{:S(2)}, u32[]{:S(2)}) collective-permute-start(bf16[32,1280]{1,0:T(8,128)(2,1)S(1)} %get-tuple-element.60), channel_id=1, source_target_pairs={{0,24},{8,16},{16,8},{24,0},{1,25},{9,17},{17,9},{25,1},{2,26},{10... | collective-permute-start | bytes 245768 | tf_op jit(solution)/shard_map/ppermute | solution.py:40
  89.8 11.3 %collective-permute-start.28 = (bf16[32,1280]{1,0:T(8,128)(2,1)S(1)}, bf16[32,1280]{1,0:T(8,128)(2,1)S(1)}, u32[]{:S(2)}, u32[]{:S(2)}) collective-permute-start(bf16[32,1280]{1,0:T(8,128)(2,1)S(1)} %get-tuple-element.61), channel_id=1, source_target_pairs={{0,16},{8,24},{16,0},{24,8},{1,17},{9,25},{17,1},{25,9},{2,18},{10... | collective-permute-start | bytes 245768 | tf_op jit(solution)/shard_map/ppermute | solution.py:40
  90.3 10.8 %collective-permute-start.27 = (bf16[32,1280]{1,0:T(8,128)(2,1)S(1)}, bf16[32,1280]{1,0:T(8,128)(2,1)S(1)}, u32[]{:S(2)}, u32[]{:S(2)}) collective-permute-start(bf16[32,1280]{1,0:T(8,128)(2,1)S(1)} %get-tuple-element.59), channel_id=1, source_target_pairs={{0,8},{8,0},{16,24},{24,16},{1,9},{9,1},{17,25},{25,17},{2,10},{10... | collective-permute-start | bytes 245768 | tf_op jit(solution)/shard_map/ppermute | solution.py:40

commit v5 on v4

--- a/solution.py
+++ b/solution.py
@@ -10,8 +10,8 @@
 
 BF16 = jnp.bfloat16
 F32 = jnp.float32
-LOAD_BYTES = 38 * 1024 * 1024
-CHUNKS = 4
+LOAD_BYTES = 24 * 1024 * 1024
+CHUNKS = 3
 PIECE = 384
 VMEM_BYTES = 40 * 1024 * 1024
 SMALL_BYTES = 16 * 1024 * 1024
@@ -286,8 +286,8 @@
 
 def weight_grads(xt, gs, finals, factor):
     features, total = xt.shape
-    width = finals[0].shape[2]
-    hidden = width * len(finals)
+    width = finals[0].shape[2] // 2
+    hidden = 2 * width * len(finals)
 
     def kernel(xt_ref, gs_ref, *refs):
         in_ref, out_ref = refs[-2:]
@@ -301,17 +301,23 @@
                 out_ref[low:high, :] = (contract(turned, gs_ref[...], 1, 0) * factor).astype(BF16)
 
         for index in range(len(finals)):
-            pl.when(step == index)(functools.partial(work, refs[index]))
-
-    return pl.pallas_call(
-        kernel,
-        grid=(len(finals),),
+            pl.when((step >= 2 * index) & (step < 2 * index + 2))(functools.partial(work, refs[index]))
+
+    def block(index):
+        def place(i):
+            return 0, 0, jnp.clip(i - 2 * index, 0, 1)
+
+        return pl.BlockSpec((2, total, width), place)
+
+    return pl.pallas_call(
+        kernel,
+        grid=(2 * len(finals),),
         out_shape=(
             jax.ShapeDtypeStruct((features, hidden), BF16),
             jax.ShapeDtypeStruct((hidden, features), BF16),
         ),
         in_specs=[whole(features, total), whole(total, features)]
-        + [whole(2, total, width)] * len(finals),
+        + [block(index) for index in range(len(finals))],
         out_specs=(
             pl.BlockSpec((features, width), lambda i: (0, i)),
             pl.BlockSpec((width, features), lambda i: (i, 0)),

time: 102 us -> 95.4 us (0.935)
  waiting for transfers between devices: 25.3 us -> 30.2 us
  local copies, waits for them, and re-layouts: 4.41 us -> 0.05 us
  Pallas kernels: 36.1 us -> 31.9 us
  starting transfers between devices: 32.9 us -> 30.1 us
    ppermute x30 -> x24, waiting for transfers between devices: 25.3 us -> 30.2 us  [exchange(): return lax.ppermute(array, axis, [(i, i ^ step) for i in range(size)])]
    pallas_call x1, Pallas kernels: 12.2 us -> 7.72 us  [load(): pl.pallas_call(kernel, out_shape=tuple((jax.ShapeDtypeStruct(w.shape, w.d...]
    unnamed x12 -> x4, local copies, waits for them, and re-layouts: 4.37 us -> 0.01 us
    ppermute x30 -> x24, starting transfers between devices: 32.9 us -> 30.1 us  [exchange(): return lax.ppermute(array, axis, [(i, i ^ step) for i in range(size)])]
    pallas_call x4 -> x3, Pallas kernels: 8.4 us -> 8.58 us  [forward(): pl.pallas_call(kernel, grid=(1,), out_shape=(jax.ShapeDtypeStruct((2, hal...]
    pallas_call x4 -> x3, Pallas kernels: 3.88 us -> 3.84 us  [input_grads(): pl.pallas_call(kernel, grid=(1,), out_shape=jax.ShapeDtypeStruct((total,...]
  transfers between devices with their start and end apart: 30 -> 24, of which waited for: 11 -> 10; matrix products, arithmetic and copies ran while one was open for 0% -> 0% of each run, Pallas kernels for 32% -> 29%
where the time goes in v5:
time: 95.4 us; the launch traced here: 95.2 us
  Pallas kernels  31.9 us (33%)
  waiting for transfers between devices  30.2 us (32%)
  starting transfers between devices  30.1 us (32%)
  other arithmetic  1.74 us (2%)
  between operations  1.01 us (1%)
    ppermute x24, waiting for transfers between devices, exchange(): return lax.ppermute(array, axis, [(i, i ^ step) for i in range(size)])  30.2 us
    ppermute x24, starting transfers between devices, exchange(): return lax.ppermute(array, axis, [(i, i ^ step) for i in range(size)])  30.1 us
    pallas_call x1, Pallas kernels, weight_grads(): pl.pallas_call(kernel, grid=(2 * len(finals),), out_shape=(jax.ShapeDtype...  10.6 us
    pallas_call x3, Pallas kernels, forward(): pl.pallas_call(kernel, grid=(1,), out_shape=(jax.ShapeDtypeStruct((2, hal...  8.58 us
    pallas_call x1, Pallas kernels, load(): pl.pallas_call(kernel, out_shape=tuple((jax.ShapeDtypeStruct(w.shape, w.d...  7.72 us
    pallas_call x3, Pallas kernels, input_grads(): pl.pallas_call(kernel, grid=(1,), out_shape=jax.ShapeDtypeStruct((total,...  3.84 us
  transfers between devices with their start and end apart: 24, of which 10 were waited for; matrix products, arithmetic and copies ran while one was open for 0% of the time, Pallas kernels for 29%

profile of v5, /device:TPU:0, one launch (start us, length us, event | category | flops | bytes accessed | tf_op | source)
XLA Modules:
  0.0 95.2 jit_solution(673359630316434257)
XLA Ops:
  0.6 0.9 pad_maximum_fusion.1.refs_0_
  1.6 3.0 %collective-permute-start = (bf16[2,32,1280]{2,1,0:T(8,128)(2,1)S(1)}, bf16[2,32,1280]{2,1,0:T(8,128)(2,1)S(1)}, u32[]{:S(2)}, u32[]{:S(2)}) collective-permute-start(bf16[2,32,1280]{2,1,0:T(8,128)(2,1)S(1)} %pad_maximum_fusion.1.refs_0_), channel_id=1, source_target_pairs={{0,8},{8,0},{16,24},{24,16},{1,9},{9,1},{17,25},{25,17},{2,10},{10... | collective-permute-start | bytes 491528 | tf_op jit(solution)/shard_map/ppermute | solution.py:40
  4.6 1.5 %collective-permute-start.1 = (bf16[2,32,1280]{2,1,0:T(8,128)(2,1)S(1)}, bf16[2,32,1280]{2,1,0:T(8,128)(2,1)S(1)}, u32[]{:S(2)}, u32[]{:S(2)}) collective-permute-start(bf16[2,32,1280]{2,1,0:T(8,128)(2,1)S(1)} %pad_maximum_fusion.1.refs_0_), channel_id=1, source_target_pairs={{0,16},{8,24},{16,0},{24,8},{1,17},{9,25},{17,1},{25,9},{2,18},{10... | collective-permute-start | bytes 491528 | tf_op jit(solution)/shard_map/ppermute | solution.py:40
  6.1 7.7 %load.1 = (bf16[1280,4608]{1,0:T(8,128)(2,1)S(1)}, bf16[4608,1280]{1,0:T(8,128)(2,1)S(1)}) custom-call(bf16[1280,4608]{1,0:T(8,128)(2,1)} %refs_0_.1, bf16[4608,1280]{1,0:T(8,128)(2,1)} %refs_1_.1), custom_call_target="tpu_custom_call" | custom-call | bytes 47185920 | tf_op jit(solution)/shard_map/load/pallas_call | solution.py:84
  13.9 2.9 %forward.3 = (f32[2,64,1536]{2,1,0:T(8,128)S(1)}, bf16[2,64,1536]{2,1,0:T(8,128)(2,1)S(1)}) custom-call(s32[1]{0:T(128)} %bitcast.rank_ref, bf16[2,32,1280]{2,1,0:T(8,128)(2,1)S(1)} %pad_maximum_fusion.1.refs_0_, bf16[2,32,1280]{2,1,0:T(8,128)(2,1)S(1)} %collective-permute-done.refs_1_, bf16[2,32,1280]{2,1,0:T(8,128)(2,1)S(1)} %collective-permute-done.1.refs_2_, ...), custom_call_target="tpu_custom_call" | custom-call | flops 1006632960 | bytes 7864320 | tf_op jit(solution)/shard_map/forward/pallas_call | solution.py:129
  16.8 0.1 collective-permute-start.3
  16.8 2.9 %forward.4 = (f32[2,64,1536]{2,1,0:T(8,128)S(1)}, bf16[2,64,1536]{2,1,0:T(8,128)(2,1)S(1)}) custom-call(s32[1]{0:T(128)} %bitcast.rank_ref, bf16[2,32,1280]{2,1,0:T(8,128)(2,1)S(1)} %pad_maximum_fusion.1.refs_0_, bf16[2,32,1280]{2,1,0:T(8,128)(2,1)S(1)} %collective-permute-done.refs_1_, bf16[2,32,1280]{2,1,0:T(8,128)(2,1)S(1)} %collective-permute-done.1.refs_2_, ...), custom_call_target="tpu_custom_call" | custom-call | flops 1006632960 | bytes 7864320 | tf_op jit(solution)/shard_map/forward/pallas_call | solution.py:129
  19.7 0.1 halve.6
  19.8 0.6 collective-permute-start.5
  20.5 2.0 %collective-permute-start.4 = (bf16[2,32,1536]{2,1,0:T(8,128)(2,1)S(1)}, bf16[2,32,1536]{2,1,0:T(8,128)(2,1)S(1)}, u32[]{:S(2)}, u32[]{:S(2)}) collective-permute-start(bf16[2,32,1536]{2,1,0:T(8,128)(2,1)S(1)} %get-tuple-element.30.rest_0_), channel_id=1, source_target_pairs={{0,2},{1,3},{2,0},{3,1},{4,6},{5,7},{6,4},{7,5},{8,10},{9,11},{10,... | collective-permute-start | bytes 589832 | tf_op jit(solution)/shard_map/ppermute | solution.py:40
  22.5 2.9 %forward.5 = (f32[2,64,1536]{2,1,0:T(8,128)S(1)}, bf16[2,64,1536]{2,1,0:T(8,128)(2,1)S(1)}) custom-call(s32[1]{0:T(128)} %bitcast.rank_ref, bf16[2,32,1280]{2,1,0:T(8,128)(2,1)S(1)} %pad_maximum_fusion.1.refs_0_, bf16[2,32,1280]{2,1,0:T(8,128)(2,1)S(1)} %collective-permute-done.refs_1_, bf16[2,32,1280]{2,1,0:T(8,128)(2,1)S(1)} %collective-permute-done.1.refs_2_, ...), custom_call_target="tpu_custom_call" | custom-call | flops 1006632960 | bytes 7864320 | tf_op jit(solution)/shard_map/forward/pallas_call | solution.py:129
  25.4 0.1 halve.7
  25.5 2.2 %collective-permute-done.4.received_ref = bf16[2,32,1536]{2,1,0:T(8,128)(2,1)S(1)} collective-permute-done((bf16[2,32,1536]{2,1,0:T(8,128)(2,1)S(1)}, bf16[2,32,1536]{2,1,0:T(8,128)(2,1)S(1)}, u32[]{:S(2)}, u32[]{:S(2)}) %collective-permute-start.4) | collective-permute-done | bytes 196640 | tf_op jit(solution)/shard_map/ppermute | solution.py:40
  27.7 0.1 collective-permute-start.6
  27.8 3.8 %collective-permute-start.11 = (bf16[2,16,1536]{2,1,0:T(8,128)(2,1)S(1)}, bf16[2,16,1536]{2,1,0:T(8,128)(2,1)S(1)}, u32[]{:S(2)}, u32[]{:S(2)}) collective-permute-start(bf16[2,16,1536]{2,1,0:T(8,128)(2,1)S(1)} %get-tuple-element.36.rest_0_), channel_id=1, source_target_pairs={{0,6},{1,7},{2,4},{3,5},{4,2},{5,3},{6,0},{7,1},{8,14},{9,15},{10,... | collective-permute-start | bytes 294920 | tf_op jit(solution)/shard_map/ppermute | solution.py:40
  31.6 3.5 %collective-permute-done.11.received_ref = bf16[2,16,1536]{2,1,0:T(8,128)(2,1)S(1)} collective-permute-done((bf16[2,16,1536]{2,1,0:T(8,128)(2,1)S(1)}, bf16[2,16,1536]{2,1,0:T(8,128)(2,1)S(1)}, u32[]{:S(2)}, u32[]{:S(2)}) %collective-permute-start.11) | collective-permute-done | bytes 98336 | tf_op jit(solution)/shard_map/ppermute | solution.py:40
  35.1 0.1 activate.4.own_ref
  35.2 3.6 %collective-permute-start.12 = (bf16[2,16,1536]{2,1,0:T(8,128)(2,1)S(1)}, bf16[2,16,1536]{2,1,0:T(8,128)(2,1)S(1)}, u32[]{:S(2)}, u32[]{:S(2)}) collective-permute-start(bf16[2,16,1536]{2,1,0:T(8,128)(2,1)S(1)} %activate.4.own_ref), channel_id=1, source_target_pairs={{0,6},{1,7},{2,4},{3,5},{4,2},{5,3},{6,0},{7,1},{8,14},{9,15},{10,... | collective-permute-start | bytes 294920 | tf_op jit(solution)/shard_map/ppermute | solution.py:40
  38.9 2.1 %collective-permute-start.7 = (bf16[2,32,1536]{2,1,0:T(8,128)(2,1)S(1)}, bf16[2,32,1536]{2,1,0:T(8,128)(2,1)S(1)}, u32[]{:S(2)}, u32[]{:S(2)}) collective-permute-start(bf16[2,32,1536]{2,1,0:T(8,128)(2,1)S(1)} %get-tuple-element.38), channel_id=1, source_target_pairs={{0,2},{1,3},{2,0},{3,1},{4,6},{5,7},{6,4},{7,5},{8,10},{9,11},{10,... | collective-permute-start | bytes 589832 | tf_op jit(solution)/shard_map/ppermute | solution.py:40
  41.0 1.8 %collective-permute-done.12.received_ref = bf16[2,16,1536]{2,1,0:T(8,128)(2,1)S(1)} collective-permute-done((bf16[2,16,1536]{2,1,0:T(8,128)(2,1)S(1)}, bf16[2,16,1536]{2,1,0:T(8,128)(2,1)S(1)}, u32[]{:S(2)}, u32[]{:S(2)}) %collective-permute-start.12) | collective-permute-done | bytes 98336 | tf_op jit(solution)/shard_map/ppermute | solution.py:40
  42.8 0.8 collective-permute-start.13
  43.6 3.3 %collective-permute-done.16.received_ref = bf16[2,32,1536]{2,1,0:T(8,128)(2,1)S(1)} collective-permute-done((bf16[2,32,1536]{2,1,0:T(8,128)(2,1)S(1)}, bf16[2,32,1536]{2,1,0:T(8,128)(2,1)S(1)}, u32[]{:S(2)}, u32[]{:S(2)}) %collective-permute-start.16) | collective-permute-done | bytes 196640 | tf_op jit(solution)/shard_map/ppermute | solution.py:40
  46.9 2.2 %collective-permute-start.17 = (bf16[2,16,1536]{2,1,0:T(8,128)(2,1)S(1)}, bf16[2,16,1536]{2,1,0:T(8,128)(2,1)S(1)}, u32[]{:S(2)}, u32[]{:S(2)}) collective-permute-start(bf16[2,16,1536]{2,1,0:T(8,128)(2,1)S(1)} %get-tuple-element.44), channel_id=1, source_target_pairs={{0,6},{1,7},{2,4},{3,5},{4,2},{5,3},{6,0},{7,1},{8,14},{9,15},{10,... | collective-permute-start | bytes 294920 | tf_op jit(solution)/shard_map/ppermute | solution.py:40
  49.1 1.9 %collective-permute-done.7.received_ref = bf16[2,32,1536]{2,1,0:T(8,128)(2,1)S(1)} collective-permute-done((bf16[2,32,1536]{2,1,0:T(8,128)(2,1)S(1)}, bf16[2,32,1536]{2,1,0:T(8,128)(2,1)S(1)}, u32[]{:S(2)}, u32[]{:S(2)}) %collective-permute-start.7) | collective-permute-done | bytes 196640 | tf_op jit(solution)/shard_map/ppermute | solution.py:40
  51.1 2.2 %collective-permute-start.8 = (bf16[2,16,1536]{2,1,0:T(8,128)(2,1)S(1)}, bf16[2,16,1536]{2,1,0:T(8,128)(2,1)S(1)}, u32[]{:S(2)}, u32[]{:S(2)}) collective-permute-start(bf16[2,16,1536]{2,1,0:T(8,128)(2,1)S(1)} %get-tuple-element.40), channel_id=1, source_target_pairs={{0,6},{1,7},{2,4},{3,5},{4,2},{5,3},{6,0},{7,1},{8,14},{9,15},{10,... | collective-permute-start | bytes 294920 | tf_op jit(solution)/shard_map/ppermute | solution.py:40
  53.4 5.2 %collective-permute-done.13.received_ref = bf16[2,32,1536]{2,1,0:T(8,128)(2,1)S(1)} collective-permute-done((bf16[2,32,1536]{2,1,0:T(8,128)(2,1)S(1)}, bf16[2,32,1536]{2,1,0:T(8,128)(2,1)S(1)}, u32[]{:S(2)}, u32[]{:S(2)}) %collective-permute-start.13) | collective-permute-done | bytes 196640 | tf_op jit(solution)/shard_map/ppermute | solution.py:40
  58.6 0.1 collective-permute-start.14
  58.8 2.2 %collective-permute-start.18 = (bf16[2,16,1536]{2,1,0:T(8,128)(2,1)S(1)}, bf16[2,16,1536]{2,1,0:T(8,128)(2,1)S(1)}, u32[]{:S(2)}, u32[]{:S(2)}) collective-permute-start(bf16[2,16,1536]{2,1,0:T(8,128)(2,1)S(1)} %activate.5.own_ref), channel_id=1, source_target_pairs={{0,6},{1,7},{2,4},{3,5},{4,2},{5,3},{6,0},{7,1},{8,14},{9,15},{10,... | collective-permute-start | bytes 294920 | tf_op jit(solution)/shard_map/ppermute | solution.py:40
  61.0 0.1 activate.3.own_ref
  61.0 1.8 %collective-permute-start.9 = (bf16[2,16,1536]{2,1,0:T(8,128)(2,1)S(1)}, bf16[2,16,1536]{2,1,0:T(8,128)(2,1)S(1)}, u32[]{:S(2)}, u32[]{:S(2)}) collective-permute-start(bf16[2,16,1536]{2,1,0:T(8,128)(2,1)S(1)} %activate.3.own_ref), channel_id=1, source_target_pairs={{0,6},{1,7},{2,4},{3,5},{4,2},{5,3},{6,0},{7,1},{8,14},{9,15},{10,... | collective-permute-start | bytes 294920 | tf_op jit(solution)/shard_map/ppermute | solution.py:40
  62.8 3.5 %collective-permute-done.18.received_ref = bf16[2,16,1536]{2,1,0:T(8,128)(2,1)S(1)} collective-permute-done((bf16[2,16,1536]{2,1,0:T(8,128)(2,1)S(1)}, bf16[2,16,1536]{2,1,0:T(8,128)(2,1)S(1)}, u32[]{:S(2)}, u32[]{:S(2)}) %collective-permute-start.18) | collective-permute-done | bytes 98336 | tf_op jit(solution)/shard_map/ppermute | solution.py:40
  66.4 0.1 collective-permute-start.19
  66.5 2.2 %collective-permute-done.9.received_ref = bf16[2,16,1536]{2,1,0:T(8,128)(2,1)S(1)} collective-permute-done((bf16[2,16,1536]{2,1,0:T(8,128)(2,1)S(1)}, bf16[2,16,1536]{2,1,0:T(8,128)(2,1)S(1)}, u32[]{:S(2)}, u32[]{:S(2)}) %collective-permute-start.9) | collective-permute-done | bytes 98336 | tf_op jit(solution)/shard_map/ppermute | solution.py:40
  68.7 0.2 collective-permute-start.10
  68.9 5.4 %collective-permute-done.19.received_ref = bf16[2,32,1536]{2,1,0:T(8,128)(2,1)S(1)} collective-permute-done((bf16[2,32,1536]{2,1,0:T(8,128)(2,1)S(1)}, bf16[2,32,1536]{2,1,0:T(8,128)(2,1)S(1)}, u32[]{:S(2)}, u32[]{:S(2)}) %collective-permute-start.19) | collective-permute-done | bytes 196640 | tf_op jit(solution)/shard_map/ppermute | solution.py:40
  74.3 0.1 collective-permute-start.20
  74.5 1.3 %input_grads.3.rest_0_.refs_0_ = f32[128,1280]{1,0:T(8,128)S(1)} custom-call(bf16[2,128,1536]{2,1,0:T(8,128)(2,1)S(1)} %join.12.grad_ref.refs_0_, bf16[1280,4608]{1,0:T(8,128)(2,1)S(1)} %get-tuple-element.25.refs_4_.wi_ref), custom_call_target="tpu_custom_call" | custom-call | flops 503316480 | bytes 3932160 | tf_op jit(solution)/shard_map/input_grads/pallas_call | solution.py:275
  75.8 1.1 %collective-permute-done.10.received_ref = bf16[2,32,1536]{2,1,0:T(8,128)(2,1)S(1)} collective-permute-done((bf16[2,32,1536]{2,1,0:T(8,128)(2,1)S(1)}, bf16[2,32,1536]{2,1,0:T(8,128)(2,1)S(1)}, u32[]{:S(2)}, u32[]{:S(2)}) %collective-permute-start.10) | collective-permute-done | bytes 196640 | tf_op jit(solution)/shard_map/ppermute | solution.py:40
  76.9 0.1 collective-permute-start.15
  77.0 0.3 convolution_convert_fusion.xt_ref
  77.4 1.3 %input_grads.4.rest_0_.refs_0_ = f32[128,1280]{1,0:T(8,128)S(1)} custom-call(bf16[2,128,1536]{2,1,0:T(8,128)(2,1)S(1)} %join.16.grad_ref.refs_1_, bf16[1280,4608]{1,0:T(8,128)(2,1)S(1)} %get-tuple-element.25.refs_4_.wi_ref, f32[128,1280]{1,0:T(8,128)S(1)} %input_grads.3.rest_0_.refs_0_), custom_call_target="tpu_custom_call" | custom-call | flops 503316480 | bytes 3932160 | tf_op jit(solution)/shard_map/input_grads/pallas_call | solution.py:275
  78.7 0.2 join.17.grad_ref.refs_2_
  79.0 1.3 %input_grads.5 = f32[128,1280]{1,0:T(8,128)S(1)} custom-call(bf16[2,128,1536]{2,1,0:T(8,128)(2,1)S(1)} %join.17.grad_ref.refs_2_, bf16[1280,4608]{1,0:T(8,128)(2,1)S(1)} %get-tuple-element.25.refs_4_.wi_ref, f32[128,1280]{1,0:T(8,128)S(1)} %input_grads.4.rest_0_.refs_0_), custom_call_target="tpu_custom_call" | custom-call | flops 503316480 | bytes 3932160 | tf_op jit(solution)/shard_map/input_grads/pallas_call | solution.py:275
  80.3 2.5 %collective-permute-start.23 = (bf16[32,1280]{1,0:T(8,128)(2,1)S(1)}, bf16[32,1280]{1,0:T(8,128)(2,1)S(1)}, u32[]{:S(2)}, u32[]{:S(2)}) collective-permute-start(bf16[32,1280]{1,0:T(8,128)(2,1)S(1)} %get-tuple-element.48), channel_id=1, source_target_pairs={{0,24},{8,16},{16,8},{24,0},{1,25},{9,17},{17,9},{25,1},{2,26},{10... | collective-permute-start | bytes 245768 | tf_op jit(solution)/shard_map/ppermute | solution.py:40
  82.8 0.5 collective-permute-start.22
  83.3 0.5 collective-permute-start.21
  83.9 10.6 %weight_grads.1 = (bf16[1280,4608]{1,0:T(8,128)(2,1)}, bf16[4608,1280]{1,0:T(8,128)(2,1)}) custom-call(bf16[1280,128]{1,0:T(8,128)(2,1)S(1)} %convolution_convert_fusion.xt_ref, bf16[128,1280]{1,0:T(8,128)(2,1)S(1)} %slice_bitcast_fusion.gs_ref, bf16[2,128,1536]{2,1,0:T(8,128)(2,1)S(1)} %join.12.grad_ref.refs_0_, ...), custom_call_target="tpu_custom_call" | custom-call | flops 3019898880 | bytes 23592960 | tf_op jit(solution)/shard_map/weight_grads/pallas_call | solution.py:312
  94.5 0.7 fusion.1
  (39 shorter events, 0.8 us)
Async XLA Ops:
  1.6 12.3 %collective-permute-start = (bf16[2,32,1280]{2,1,0:T(8,128)(2,1)S(1)}, bf16[2,32,1280]{2,1,0:T(8,128)(2,1)S(1)}, u32[]{:S(2)}, u32[]{:S(2)}) collective-permute-start(bf16[2,32,1280]{2,1,0:T(8,128)(2,1)S(1)} %pad_maximum_fusion.1.refs_0_), channel_id=1, source_target_pairs={{0,8},{8,0},{16,24},{24,16},{1,9},{9,1},{17,25},{25,17},{2,10},{10... | collective-permute-start | bytes 491528 | tf_op jit(solution)/shard_map/ppermute | solution.py:40
  4.6 9.3 %collective-permute-start.1 = (bf16[2,32,1280]{2,1,0:T(8,128)(2,1)S(1)}, bf16[2,32,1280]{2,1,0:T(8,128)(2,1)S(1)}, u32[]{:S(2)}, u32[]{:S(2)}) collective-permute-start(bf16[2,32,1280]{2,1,0:T(8,128)(2,1)S(1)} %pad_maximum_fusion.1.refs_0_), channel_id=1, source_target_pairs={{0,16},{8,24},{16,0},{24,8},{1,17},{9,25},{17,1},{25,9},{2,18},{10... | collective-permute-start | bytes 491528 | tf_op jit(solution)/shard_map/ppermute | solution.py:40
  6.1 7.8 %collective-permute-start.2 = (bf16[2,32,1280]{2,1,0:T(8,128)(2,1)S(1)}, bf16[2,32,1280]{2,1,0:T(8,128)(2,1)S(1)}, u32[]{:S(2)}, u32[]{:S(2)}) collective-permute-start(bf16[2,32,1280]{2,1,0:T(8,128)(2,1)S(1)} %pad_maximum_fusion.1.refs_0_), channel_id=1, source_target_pairs={{0,24},{8,16},{16,8},{24,0},{1,25},{9,17},{17,9},{25,1},{2,26},{10... | collective-permute-start | bytes 491528 | tf_op jit(solution)/shard_map/ppermute | solution.py:40
  16.8 3.0 %collective-permute-start.3 = (bf16[2,64,1536]{2,1,0:T(8,128)(2,1)S(1)}, bf16[2,64,1536]{2,1,0:T(8,128)(2,1)S(1)}, u32[]{:S(2)}, u32[]{:S(2)}) collective-permute-start(bf16[2,64,1536]{2,1,0:T(8,128)(2,1)S(1)} %get-tuple-element.27.refs_6_), channel_id=1, source_target_pairs={{0,1},{1,0},{2,3},{3,2},{4,5},{5,4},{6,7},{7,6},{8,9},{9,8},{10,11... | collective-permute-start | bytes 1179656 | tf_op jit(solution)/shard_map/ppermute | solution.py:40
  19.8 5.5 %collective-permute-start.5 = (bf16[2,64,1536]{2,1,0:T(8,128)(2,1)S(1)}, bf16[2,64,1536]{2,1,0:T(8,128)(2,1)S(1)}, u32[]{:S(2)}, u32[]{:S(2)}) collective-permute-start(bf16[2,64,1536]{2,1,0:T(8,128)(2,1)S(1)} %relay.2.refs_6_), channel_id=1, source_target_pairs={{0,1},{1,0},{2,3},{3,2},{4,5},{5,4},{6,7},{7,6},{8,9},{9,8},{10,11... | collective-permute-start | bytes 1179656 | tf_op jit(solution)/shard_map/ppermute | solution.py:40
  20.5 7.2 %collective-permute-start.4 = (bf16[2,32,1536]{2,1,0:T(8,128)(2,1)S(1)}, bf16[2,32,1536]{2,1,0:T(8,128)(2,1)S(1)}, u32[]{:S(2)}, u32[]{:S(2)}) collective-permute-start(bf16[2,32,1536]{2,1,0:T(8,128)(2,1)S(1)} %get-tuple-element.30.rest_0_), channel_id=1, source_target_pairs={{0,2},{1,3},{2,0},{3,1},{4,6},{5,7},{6,4},{7,5},{8,10},{9,11},{10,... | collective-permute-start | bytes 589832 | tf_op jit(solution)/shard_map/ppermute | solution.py:40
  27.7 11.1 %collective-permute-start.6 = (bf16[2,64,1536]{2,1,0:T(8,128)(2,1)S(1)}, bf16[2,64,1536]{2,1,0:T(8,128)(2,1)S(1)}, u32[]{:S(2)}, u32[]{:S(2)}) collective-permute-start(bf16[2,64,1536]{2,1,0:T(8,128)(2,1)S(1)} %relay.3), channel_id=1, source_target_pairs={{0,1},{1,0},{2,3},{3,2},{4,5},{5,4},{6,7},{7,6},{8,9},{9,8},{10,11... | collective-permute-start | bytes 1179656 | tf_op jit(solution)/shard_map/ppermute | solution.py:40
  27.8 7.3 %collective-permute-start.11 = (bf16[2,16,1536]{2,1,0:T(8,128)(2,1)S(1)}, bf16[2,16,1536]{2,1,0:T(8,128)(2,1)S(1)}, u32[]{:S(2)}, u32[]{:S(2)}) collective-permute-start(bf16[2,16,1536]{2,1,0:T(8,128)(2,1)S(1)} %get-tuple-element.36.rest_0_), channel_id=1, source_target_pairs={{0,6},{1,7},{2,4},{3,5},{4,2},{5,3},{6,0},{7,1},{8,14},{9,15},{10,... | collective-permute-start | bytes 294920 | tf_op jit(solution)/shard_map/ppermute | solution.py:40
  35.2 7.6 %collective-permute-start.12 = (bf16[2,16,1536]{2,1,0:T(8,128)(2,1)S(1)}, bf16[2,16,1536]{2,1,0:T(8,128)(2,1)S(1)}, u32[]{:S(2)}, u32[]{:S(2)}) collective-permute-start(bf16[2,16,1536]{2,1,0:T(8,128)(2,1)S(1)} %activate.4.own_ref), channel_id=1, source_target_pairs={{0,6},{1,7},{2,4},{3,5},{4,2},{5,3},{6,0},{7,1},{8,14},{9,15},{10,... | collective-permute-start | bytes 294920 | tf_op jit(solution)/shard_map/ppermute | solution.py:40
  38.8 8.0 %collective-permute-start.16 = (bf16[2,32,1536]{2,1,0:T(8,128)(2,1)S(1)}, bf16[2,32,1536]{2,1,0:T(8,128)(2,1)S(1)}, u32[]{:S(2)}, u32[]{:S(2)}) collective-permute-start(bf16[2,32,1536]{2,1,0:T(8,128)(2,1)S(1)} %get-tuple-element.35.rest_0_), channel_id=1, source_target_pairs={{0,2},{1,3},{2,0},{3,1},{4,6},{5,7},{6,4},{7,5},{8,10},{9,11},{10,... | collective-permute-start | bytes 589832 | tf_op jit(solution)/shard_map/ppermute | solution.py:40
  38.9 12.2 %collective-permute-start.7 = (bf16[2,32,1536]{2,1,0:T(8,128)(2,1)S(1)}, bf16[2,32,1536]{2,1,0:T(8,128)(2,1)S(1)}, u32[]{:S(2)}, u32[]{:S(2)}) collective-permute-start(bf16[2,32,1536]{2,1,0:T(8,128)(2,1)S(1)} %get-tuple-element.38), channel_id=1, source_target_pairs={{0,2},{1,3},{2,0},{3,1},{4,6},{5,7},{6,4},{7,5},{8,10},{9,11},{10,... | collective-permute-start | bytes 589832 | tf_op jit(solution)/shard_map/ppermute | solution.py:40
  42.8 15.8 %collective-permute-start.13 = (bf16[2,32,1536]{2,1,0:T(8,128)(2,1)S(1)}, bf16[2,32,1536]{2,1,0:T(8,128)(2,1)S(1)}, u32[]{:S(2)}, u32[]{:S(2)}) collective-permute-start(bf16[2,32,1536]{2,1,0:T(8,128)(2,1)S(1)} %join.10.own_ref), channel_id=1, source_target_pairs={{0,2},{1,3},{2,0},{3,1},{4,6},{5,7},{6,4},{7,5},{8,10},{9,11},{10,... | collective-permute-start | bytes 589832 | tf_op jit(solution)/shard_map/ppermute | solution.py:40
  46.9 11.8 %collective-permute-start.17 = (bf16[2,16,1536]{2,1,0:T(8,128)(2,1)S(1)}, bf16[2,16,1536]{2,1,0:T(8,128)(2,1)S(1)}, u32[]{:S(2)}, u32[]{:S(2)}) collective-permute-start(bf16[2,16,1536]{2,1,0:T(8,128)(2,1)S(1)} %get-tuple-element.44), channel_id=1, source_target_pairs={{0,6},{1,7},{2,4},{3,5},{4,2},{5,3},{6,0},{7,1},{8,14},{9,15},{10,... | collective-permute-start | bytes 294920 | tf_op jit(solution)/shard_map/ppermute | solution.py:40
  51.1 17.7 %copy-start = (bf16[32,1280]{1,0:T(8,128)(2,1)S(1)}, bf16[32,1280]{1,0:T(8,128)(2,1)}, u32[]{:S(2)}) copy-start(bf16[32,1280]{1,0:T(8,128)(2,1)} %param.5) | copy-start | bytes 245764
  51.1 17.7 %copy-start.1 = (bf16[32,1280]{1,0:T(8,128)(2,1)S(1)}, bf16[32,1280]{1,0:T(8,128)(2,1)}, u32[]{:S(2)}) copy-start(bf16[32,1280]{1,0:T(8,128)(2,1)} %param.4) | copy-start | bytes 245764
  51.1 9.8 %collective-permute-start.8 = (bf16[2,16,1536]{2,1,0:T(8,128)(2,1)S(1)}, bf16[2,16,1536]{2,1,0:T(8,128)(2,1)S(1)}, u32[]{:S(2)}, u32[]{:S(2)}) collective-permute-start(bf16[2,16,1536]{2,1,0:T(8,128)(2,1)S(1)} %get-tuple-element.40), channel_id=1, source_target_pairs={{0,6},{1,7},{2,4},{3,5},{4,2},{5,3},{6,0},{7,1},{8,14},{9,15},{10,... | collective-permute-start | bytes 294920 | tf_op jit(solution)/shard_map/ppermute | solution.py:40
  58.6 15.8 %collective-permute-start.14 = (bf16[2,64,1536]{2,1,0:T(8,128)(2,1)S(1)}, bf16[2,64,1536]{2,1,0:T(8,128)(2,1)S(1)}, u32[]{:S(2)}, u32[]{:S(2)}) collective-permute-start(bf16[2,64,1536]{2,1,0:T(8,128)(2,1)S(1)} %join.11.own_ref), channel_id=1, source_target_pairs={{0,1},{1,0},{2,3},{3,2},{4,5},{5,4},{6,7},{7,6},{8,9},{9,8},{10,11... | collective-permute-start | bytes 1179656 | tf_op jit(solution)/shard_map/ppermute | solution.py:40
  58.8 7.6 %collective-permute-start.18 = (bf16[2,16,1536]{2,1,0:T(8,128)(2,1)S(1)}, bf16[2,16,1536]{2,1,0:T(8,128)(2,1)S(1)}, u32[]{:S(2)}, u32[]{:S(2)}) collective-permute-start(bf16[2,16,1536]{2,1,0:T(8,128)(2,1)S(1)} %activate.5.own_ref), channel_id=1, source_target_pairs={{0,6},{1,7},{2,4},{3,5},{4,2},{5,3},{6,0},{7,1},{8,14},{9,15},{10,... | collective-permute-start | bytes 294920 | tf_op jit(solution)/shard_map/ppermute | solution.py:40
  61.0 7.6 %collective-permute-start.9 = (bf16[2,16,1536]{2,1,0:T(8,128)(2,1)S(1)}, bf16[2,16,1536]{2,1,0:T(8,128)(2,1)S(1)}, u32[]{:S(2)}, u32[]{:S(2)}) collective-permute-start(bf16[2,16,1536]{2,1,0:T(8,128)(2,1)S(1)} %activate.3.own_ref), channel_id=1, source_target_pairs={{0,6},{1,7},{2,4},{3,5},{4,2},{5,3},{6,0},{7,1},{8,14},{9,15},{10,... | collective-permute-start | bytes 294920 | tf_op jit(solution)/shard_map/ppermute | solution.py:40
  66.4 7.9 %collective-permute-start.19 = (bf16[2,32,1536]{2,1,0:T(8,128)(2,1)S(1)}, bf16[2,32,1536]{2,1,0:T(8,128)(2,1)S(1)}, u32[]{:S(2)}, u32[]{:S(2)}) collective-permute-start(bf16[2,32,1536]{2,1,0:T(8,128)(2,1)S(1)} %join.14.own_ref), channel_id=1, source_target_pairs={{0,2},{1,3},{2,0},{3,1},{4,6},{5,7},{6,4},{7,5},{8,10},{9,11},{10,... | collective-permute-start | bytes 589832 | tf_op jit(solution)/shard_map/ppermute | solution.py:40
  68.7 8.2 %collective-permute-start.10 = (bf16[2,32,1536]{2,1,0:T(8,128)(2,1)S(1)}, bf16[2,32,1536]{2,1,0:T(8,128)(2,1)S(1)}, u32[]{:S(2)}, u32[]{:S(2)}) collective-permute-start(bf16[2,32,1536]{2,1,0:T(8,128)(2,1)S(1)} %join.9.own_ref), channel_id=1, source_target_pairs={{0,2},{1,3},{2,0},{3,1},{4,6},{5,7},{6,4},{7,5},{8,10},{9,11},{10,... | collective-permute-start | bytes 589832 | tf_op jit(solution)/shard_map/ppermute | solution.py:40
  74.3 3.0 %collective-permute-start.20 = (bf16[2,64,1536]{2,1,0:T(8,128)(2,1)S(1)}, bf16[2,64,1536]{2,1,0:T(8,128)(2,1)S(1)}, u32[]{:S(2)}, u32[]{:S(2)}) collective-permute-start(bf16[2,64,1536]{2,1,0:T(8,128)(2,1)S(1)} %join.15.own_ref), channel_id=1, source_target_pairs={{0,1},{1,0},{2,3},{3,2},{4,5},{5,4},{6,7},{7,6},{8,9},{9,8},{10,11... | collective-permute-start | bytes 1179656 | tf_op jit(solution)/shard_map/ppermute | solution.py:40
  76.9 1.8 %collective-permute-start.15 = (bf16[2,64,1536]{2,1,0:T(8,128)(2,1)S(1)}, bf16[2,64,1536]{2,1,0:T(8,128)(2,1)S(1)}, u32[]{:S(2)}, u32[]{:S(2)}) collective-permute-start(bf16[2,64,1536]{2,1,0:T(8,128)(2,1)S(1)} %join.13.own_ref), channel_id=1, source_target_pairs={{0,1},{1,0},{2,3},{3,2},{4,5},{5,4},{6,7},{7,6},{8,9},{9,8},{10,11... | collective-permute-start | bytes 1179656 | tf_op jit(solution)/shard_map/ppermute | solution.py:40
  80.3 14.2 %collective-permute-start.23 = (bf16[32,1280]{1,0:T(8,128)(2,1)S(1)}, bf16[32,1280]{1,0:T(8,128)(2,1)S(1)}, u32[]{:S(2)}, u32[]{:S(2)}) collective-permute-start(bf16[32,1280]{1,0:T(8,128)(2,1)S(1)} %get-tuple-element.48), channel_id=1, source_target_pairs={{0,24},{8,16},{16,8},{24,0},{1,25},{9,17},{17,9},{25,1},{2,26},{10... | collective-permute-start | bytes 245768 | tf_op jit(solution)/shard_map/ppermute | solution.py:40
  82.8 11.7 %collective-permute-start.22 = (bf16[32,1280]{1,0:T(8,128)(2,1)S(1)}, bf16[32,1280]{1,0:T(8,128)(2,1)S(1)}, u32[]{:S(2)}, u32[]{:S(2)}) collective-permute-start(bf16[32,1280]{1,0:T(8,128)(2,1)S(1)} %get-tuple-element.49), channel_id=1, source_target_pairs={{0,16},{8,24},{16,0},{24,8},{1,17},{9,25},{17,1},{25,9},{2,18},{10... | collective-permute-start | bytes 245768 | tf_op jit(solution)/shard_map/ppermute | solution.py:40
  83.3 11.2 %collective-permute-start.21 = (bf16[32,1280]{1,0:T(8,128)(2,1)S(1)}, bf16[32,1280]{1,0:T(8,128)(2,1)S(1)}, u32[]{:S(2)}, u32[]{:S(2)}) collective-permute-start(bf16[32,1280]{1,0:T(8,128)(2,1)S(1)} %get-tuple-element.47), channel_id=1, source_target_pairs={{0,8},{8,0},{16,24},{24,16},{1,9},{9,1},{17,25},{25,17},{2,10},{10... | collective-permute-start | bytes 245768 | tf_op jit(solution)/shard_map/ppermute | solution.py:40

commit v6 on v5

--- a/solution.py
+++ b/solution.py
@@ -354,13 +354,15 @@
         chunks.append(Chunk(rank, mp, keep, send))
 
     steps = 2 * chunks[0].levels
-    partials, partial = [], None
-    for index, (start, chunk) in enumerate(zip(starts, chunks)):
-        chunk.reach(steps - 2)
-        chunk.advance(partials[index - 2 : index - 1] if index > 1 else [])
-        chunk.advance(partials[index - 1 :])
-        partial = input_grads(chunk.send, w_in, partial, start)
-        partials.append(partial)
+    partial = None
+    while chunks[-1].done < steps:
+        for chunk in chunks[::-1]:
+            if chunk.done < steps:
+                after = [chunk.advance(after)]
+                if chunk.done == steps:
+                    start = starts[chunks.index(chunk)]
+                    partial = input_grads(chunk.send, w_in, partial, start)
+                    after = [partial]
     finals = [chunk.send for chunk in chunks]
 
     in_total = partial[:rows]

time: 95.4 us -> 94.1 us (0.986)
  waiting for transfers between devices: 30.2 us -> 28.6 us
    ppermute x24, waiting for transfers between devices: 30.2 us -> 28.6 us  [exchange(): return lax.ppermute(array, axis, [(i, i ^ step) for i in range(size)])]
  transfers between devices with their start and end apart: 24 -> 24, of which waited for: 10 -> 11; matrix products, arithmetic and copies ran while one was open for 0% -> 0% of each run, Pallas kernels for 29% -> 29%
where the time goes in v6:
time: 94.1 us; the launch traced here: 93.9 us
  Pallas kernels  31.9 us (34%)
  starting transfers between devices  30.3 us (32%)
  waiting for transfers between devices  28.6 us (30%)
  other arithmetic  1.73 us (2%)
  between operations  0.99 us (1%)
    ppermute x24, starting transfers between devices, exchange(): return lax.ppermute(array, axis, [(i, i ^ step) for i in range(size)])  30.3 us
    ppermute x24, waiting for transfers between devices, exchange(): return lax.ppermute(array, axis, [(i, i ^ step) for i in range(size)])  28.6 us
    pallas_call x1, Pallas kernels, weight_grads(): pl.pallas_call(kernel, grid=(2 * len(finals),), out_shape=(jax.ShapeDtype...  10.6 us
    pallas_call x3, Pallas kernels, forward(): pl.pallas_call(kernel, grid=(1,), out_shape=(jax.ShapeDtypeStruct((2, hal...  8.59 us
    pallas_call x1, Pallas kernels, load(): pl.pallas_call(kernel, out_shape=tuple((jax.ShapeDtypeStruct(w.shape, w.d...  7.72 us
    pallas_call x3, Pallas kernels, input_grads(): pl.pallas_call(kernel, grid=(1,), out_shape=jax.ShapeDtypeStruct((total,...  3.85 us
  transfers between devices with their start and end apart: 24, of which 11 were waited for; matrix products, arithmetic and copies ran while one was open for 0% of the time, Pallas kernels for 29%

profile of v6, /device:TPU:0, one launch (start us, length us, event | category | flops | bytes accessed | tf_op | source)
XLA Modules:
  0.0 93.9 jit_solution(12821687545828987076)
XLA Ops:
  0.6 0.9 %pad_maximum_fusion.1.refs_0_ = bf16[2,32,1280]{2,1,0:T(8,128)(2,1)S(1)} fusion(bf16[1,32,1280]{2,1,0:T(8,128)(2,1)} %bitcast.8, bf16[1,32,1280]{2,1,0:T(8,128)(2,1)} %bitcast.10), kind=kLoop, calls=%fused_computation.7 | loop fusion | flops 81920 | bytes 327680 | tf_op jit(solution)/shard_map/stack | solution.py:340
  1.6 3.0 %collective-permute-start = (bf16[2,32,1280]{2,1,0:T(8,128)(2,1)S(1)}, bf16[2,32,1280]{2,1,0:T(8,128)(2,1)S(1)}, u32[]{:S(2)}, u32[]{:S(2)}) collective-permute-start(bf16[2,32,1280]{2,1,0:T(8,128)(2,1)S(1)} %pad_maximum_fusion.1.refs_0_), channel_id=1, source_target_pairs={{0,8},{8,0},{16,24},{24,16},{1,9},{9,1},{17,25},{25,17},{2,10},{10... | collective-permute-start | bytes 491528 | tf_op jit(solution)/shard_map/ppermute | solution.py:40
  4.6 1.5 %collective-permute-start.1 = (bf16[2,32,1280]{2,1,0:T(8,128)(2,1)S(1)}, bf16[2,32,1280]{2,1,0:T(8,128)(2,1)S(1)}, u32[]{:S(2)}, u32[]{:S(2)}) collective-permute-start(bf16[2,32,1280]{2,1,0:T(8,128)(2,1)S(1)} %pad_maximum_fusion.1.refs_0_), channel_id=1, source_target_pairs={{0,16},{8,24},{16,0},{24,8},{1,17},{9,25},{17,1},{25,9},{2,18},{10... | collective-permute-start | bytes 491528 | tf_op jit(solution)/shard_map/ppermute | solution.py:40
  6.1 7.7 %load.1 = (bf16[1280,4608]{1,0:T(8,128)(2,1)S(1)}, bf16[4608,1280]{1,0:T(8,128)(2,1)S(1)}) custom-call(bf16[1280,4608]{1,0:T(8,128)(2,1)} %refs_0_.1, bf16[4608,1280]{1,0:T(8,128)(2,1)} %refs_1_.1), custom_call_target="tpu_custom_call" | custom-call | bytes 47185920 | tf_op jit(solution)/shard_map/load/pallas_call | solution.py:84
  13.9 2.9 %forward.3 = (f32[2,64,1536]{2,1,0:T(8,128)S(1)}, bf16[2,64,1536]{2,1,0:T(8,128)(2,1)S(1)}) custom-call(s32[1]{0:T(128)} %bitcast.rank_ref, bf16[2,32,1280]{2,1,0:T(8,128)(2,1)S(1)} %pad_maximum_fusion.1.refs_0_, bf16[2,32,1280]{2,1,0:T(8,128)(2,1)S(1)} %collective-permute-done.refs_1_, bf16[2,32,1280]{2,1,0:T(8,128)(2,1)S(1)} %collective-permute-done.1.refs_2_, ...), custom_call_target="tpu_custom_call" | custom-call | flops 1006632960 | bytes 7864320 | tf_op jit(solution)/shard_map/forward/pallas_call | solution.py:129
  16.8 0.1 collective-permute-start.3
  16.8 2.9 %forward.4 = (f32[2,64,1536]{2,1,0:T(8,128)S(1)}, bf16[2,64,1536]{2,1,0:T(8,128)(2,1)S(1)}) custom-call(s32[1]{0:T(128)} %bitcast.rank_ref, bf16[2,32,1280]{2,1,0:T(8,128)(2,1)S(1)} %pad_maximum_fusion.1.refs_0_, bf16[2,32,1280]{2,1,0:T(8,128)(2,1)S(1)} %collective-permute-done.refs_1_, bf16[2,32,1280]{2,1,0:T(8,128)(2,1)S(1)} %collective-permute-done.1.refs_2_, ...), custom_call_target="tpu_custom_call" | custom-call | flops 1006632960 | bytes 7864320 | tf_op jit(solution)/shard_map/forward/pallas_call | solution.py:129
  19.7 0.1 halve.6
  19.9 0.6 collective-permute-start.5
  20.5 2.0 %collective-permute-start.4 = (bf16[2,32,1536]{2,1,0:T(8,128)(2,1)S(1)}, bf16[2,32,1536]{2,1,0:T(8,128)(2,1)S(1)}, u32[]{:S(2)}, u32[]{:S(2)}) collective-permute-start(bf16[2,32,1536]{2,1,0:T(8,128)(2,1)S(1)} %get-tuple-element.30.rest_0_), channel_id=1, source_target_pairs={{0,2},{1,3},{2,0},{3,1},{4,6},{5,7},{6,4},{7,5},{8,10},{9,11},{10,... | collective-permute-start | bytes 589832 | tf_op jit(solution)/shard_map/ppermute | solution.py:40
  22.5 2.9 %forward.5 = (f32[2,64,1536]{2,1,0:T(8,128)S(1)}, bf16[2,64,1536]{2,1,0:T(8,128)(2,1)S(1)}) custom-call(s32[1]{0:T(128)} %bitcast.rank_ref, bf16[2,32,1280]{2,1,0:T(8,128)(2,1)S(1)} %pad_maximum_fusion.1.refs_0_, bf16[2,32,1280]{2,1,0:T(8,128)(2,1)S(1)} %collective-permute-done.refs_1_, bf16[2,32,1280]{2,1,0:T(8,128)(2,1)S(1)} %collective-permute-done.1.refs_2_, ...), custom_call_target="tpu_custom_call" | custom-call | flops 1006632960 | bytes 7864320 | tf_op jit(solution)/shard_map/forward/pallas_call | solution.py:129
  25.4 0.1 halve.7
  25.5 2.2 %collective-permute-done.4.received_ref = bf16[2,32,1536]{2,1,0:T(8,128)(2,1)S(1)} collective-permute-done((bf16[2,32,1536]{2,1,0:T(8,128)(2,1)S(1)}, bf16[2,32,1536]{2,1,0:T(8,128)(2,1)S(1)}, u32[]{:S(2)}, u32[]{:S(2)}) %collective-permute-start.4) | collective-permute-done | bytes 196640 | tf_op jit(solution)/shard_map/ppermute | solution.py:40
  27.7 0.1 collective-permute-start.6
  27.8 1.8 %collective-permute-start.9 = (bf16[2,32,1536]{2,1,0:T(8,128)(2,1)S(1)}, bf16[2,32,1536]{2,1,0:T(8,128)(2,1)S(1)}, u32[]{:S(2)}, u32[]{:S(2)}) collective-permute-start(bf16[2,32,1536]{2,1,0:T(8,128)(2,1)S(1)} %get-tuple-element.35.rest_0_), channel_id=1, source_target_pairs={{0,2},{1,3},{2,0},{3,1},{4,6},{5,7},{6,4},{7,5},{8,10},{9,11},{10,... | collective-permute-start | bytes 589832 | tf_op jit(solution)/shard_map/ppermute | solution.py:40
  29.7 1.7 %collective-permute-start.7 = (bf16[2,32,1536]{2,1,0:T(8,128)(2,1)S(1)}, bf16[2,32,1536]{2,1,0:T(8,128)(2,1)S(1)}, u32[]{:S(2)}, u32[]{:S(2)}) collective-permute-start(bf16[2,32,1536]{2,1,0:T(8,128)(2,1)S(1)} %get-tuple-element.38.rest_0_), channel_id=1, source_target_pairs={{0,2},{1,3},{2,0},{3,1},{4,6},{5,7},{6,4},{7,5},{8,10},{9,11},{10,... | collective-permute-start | bytes 589832 | tf_op jit(solution)/shard_map/ppermute | solution.py:40
  31.4 2.5 %collective-permute-start.8 = (bf16[2,16,1536]{2,1,0:T(8,128)(2,1)S(1)}, bf16[2,16,1536]{2,1,0:T(8,128)(2,1)S(1)}, u32[]{:S(2)}, u32[]{:S(2)}) collective-permute-start(bf16[2,16,1536]{2,1,0:T(8,128)(2,1)S(1)} %get-tuple-element.36.rest_0_), channel_id=1, source_target_pairs={{0,6},{1,7},{2,4},{3,5},{4,2},{5,3},{6,0},{7,1},{8,14},{9,15},{10,... | collective-permute-start | bytes 294920 | tf_op jit(solution)/shard_map/ppermute | solution.py:40
  33.9 1.7 %collective-permute-done.9.received_ref = bf16[2,32,1536]{2,1,0:T(8,128)(2,1)S(1)} collective-permute-done((bf16[2,32,1536]{2,1,0:T(8,128)(2,1)S(1)}, bf16[2,32,1536]{2,1,0:T(8,128)(2,1)S(1)}, u32[]{:S(2)}, u32[]{:S(2)}) %collective-permute-start.9) | collective-permute-done | bytes 196640 | tf_op jit(solution)/shard_map/ppermute | solution.py:40
  35.6 3.8 %collective-permute-start.12 = (bf16[2,16,1536]{2,1,0:T(8,128)(2,1)S(1)}, bf16[2,16,1536]{2,1,0:T(8,128)(2,1)S(1)}, u32[]{:S(2)}, u32[]{:S(2)}) collective-permute-start(bf16[2,16,1536]{2,1,0:T(8,128)(2,1)S(1)} %get-tuple-element.41.rest_0_), channel_id=1, source_target_pairs={{0,6},{1,7},{2,4},{3,5},{4,2},{5,3},{6,0},{7,1},{8,14},{9,15},{10,... | collective-permute-start | bytes 294920 | tf_op jit(solution)/shard_map/ppermute | solution.py:40
  39.5 4.7 %collective-permute-done.8.received_ref = bf16[2,16,1536]{2,1,0:T(8,128)(2,1)S(1)} collective-permute-done((bf16[2,16,1536]{2,1,0:T(8,128)(2,1)S(1)}, bf16[2,16,1536]{2,1,0:T(8,128)(2,1)S(1)}, u32[]{:S(2)}, u32[]{:S(2)}) %collective-permute-start.8) | collective-permute-done | bytes 98336 | tf_op jit(solution)/shard_map/ppermute | solution.py:40
  44.2 0.1 activate.3.rest_0_.own_ref
  44.3 1.5 %collective-permute-start.11 = (bf16[2,16,1536]{2,1,0:T(8,128)(2,1)S(1)}, bf16[2,16,1536]{2,1,0:T(8,128)(2,1)S(1)}, u32[]{:S(2)}, u32[]{:S(2)}) collective-permute-start(bf16[2,16,1536]{2,1,0:T(8,128)(2,1)S(1)} %activate.3.rest_0_.own_ref), channel_id=1, source_target_pairs={{0,6},{1,7},{2,4},{3,5},{4,2},{5,3},{6,0},{7,1},{8,14},{9,15},{10,... | collective-permute-start | bytes 294920 | tf_op jit(solution)/shard_map/ppermute | solution.py:40
  45.9 4.8 %collective-permute-done.11.received_ref = bf16[2,16,1536]{2,1,0:T(8,128)(2,1)S(1)} collective-permute-done((bf16[2,16,1536]{2,1,0:T(8,128)(2,1)S(1)}, bf16[2,16,1536]{2,1,0:T(8,128)(2,1)S(1)}, u32[]{:S(2)}, u32[]{:S(2)}) %collective-permute-start.11) | collective-permute-done | bytes 98336 | tf_op jit(solution)/shard_map/ppermute | solution.py:40
  50.9 1.5 %collective-permute-start.10 = (bf16[2,16,1536]{2,1,0:T(8,128)(2,1)S(1)}, bf16[2,16,1536]{2,1,0:T(8,128)(2,1)S(1)}, u32[]{:S(2)}, u32[]{:S(2)}) collective-permute-start(bf16[2,16,1536]{2,1,0:T(8,128)(2,1)S(1)} %get-tuple-element.43.rest_0_), channel_id=1, source_target_pairs={{0,6},{1,7},{2,4},{3,5},{4,2},{5,3},{6,0},{7,1},{8,14},{9,15},{10,... | collective-permute-start | bytes 294920 | tf_op jit(solution)/shard_map/ppermute | solution.py:40
  52.3 2.4 %collective-permute-start.15 = (bf16[2,16,1536]{2,1,0:T(8,128)(2,1)S(1)}, bf16[2,16,1536]{2,1,0:T(8,128)(2,1)S(1)}, u32[]{:S(2)}, u32[]{:S(2)}) collective-permute-start(bf16[2,16,1536]{2,1,0:T(8,128)(2,1)S(1)} %activate.4.rest_0_.own_ref), channel_id=1, source_target_pairs={{0,6},{1,7},{2,4},{3,5},{4,2},{5,3},{6,0},{7,1},{8,14},{9,15},{10,... | collective-permute-start | bytes 294920 | tf_op jit(solution)/shard_map/ppermute | solution.py:40
  54.7 3.9 %collective-permute-done.10.received_ref = bf16[2,16,1536]{2,1,0:T(8,128)(2,1)S(1)} collective-permute-done((bf16[2,16,1536]{2,1,0:T(8,128)(2,1)S(1)}, bf16[2,16,1536]{2,1,0:T(8,128)(2,1)S(1)}, u32[]{:S(2)}, u32[]{:S(2)}) %collective-permute-start.10) | collective-permute-done | bytes 98336 | tf_op jit(solution)/shard_map/ppermute | solution.py:40
  58.7 0.1 activate.5.rest_0_.own_ref
  58.8 1.0 %collective-permute-done.15.received_ref = bf16[2,16,1536]{2,1,0:T(8,128)(2,1)S(1)} collective-permute-done((bf16[2,16,1536]{2,1,0:T(8,128)(2,1)S(1)}, bf16[2,16,1536]{2,1,0:T(8,128)(2,1)S(1)}, u32[]{:S(2)}, u32[]{:S(2)}) %collective-permute-start.15) | collective-permute-done | bytes 98336 | tf_op jit(solution)/shard_map/ppermute | solution.py:40
  59.8 0.2 collective-permute-done.14.received_ref
  60.0 0.1 collective-permute-start.17
  60.1 2.2 %collective-permute-start.13 = (bf16[2,16,1536]{2,1,0:T(8,128)(2,1)S(1)}, bf16[2,16,1536]{2,1,0:T(8,128)(2,1)S(1)}, u32[]{:S(2)}, u32[]{:S(2)}) collective-permute-start(bf16[2,16,1536]{2,1,0:T(8,128)(2,1)S(1)} %activate.5.rest_0_.own_ref), channel_id=1, source_target_pairs={{0,6},{1,7},{2,4},{3,5},{4,2},{5,3},{6,0},{7,1},{8,14},{9,15},{10,... | collective-permute-start | bytes 294920 | tf_op jit(solution)/shard_map/ppermute | solution.py:40
  62.3 0.2 collective-permute-start.18
  62.5 5.1 %collective-permute-done.13.received_ref = bf16[2,16,1536]{2,1,0:T(8,128)(2,1)S(1)} collective-permute-done((bf16[2,16,1536]{2,1,0:T(8,128)(2,1)S(1)}, bf16[2,16,1536]{2,1,0:T(8,128)(2,1)S(1)}, u32[]{:S(2)}, u32[]{:S(2)}) %collective-permute-start.13) | collective-permute-done | bytes 98336 | tf_op jit(solution)/shard_map/ppermute | solution.py:40
  67.6 1.5 %collective-permute-start.16 = (bf16[2,32,1536]{2,1,0:T(8,128)(2,1)S(1)}, bf16[2,32,1536]{2,1,0:T(8,128)(2,1)S(1)}, u32[]{:S(2)}, u32[]{:S(2)}) collective-permute-start(bf16[2,32,1536]{2,1,0:T(8,128)(2,1)S(1)} %join.12.rest_0_.own_ref), channel_id=1, source_target_pairs={{0,2},{1,3},{2,0},{3,1},{4,6},{5,7},{6,4},{7,5},{8,10},{9,11},{10,... | collective-permute-start | bytes 589832 | tf_op jit(solution)/shard_map/ppermute | solution.py:40
  69.2 2.3 %collective-permute-done.18.received_ref = bf16[2,32,1536]{2,1,0:T(8,128)(2,1)S(1)} collective-permute-done((bf16[2,32,1536]{2,1,0:T(8,128)(2,1)S(1)}, bf16[2,32,1536]{2,1,0:T(8,128)(2,1)S(1)}, u32[]{:S(2)}, u32[]{:S(2)}) %collective-permute-start.18) | collective-permute-done | bytes 196640 | tf_op jit(solution)/shard_map/ppermute | solution.py:40
  71.6 0.1 collective-permute-start.20
  71.7 1.3 %input_grads.3.rest_0_.refs_0_ = f32[128,1280]{1,0:T(8,128)S(1)} custom-call(bf16[2,128,1536]{2,1,0:T(8,128)(2,1)S(1)} %join.14.grad_ref.refs_0_, bf16[1280,4608]{1,0:T(8,128)(2,1)S(1)} %get-tuple-element.25.refs_4_.wi_ref), custom_call_target="tpu_custom_call" | custom-call | flops 503316480 | bytes 3932160 | tf_op jit(solution)/shard_map/input_grads/pallas_call | solution.py:275
  73.0 2.6 %collective-permute-done.16.received_ref = bf16[2,32,1536]{2,1,0:T(8,128)(2,1)S(1)} collective-permute-done((bf16[2,32,1536]{2,1,0:T(8,128)(2,1)S(1)}, bf16[2,32,1536]{2,1,0:T(8,128)(2,1)S(1)}, u32[]{:S(2)}, u32[]{:S(2)}) %collective-permute-start.16) | collective-permute-done | bytes 196640 | tf_op jit(solution)/shard_map/ppermute | solution.py:40
  75.6 0.1 collective-permute-start.19
  75.7 0.3 convolution_convert_fusion.xt_ref
  76.1 1.3 %input_grads.4.rest_0_.refs_0_ = f32[128,1280]{1,0:T(8,128)S(1)} custom-call(bf16[2,128,1536]{2,1,0:T(8,128)(2,1)S(1)} %join.16.grad_ref.refs_1_, bf16[1280,4608]{1,0:T(8,128)(2,1)S(1)} %get-tuple-element.25.refs_4_.wi_ref, f32[128,1280]{1,0:T(8,128)S(1)} %input_grads.3.rest_0_.refs_0_), custom_call_target="tpu_custom_call" | custom-call | flops 503316480 | bytes 3932160 | tf_op jit(solution)/shard_map/input_grads/pallas_call | solution.py:275
  77.4 0.2 join.17.grad_ref.refs_2_
  77.6 1.3 %input_grads.5 = f32[128,1280]{1,0:T(8,128)S(1)} custom-call(bf16[2,128,1536]{2,1,0:T(8,128)(2,1)S(1)} %join.17.grad_ref.refs_2_, bf16[1280,4608]{1,0:T(8,128)(2,1)S(1)} %get-tuple-element.25.refs_4_.wi_ref, f32[128,1280]{1,0:T(8,128)S(1)} %input_grads.4.rest_0_.refs_0_), custom_call_target="tpu_custom_call" | custom-call | flops 503316480 | bytes 3932160 | tf_op jit(solution)/shard_map/input_grads/pallas_call | solution.py:275
  79.0 2.5 %collective-permute-start.23 = (bf16[32,1280]{1,0:T(8,128)(2,1)S(1)}, bf16[32,1280]{1,0:T(8,128)(2,1)S(1)}, u32[]{:S(2)}, u32[]{:S(2)}) collective-permute-start(bf16[32,1280]{1,0:T(8,128)(2,1)S(1)} %get-tuple-element.48), channel_id=1, source_target_pairs={{0,24},{8,16},{16,8},{24,0},{1,25},{9,17},{17,9},{25,1},{2,26},{10... | collective-permute-start | bytes 245768 | tf_op jit(solution)/shard_map/ppermute | solution.py:40
  81.5 0.5 collective-permute-start.22
  82.0 0.5 collective-permute-start.21
  82.5 10.6 %weight_grads.1 = (bf16[1280,4608]{1,0:T(8,128)(2,1)}, bf16[4608,1280]{1,0:T(8,128)(2,1)}) custom-call(bf16[1280,128]{1,0:T(8,128)(2,1)S(1)} %convolution_convert_fusion.xt_ref, bf16[128,1280]{1,0:T(8,128)(2,1)S(1)} %slice_bitcast_fusion.gs_ref, bf16[2,128,1536]{2,1,0:T(8,128)(2,1)S(1)} %join.14.grad_ref.refs_0_, ...), custom_call_target="tpu_custom_call" | custom-call | flops 3019898880 | bytes 23592960 | tf_op jit(solution)/shard_map/weight_grads/pallas_call | solution.py:312
  93.2 0.7 fusion.1
  (39 shorter events, 0.9 us)
Async XLA Ops:
  1.6 12.3 %collective-permute-start = (bf16[2,32,1280]{2,1,0:T(8,128)(2,1)S(1)}, bf16[2,32,1280]{2,1,0:T(8,128)(2,1)S(1)}, u32[]{:S(2)}, u32[]{:S(2)}) collective-permute-start(bf16[2,32,1280]{2,1,0:T(8,128)(2,1)S(1)} %pad_maximum_fusion.1.refs_0_), channel_id=1, source_target_pairs={{0,8},{8,0},{16,24},{24,16},{1,9},{9,1},{17,25},{25,17},{2,10},{10... | collective-permute-start | bytes 491528 | tf_op jit(solution)/shard_map/ppermute | solution.py:40
  4.6 9.3 %collective-permute-start.1 = (bf16[2,32,1280]{2,1,0:T(8,128)(2,1)S(1)}, bf16[2,32,1280]{2,1,0:T(8,128)(2,1)S(1)}, u32[]{:S(2)}, u32[]{:S(2)}) collective-permute-start(bf16[2,32,1280]{2,1,0:T(8,128)(2,1)S(1)} %pad_maximum_fusion.1.refs_0_), channel_id=1, source_target_pairs={{0,16},{8,24},{16,0},{24,8},{1,17},{9,25},{17,1},{25,9},{2,18},{10... | collective-permute-start | bytes 491528 | tf_op jit(solution)/shard_map/ppermute | solution.py:40
  6.1 7.8 %collective-permute-start.2 = (bf16[2,32,1280]{2,1,0:T(8,128)(2,1)S(1)}, bf16[2,32,1280]{2,1,0:T(8,128)(2,1)S(1)}, u32[]{:S(2)}, u32[]{:S(2)}) collective-permute-start(bf16[2,32,1280]{2,1,0:T(8,128)(2,1)S(1)} %pad_maximum_fusion.1.refs_0_), channel_id=1, source_target_pairs={{0,24},{8,16},{16,8},{24,0},{1,25},{9,17},{17,9},{25,1},{2,26},{10... | collective-permute-start | bytes 491528 | tf_op jit(solution)/shard_map/ppermute | solution.py:40
  16.8 3.0 %collective-permute-start.3 = (bf16[2,64,1536]{2,1,0:T(8,128)(2,1)S(1)}, bf16[2,64,1536]{2,1,0:T(8,128)(2,1)S(1)}, u32[]{:S(2)}, u32[]{:S(2)}) collective-permute-start(bf16[2,64,1536]{2,1,0:T(8,128)(2,1)S(1)} %get-tuple-element.27.refs_6_), channel_id=1, source_target_pairs={{0,1},{1,0},{2,3},{3,2},{4,5},{5,4},{6,7},{7,6},{8,9},{9,8},{10,11... | collective-permute-start | bytes 1179656 | tf_op jit(solution)/shard_map/ppermute | solution.py:40
  19.9 5.5 %collective-permute-start.5 = (bf16[2,64,1536]{2,1,0:T(8,128)(2,1)S(1)}, bf16[2,64,1536]{2,1,0:T(8,128)(2,1)S(1)}, u32[]{:S(2)}, u32[]{:S(2)}) collective-permute-start(bf16[2,64,1536]{2,1,0:T(8,128)(2,1)S(1)} %relay.2.refs_6_), channel_id=1, source_target_pairs={{0,1},{1,0},{2,3},{3,2},{4,5},{5,4},{6,7},{7,6},{8,9},{9,8},{10,11... | collective-permute-start | bytes 1179656 | tf_op jit(solution)/shard_map/ppermute | solution.py:40
  20.5 7.2 %collective-permute-start.4 = (bf16[2,32,1536]{2,1,0:T(8,128)(2,1)S(1)}, bf16[2,32,1536]{2,1,0:T(8,128)(2,1)S(1)}, u32[]{:S(2)}, u32[]{:S(2)}) collective-permute-start(bf16[2,32,1536]{2,1,0:T(8,128)(2,1)S(1)} %get-tuple-element.30.rest_0_), channel_id=1, source_target_pairs={{0,2},{1,3},{2,0},{3,1},{4,6},{5,7},{6,4},{7,5},{8,10},{9,11},{10,... | collective-permute-start | bytes 589832 | tf_op jit(solution)/shard_map/ppermute | solution.py:40
  27.7 1.9 %collective-permute-start.6 = (bf16[2,64,1536]{2,1,0:T(8,128)(2,1)S(1)}, bf16[2,64,1536]{2,1,0:T(8,128)(2,1)S(1)}, u32[]{:S(2)}, u32[]{:S(2)}) collective-permute-start(bf16[2,64,1536]{2,1,0:T(8,128)(2,1)S(1)} %relay.3.rest_0_), channel_id=1, source_target_pairs={{0,1},{1,0},{2,3},{3,2},{4,5},{5,4},{6,7},{7,6},{8,9},{9,8},{10,11... | collective-permute-start | bytes 1179656 | tf_op jit(solution)/shard_map/ppermute | solution.py:40
  27.8 7.8 %collective-permute-start.9 = (bf16[2,32,1536]{2,1,0:T(8,128)(2,1)S(1)}, bf16[2,32,1536]{2,1,0:T(8,128)(2,1)S(1)}, u32[]{:S(2)}, u32[]{:S(2)}) collective-permute-start(bf16[2,32,1536]{2,1,0:T(8,128)(2,1)S(1)} %get-tuple-element.35.rest_0_), channel_id=1, source_target_pairs={{0,2},{1,3},{2,0},{3,1},{4,6},{5,7},{6,4},{7,5},{8,10},{9,11},{10,... | collective-permute-start | bytes 589832 | tf_op jit(solution)/shard_map/ppermute | solution.py:40
  29.7 16.0 %collective-permute-start.7 = (bf16[2,32,1536]{2,1,0:T(8,128)(2,1)S(1)}, bf16[2,32,1536]{2,1,0:T(8,128)(2,1)S(1)}, u32[]{:S(2)}, u32[]{:S(2)}) collective-permute-start(bf16[2,32,1536]{2,1,0:T(8,128)(2,1)S(1)} %get-tuple-element.38.rest_0_), channel_id=1, source_target_pairs={{0,2},{1,3},{2,0},{3,1},{4,6},{5,7},{6,4},{7,5},{8,10},{9,11},{10,... | collective-permute-start | bytes 589832 | tf_op jit(solution)/shard_map/ppermute | solution.py:40
  31.4 12.8 %collective-permute-start.8 = (bf16[2,16,1536]{2,1,0:T(8,128)(2,1)S(1)}, bf16[2,16,1536]{2,1,0:T(8,128)(2,1)S(1)}, u32[]{:S(2)}, u32[]{:S(2)}) collective-permute-start(bf16[2,16,1536]{2,1,0:T(8,128)(2,1)S(1)} %get-tuple-element.36.rest_0_), channel_id=1, source_target_pairs={{0,6},{1,7},{2,4},{3,5},{4,2},{5,3},{6,0},{7,1},{8,14},{9,15},{10,... | collective-permute-start | bytes 294920 | tf_op jit(solution)/shard_map/ppermute | solution.py:40
  35.6 10.2 %collective-permute-start.12 = (bf16[2,16,1536]{2,1,0:T(8,128)(2,1)S(1)}, bf16[2,16,1536]{2,1,0:T(8,128)(2,1)S(1)}, u32[]{:S(2)}, u32[]{:S(2)}) collective-permute-start(bf16[2,16,1536]{2,1,0:T(8,128)(2,1)S(1)} %get-tuple-element.41.rest_0_), channel_id=1, source_target_pairs={{0,6},{1,7},{2,4},{3,5},{4,2},{5,3},{6,0},{7,1},{8,14},{9,15},{10,... | collective-permute-start | bytes 294920 | tf_op jit(solution)/shard_map/ppermute | solution.py:40
  44.3 6.5 %collective-permute-start.11 = (bf16[2,16,1536]{2,1,0:T(8,128)(2,1)S(1)}, bf16[2,16,1536]{2,1,0:T(8,128)(2,1)S(1)}, u32[]{:S(2)}, u32[]{:S(2)}) collective-permute-start(bf16[2,16,1536]{2,1,0:T(8,128)(2,1)S(1)} %activate.3.rest_0_.own_ref), channel_id=1, source_target_pairs={{0,6},{1,7},{2,4},{3,5},{4,2},{5,3},{6,0},{7,1},{8,14},{9,15},{10,... | collective-permute-start | bytes 294920 | tf_op jit(solution)/shard_map/ppermute | solution.py:40
  50.8 9.2 %collective-permute-start.14 = (bf16[2,32,1536]{2,1,0:T(8,128)(2,1)S(1)}, bf16[2,32,1536]{2,1,0:T(8,128)(2,1)S(1)}, u32[]{:S(2)}, u32[]{:S(2)}) collective-permute-start(bf16[2,32,1536]{2,1,0:T(8,128)(2,1)S(1)} %join.9.rest_0_.own_ref), channel_id=1, source_target_pairs={{0,2},{1,3},{2,0},{3,1},{4,6},{5,7},{6,4},{7,5},{8,10},{9,11},{10,... | collective-permute-start | bytes 589832 | tf_op jit(solution)/shard_map/ppermute | solution.py:40
  50.9 7.8 %collective-permute-start.10 = (bf16[2,16,1536]{2,1,0:T(8,128)(2,1)S(1)}, bf16[2,16,1536]{2,1,0:T(8,128)(2,1)S(1)}, u32[]{:S(2)}, u32[]{:S(2)}) collective-permute-start(bf16[2,16,1536]{2,1,0:T(8,128)(2,1)S(1)} %get-tuple-element.43.rest_0_), channel_id=1, source_target_pairs={{0,6},{1,7},{2,4},{3,5},{4,2},{5,3},{6,0},{7,1},{8,14},{9,15},{10,... | collective-permute-start | bytes 294920 | tf_op jit(solution)/shard_map/ppermute | solution.py:40
  52.3 7.4 %collective-permute-start.15 = (bf16[2,16,1536]{2,1,0:T(8,128)(2,1)S(1)}, bf16[2,16,1536]{2,1,0:T(8,128)(2,1)S(1)}, u32[]{:S(2)}, u32[]{:S(2)}) collective-permute-start(bf16[2,16,1536]{2,1,0:T(8,128)(2,1)S(1)} %activate.4.rest_0_.own_ref), channel_id=1, source_target_pairs={{0,6},{1,7},{2,4},{3,5},{4,2},{5,3},{6,0},{7,1},{8,14},{9,15},{10,... | collective-permute-start | bytes 294920 | tf_op jit(solution)/shard_map/ppermute | solution.py:40
  58.7 10.5 %copy-start = (bf16[32,1280]{1,0:T(8,128)(2,1)S(1)}, bf16[32,1280]{1,0:T(8,128)(2,1)}, u32[]{:S(2)}) copy-start(bf16[32,1280]{1,0:T(8,128)(2,1)} %param.5) | copy-start | bytes 245764
  58.7 10.5 %copy-start.1 = (bf16[32,1280]{1,0:T(8,128)(2,1)S(1)}, bf16[32,1280]{1,0:T(8,128)(2,1)}, u32[]{:S(2)}) copy-start(bf16[32,1280]{1,0:T(8,128)(2,1)} %param.4) | copy-start | bytes 245764
  60.0 11.6 %collective-permute-start.17 = (bf16[2,64,1536]{2,1,0:T(8,128)(2,1)S(1)}, bf16[2,64,1536]{2,1,0:T(8,128)(2,1)S(1)}, u32[]{:S(2)}, u32[]{:S(2)}) collective-permute-start(bf16[2,64,1536]{2,1,0:T(8,128)(2,1)S(1)} %join.11.rest_0_.own_ref), channel_id=1, source_target_pairs={{0,1},{1,0},{2,3},{3,2},{4,5},{5,4},{6,7},{7,6},{8,9},{9,8},{10,11... | collective-permute-start | bytes 1179656 | tf_op jit(solution)/shard_map/ppermute | solution.py:40
  60.1 7.5 %collective-permute-start.13 = (bf16[2,16,1536]{2,1,0:T(8,128)(2,1)S(1)}, bf16[2,16,1536]{2,1,0:T(8,128)(2,1)S(1)}, u32[]{:S(2)}, u32[]{:S(2)}) collective-permute-start(bf16[2,16,1536]{2,1,0:T(8,128)(2,1)S(1)} %activate.5.rest_0_.own_ref), channel_id=1, source_target_pairs={{0,6},{1,7},{2,4},{3,5},{4,2},{5,3},{6,0},{7,1},{8,14},{9,15},{10,... | collective-permute-start | bytes 294920 | tf_op jit(solution)/shard_map/ppermute | solution.py:40
  62.3 9.2 %collective-permute-start.18 = (bf16[2,32,1536]{2,1,0:T(8,128)(2,1)S(1)}, bf16[2,32,1536]{2,1,0:T(8,128)(2,1)S(1)}, u32[]{:S(2)}, u32[]{:S(2)}) collective-permute-start(bf16[2,32,1536]{2,1,0:T(8,128)(2,1)S(1)} %join.10.rest_0_.own_ref), channel_id=1, source_target_pairs={{0,2},{1,3},{2,0},{3,1},{4,6},{5,7},{6,4},{7,5},{8,10},{9,11},{10,... | collective-permute-start | bytes 589832 | tf_op jit(solution)/shard_map/ppermute | solution.py:40
  67.6 7.9 %collective-permute-start.16 = (bf16[2,32,1536]{2,1,0:T(8,128)(2,1)S(1)}, bf16[2,32,1536]{2,1,0:T(8,128)(2,1)S(1)}, u32[]{:S(2)}, u32[]{:S(2)}) collective-permute-start(bf16[2,32,1536]{2,1,0:T(8,128)(2,1)S(1)} %join.12.rest_0_.own_ref), channel_id=1, source_target_pairs={{0,2},{1,3},{2,0},{3,1},{4,6},{5,7},{6,4},{7,5},{8,10},{9,11},{10,... | collective-permute-start | bytes 589832 | tf_op jit(solution)/shard_map/ppermute | solution.py:40
  71.6 4.4 %collective-permute-start.20 = (bf16[2,64,1536]{2,1,0:T(8,128)(2,1)S(1)}, bf16[2,64,1536]{2,1,0:T(8,128)(2,1)S(1)}, u32[]{:S(2)}, u32[]{:S(2)}) collective-permute-start(bf16[2,64,1536]{2,1,0:T(8,128)(2,1)S(1)} %join.13.rest_0_.own_ref), channel_id=1, source_target_pairs={{0,1},{1,0},{2,3},{3,2},{4,5},{5,4},{6,7},{7,6},{8,9},{9,8},{10,11... | collective-permute-start | bytes 1179656 | tf_op jit(solution)/shard_map/ppermute | solution.py:40
  75.6 1.8 %collective-permute-start.19 = (bf16[2,64,1536]{2,1,0:T(8,128)(2,1)S(1)}, bf16[2,64,1536]{2,1,0:T(8,128)(2,1)S(1)}, u32[]{:S(2)}, u32[]{:S(2)}) collective-permute-start(bf16[2,64,1536]{2,1,0:T(8,128)(2,1)S(1)} %join.15.rest_0_.own_ref), channel_id=1, source_target_pairs={{0,1},{1,0},{2,3},{3,2},{4,5},{5,4},{6,7},{7,6},{8,9},{9,8},{10,11... | collective-permute-start | bytes 1179656 | tf_op jit(solution)/shard_map/ppermute | solution.py:40
  79.0 14.2 %collective-permute-start.23 = (bf16[32,1280]{1,0:T(8,128)(2,1)S(1)}, bf16[32,1280]{1,0:T(8,128)(2,1)S(1)}, u32[]{:S(2)}, u32[]{:S(2)}) collective-permute-start(bf16[32,1280]{1,0:T(8,128)(2,1)S(1)} %get-tuple-element.48), channel_id=1, source_target_pairs={{0,24},{8,16},{16,8},{24,0},{1,25},{9,17},{17,9},{25,1},{2,26},{10... | collective-permute-start | bytes 245768 | tf_op jit(solution)/shard_map/ppermute | solution.py:40
  81.5 11.7 %collective-permute-start.22 = (bf16[32,1280]{1,0:T(8,128)(2,1)S(1)}, bf16[32,1280]{1,0:T(8,128)(2,1)S(1)}, u32[]{:S(2)}, u32[]{:S(2)}) collective-permute-start(bf16[32,1280]{1,0:T(8,128)(2,1)S(1)} %get-tuple-element.49), channel_id=1, source_target_pairs={{0,16},{8,24},{16,0},{24,8},{1,17},{9,25},{17,1},{25,9},{2,18},{10... | collective-permute-start | bytes 245768 | tf_op jit(solution)/shard_map/ppermute | solution.py:40
  82.0 11.2 %collective-permute-start.21 = (bf16[32,1280]{1,0:T(8,128)(2,1)S(1)}, bf16[32,1280]{1,0:T(8,128)(2,1)S(1)}, u32[]{:S(2)}, u32[]{:S(2)}) collective-permute-start(bf16[32,1280]{1,0:T(8,128)(2,1)S(1)} %get-tuple-element.47), channel_id=1, source_target_pairs={{0,8},{8,0},{16,24},{24,16},{1,9},{9,1},{17,25},{25,17},{2,10},{10... | collective-permute-start | bytes 245768 | tf_op jit(solution)/shard_map/ppermute | solution.py:40

commit v7 on v6

--- a/solution.py
+++ b/solution.py
@@ -236,14 +236,53 @@
     )(rank, own, received, *after)
 
 
+def join_line(rank, own, others, after=()):
+    _, part, width = own.shape
+
+    def kernel(rank_ref, own_ref, one_ref, two_ref, three_ref, *rest):
+        out_ref = rest[-1]
+
+        def outer(first):
+            def inner(second):
+                for flip, source in (
+                    ((0, 0), own_ref),
+                    ((1, 0), one_ref),
+                    ((1, 1), two_ref),
+                    ((0, 1), three_ref),
+                ):
+                    place = 2 * (first ^ flip[0]) + (second ^ flip[1])
+                    out_ref[:, place * part : (place + 1) * part] = source[...]
+
+            by_side(rank_ref, 2, inner)
+
+        by_side(rank_ref, 1, outer)
+
+    return pl.pallas_call(
+        kernel,
+        grid=(1,),
+        out_shape=jax.ShapeDtypeStruct((2, 4 * part, width), BF16),
+        in_specs=[SCALAR] + [whole(2, part, width)] * 4 + [ANY] * len(after),
+        out_specs=whole(2, 4 * part, width),
+        compiler_params=params(SMALL_BYTES),
+        cost_estimate=cost(0, 16 * own.size),
+        name="join_line",
+    )(rank, own, *others, *after)
+
+
 class Chunk:
-    def __init__(self, rank, mp, keep, send):
+    def __init__(self, rank, mp, keep, send, direct):
         self.rank, self.mp, self.levels = rank, mp, mp.bit_length() - 1
         self.keep, self.send, self.done = keep, send, 0
+        self.direct = direct
 
     def advance(self, after=()):
         index, self.done = self.done, self.done + 1
         level = min(index, 2 * self.levels - 1 - index)
+        if self.direct and index >= self.levels and level == 2:
+            others = [exchange(self.send, "mp", self.mp, step) for step in (2, 4, 6)]
+            self.done += 1
+            self.send = join_line(self.rank, self.send, others, after)
+            return self.send
         received = exchange(self.send, "mp", self.mp, partner_step(level))
         if index < self.levels - 1:
             self.keep, self.send = halve(
@@ -351,12 +390,12 @@
         if chunks:
             after = [relay(send, after)]
             send = after[0]
-        chunks.append(Chunk(rank, mp, keep, send))
+        chunks.append(Chunk(rank, mp, keep, send, start == starts[-1]))
 
     steps = 2 * chunks[0].levels
     partial = None
-    while chunks[-1].done < steps:
-        for chunk in chunks[::-1]:
+    while any(chunk.done < steps for chunk in chunks):
+        for chunk in chunks if chunks[0].done >= steps - 1 else chunks[::-1]:
             if chunk.done < steps:
                 after = [chunk.advance(after)]
                 if chunk.done == steps:

time: 94.1 us -> 94.1 us (level)
  waiting for transfers between devices: 28.6 us -> 26.9 us
  starting transfers between devices: 30.3 us -> 32 us
    ppermute x24 -> x25, starting transfers between devices: 30.3 us -> 32 us  [exchange(): return lax.ppermute(array, axis, [(i, i ^ step) for i in range(size)])]
    ppermute x24 -> x25, waiting for transfers between devices: 28.6 us -> 26.9 us  [exchange(): return lax.ppermute(array, axis, [(i, i ^ step) for i in range(size)])]
  transfers between devices with their start and end apart: 24 -> 25, of which waited for: 11 -> 10; matrix products, arithmetic and copies ran while one was open for 0% -> 0% of each run, Pallas kernels for 29% -> 29%
where the time goes in v7:
time: 94.1 us; the launch traced here: 94 us
  starting transfers between devices  32 us (34%)
  Pallas kernels  31.9 us (34%)
  waiting for transfers between devices  26.9 us (29%)
  other arithmetic  1.73 us (2%)
  between operations  1.01 us (1%)
    ppermute x25, starting transfers between devices, exchange(): return lax.ppermute(array, axis, [(i, i ^ step) for i in range(size)])  32 us
    ppermute x25, waiting for transfers between devices, exchange(): return lax.ppermute(array, axis, [(i, i ^ step) for i in range(size)])  26.9 us
    pallas_call x1, Pallas kernels, weight_grads(): pl.pallas_call(kernel, grid=(2 * len(finals),), out_shape=(jax.ShapeDtype...  10.6 us
    pallas_call x3, Pallas kernels, forward(): pl.pallas_call(kernel, grid=(1,), out_shape=(jax.ShapeDtypeStruct((2, hal...  8.59 us
    pallas_call x1, Pallas kernels, load(): pl.pallas_call(kernel, out_shape=tuple((jax.ShapeDtypeStruct(w.shape, w.d...  7.72 us
    pallas_call x3, Pallas kernels, input_grads(): pl.pallas_call(kernel, grid=(1,), out_shape=jax.ShapeDtypeStruct((total,...  3.86 us
  transfers between devices with their start and end apart: 25, of which 10 were waited for; matrix products, arithmetic and copies ran while one was open for 0% of the time, Pallas kernels for 29%

profile of v7, /device:TPU:0, one launch (start us, length us, event | category | flops | bytes accessed | tf_op | source)
XLA Modules:
  0.0 94.0 jit_solution(18324817568999927580)
XLA Ops:
  0.6 0.9 %pad_maximum_fusion.1.refs_0_ = bf16[2,32,1280]{2,1,0:T(8,128)(2,1)S(1)} fusion(bf16[1,32,1280]{2,1,0:T(8,128)(2,1)} %bitcast.8, bf16[1,32,1280]{2,1,0:T(8,128)(2,1)} %bitcast.10), kind=kLoop, calls=%fused_computation.7 | loop fusion | flops 81920 | bytes 327680 | tf_op jit(solution)/shard_map/stack | solution.py:379
  1.6 3.0 %collective-permute-start = (bf16[2,32,1280]{2,1,0:T(8,128)(2,1)S(1)}, bf16[2,32,1280]{2,1,0:T(8,128)(2,1)S(1)}, u32[]{:S(2)}, u32[]{:S(2)}) collective-permute-start(bf16[2,32,1280]{2,1,0:T(8,128)(2,1)S(1)} %pad_maximum_fusion.1.refs_0_), channel_id=1, source_target_pairs={{0,8},{8,0},{16,24},{24,16},{1,9},{9,1},{17,25},{25,17},{2,10},{10... | collective-permute-start | bytes 491528 | tf_op jit(solution)/shard_map/ppermute | solution.py:40
  4.6 1.5 %collective-permute-start.1 = (bf16[2,32,1280]{2,1,0:T(8,128)(2,1)S(1)}, bf16[2,32,1280]{2,1,0:T(8,128)(2,1)S(1)}, u32[]{:S(2)}, u32[]{:S(2)}) collective-permute-start(bf16[2,32,1280]{2,1,0:T(8,128)(2,1)S(1)} %pad_maximum_fusion.1.refs_0_), channel_id=1, source_target_pairs={{0,16},{8,24},{16,0},{24,8},{1,17},{9,25},{17,1},{25,9},{2,18},{10... | collective-permute-start | bytes 491528 | tf_op jit(solution)/shard_map/ppermute | solution.py:40
  6.1 7.7 %load.1 = (bf16[1280,4608]{1,0:T(8,128)(2,1)S(1)}, bf16[4608,1280]{1,0:T(8,128)(2,1)S(1)}) custom-call(bf16[1280,4608]{1,0:T(8,128)(2,1)} %refs_0_.1, bf16[4608,1280]{1,0:T(8,128)(2,1)} %refs_1_.1), custom_call_target="tpu_custom_call" | custom-call | bytes 47185920 | tf_op jit(solution)/shard_map/load/pallas_call | solution.py:84
  13.9 2.9 %forward.3 = (f32[2,64,1536]{2,1,0:T(8,128)S(1)}, bf16[2,64,1536]{2,1,0:T(8,128)(2,1)S(1)}) custom-call(s32[1]{0:T(128)} %bitcast.rank_ref, bf16[2,32,1280]{2,1,0:T(8,128)(2,1)S(1)} %pad_maximum_fusion.1.refs_0_, bf16[2,32,1280]{2,1,0:T(8,128)(2,1)S(1)} %collective-permute-done.refs_1_, bf16[2,32,1280]{2,1,0:T(8,128)(2,1)S(1)} %collective-permute-done.1.refs_2_, ...), custom_call_target="tpu_custom_call" | custom-call | flops 1006632960 | bytes 7864320 | tf_op jit(solution)/shard_map/forward/pallas_call | solution.py:129
  16.8 0.1 collective-permute-start.3
  16.8 2.9 %forward.4 = (f32[2,64,1536]{2,1,0:T(8,128)S(1)}, bf16[2,64,1536]{2,1,0:T(8,128)(2,1)S(1)}) custom-call(s32[1]{0:T(128)} %bitcast.rank_ref, bf16[2,32,1280]{2,1,0:T(8,128)(2,1)S(1)} %pad_maximum_fusion.1.refs_0_, bf16[2,32,1280]{2,1,0:T(8,128)(2,1)S(1)} %collective-permute-done.refs_1_, bf16[2,32,1280]{2,1,0:T(8,128)(2,1)S(1)} %collective-permute-done.1.refs_2_, ...), custom_call_target="tpu_custom_call" | custom-call | flops 1006632960 | bytes 7864320 | tf_op jit(solution)/shard_map/forward/pallas_call | solution.py:129
  19.7 0.1 halve.6
  19.9 0.6 collective-permute-start.5
  20.5 2.0 %collective-permute-start.4 = (bf16[2,32,1536]{2,1,0:T(8,128)(2,1)S(1)}, bf16[2,32,1536]{2,1,0:T(8,128)(2,1)S(1)}, u32[]{:S(2)}, u32[]{:S(2)}) collective-permute-start(bf16[2,32,1536]{2,1,0:T(8,128)(2,1)S(1)} %get-tuple-element.30.rest_0_), channel_id=1, source_target_pairs={{0,2},{1,3},{2,0},{3,1},{4,6},{5,7},{6,4},{7,5},{8,10},{9,11},{10,... | collective-permute-start | bytes 589832 | tf_op jit(solution)/shard_map/ppermute | solution.py:40
  22.5 2.9 %forward.5 = (f32[2,64,1536]{2,1,0:T(8,128)S(1)}, bf16[2,64,1536]{2,1,0:T(8,128)(2,1)S(1)}) custom-call(s32[1]{0:T(128)} %bitcast.rank_ref, bf16[2,32,1280]{2,1,0:T(8,128)(2,1)S(1)} %pad_maximum_fusion.1.refs_0_, bf16[2,32,1280]{2,1,0:T(8,128)(2,1)S(1)} %collective-permute-done.refs_1_, bf16[2,32,1280]{2,1,0:T(8,128)(2,1)S(1)} %collective-permute-done.1.refs_2_, ...), custom_call_target="tpu_custom_call" | custom-call | flops 1006632960 | bytes 7864320 | tf_op jit(solution)/shard_map/forward/pallas_call | solution.py:129
  25.4 0.1 halve.7
  25.5 2.2 %collective-permute-done.4.received_ref = bf16[2,32,1536]{2,1,0:T(8,128)(2,1)S(1)} collective-permute-done((bf16[2,32,1536]{2,1,0:T(8,128)(2,1)S(1)}, bf16[2,32,1536]{2,1,0:T(8,128)(2,1)S(1)}, u32[]{:S(2)}, u32[]{:S(2)}) %collective-permute-start.4) | collective-permute-done | bytes 196640 | tf_op jit(solution)/shard_map/ppermute | solution.py:40
  27.7 0.1 collective-permute-start.6
  27.8 1.8 %collective-permute-start.9 = (bf16[2,32,1536]{2,1,0:T(8,128)(2,1)S(1)}, bf16[2,32,1536]{2,1,0:T(8,128)(2,1)S(1)}, u32[]{:S(2)}, u32[]{:S(2)}) collective-permute-start(bf16[2,32,1536]{2,1,0:T(8,128)(2,1)S(1)} %get-tuple-element.35.rest_0_), channel_id=1, source_target_pairs={{0,2},{1,3},{2,0},{3,1},{4,6},{5,7},{6,4},{7,5},{8,10},{9,11},{10,... | collective-permute-start | bytes 589832 | tf_op jit(solution)/shard_map/ppermute | solution.py:40
  29.7 1.7 %collective-permute-start.7 = (bf16[2,32,1536]{2,1,0:T(8,128)(2,1)S(1)}, bf16[2,32,1536]{2,1,0:T(8,128)(2,1)S(1)}, u32[]{:S(2)}, u32[]{:S(2)}) collective-permute-start(bf16[2,32,1536]{2,1,0:T(8,128)(2,1)S(1)} %get-tuple-element.38.rest_0_), channel_id=1, source_target_pairs={{0,2},{1,3},{2,0},{3,1},{4,6},{5,7},{6,4},{7,5},{8,10},{9,11},{10,... | collective-permute-start | bytes 589832 | tf_op jit(solution)/shard_map/ppermute | solution.py:40
  31.4 2.5 %collective-permute-start.8 = (bf16[2,16,1536]{2,1,0:T(8,128)(2,1)S(1)}, bf16[2,16,1536]{2,1,0:T(8,128)(2,1)S(1)}, u32[]{:S(2)}, u32[]{:S(2)}) collective-permute-start(bf16[2,16,1536]{2,1,0:T(8,128)(2,1)S(1)} %get-tuple-element.36.rest_0_), channel_id=1, source_target_pairs={{0,6},{1,7},{2,4},{3,5},{4,2},{5,3},{6,0},{7,1},{8,14},{9,15},{10,... | collective-permute-start | bytes 294920 | tf_op jit(solution)/shard_map/ppermute | solution.py:40
  33.9 1.7 %collective-permute-done.9.received_ref = bf16[2,32,1536]{2,1,0:T(8,128)(2,1)S(1)} collective-permute-done((bf16[2,32,1536]{2,1,0:T(8,128)(2,1)S(1)}, bf16[2,32,1536]{2,1,0:T(8,128)(2,1)S(1)}, u32[]{:S(2)}, u32[]{:S(2)}) %collective-permute-start.9) | collective-permute-done | bytes 196640 | tf_op jit(solution)/shard_map/ppermute | solution.py:40
  35.6 3.8 %collective-permute-start.12 = (bf16[2,16,1536]{2,1,0:T(8,128)(2,1)S(1)}, bf16[2,16,1536]{2,1,0:T(8,128)(2,1)S(1)}, u32[]{:S(2)}, u32[]{:S(2)}) collective-permute-start(bf16[2,16,1536]{2,1,0:T(8,128)(2,1)S(1)} %get-tuple-element.41.rest_0_), channel_id=1, source_target_pairs={{0,6},{1,7},{2,4},{3,5},{4,2},{5,3},{6,0},{7,1},{8,14},{9,15},{10,... | collective-permute-start | bytes 294920 | tf_op jit(solution)/shard_map/ppermute | solution.py:40
  39.5 4.7 %collective-permute-done.8.received_ref = bf16[2,16,1536]{2,1,0:T(8,128)(2,1)S(1)} collective-permute-done((bf16[2,16,1536]{2,1,0:T(8,128)(2,1)S(1)}, bf16[2,16,1536]{2,1,0:T(8,128)(2,1)S(1)}, u32[]{:S(2)}, u32[]{:S(2)}) %collective-permute-start.8) | collective-permute-done | bytes 98336 | tf_op jit(solution)/shard_map/ppermute | solution.py:40
  44.2 0.1 activate.3.rest_0_.own_ref
  44.3 1.5 %collective-permute-start.11 = (bf16[2,16,1536]{2,1,0:T(8,128)(2,1)S(1)}, bf16[2,16,1536]{2,1,0:T(8,128)(2,1)S(1)}, u32[]{:S(2)}, u32[]{:S(2)}) collective-permute-start(bf16[2,16,1536]{2,1,0:T(8,128)(2,1)S(1)} %activate.3.rest_0_.own_ref), channel_id=1, source_target_pairs={{0,6},{1,7},{2,4},{3,5},{4,2},{5,3},{6,0},{7,1},{8,14},{9,15},{10,... | collective-permute-start | bytes 294920 | tf_op jit(solution)/shard_map/ppermute | solution.py:40
  46.0 4.8 %collective-permute-done.11.received_ref = bf16[2,16,1536]{2,1,0:T(8,128)(2,1)S(1)} collective-permute-done((bf16[2,16,1536]{2,1,0:T(8,128)(2,1)S(1)}, bf16[2,16,1536]{2,1,0:T(8,128)(2,1)S(1)}, u32[]{:S(2)}, u32[]{:S(2)}) %collective-permute-start.11) | collective-permute-done | bytes 98336 | tf_op jit(solution)/shard_map/ppermute | solution.py:40
  50.8 0.1 collective-permute-start.18
  50.9 1.5 %collective-permute-start.10 = (bf16[2,16,1536]{2,1,0:T(8,128)(2,1)S(1)}, bf16[2,16,1536]{2,1,0:T(8,128)(2,1)S(1)}, u32[]{:S(2)}, u32[]{:S(2)}) collective-permute-start(bf16[2,16,1536]{2,1,0:T(8,128)(2,1)S(1)} %get-tuple-element.43.rest_0_), channel_id=1, source_target_pairs={{0,6},{1,7},{2,4},{3,5},{4,2},{5,3},{6,0},{7,1},{8,14},{9,15},{10,... | collective-permute-start | bytes 294920 | tf_op jit(solution)/shard_map/ppermute | solution.py:40
  52.3 2.4 %collective-permute-start.16 = (bf16[2,16,1536]{2,1,0:T(8,128)(2,1)S(1)}, bf16[2,16,1536]{2,1,0:T(8,128)(2,1)S(1)}, u32[]{:S(2)}, u32[]{:S(2)}) collective-permute-start(bf16[2,16,1536]{2,1,0:T(8,128)(2,1)S(1)} %activate.4.rest_0_.own_ref), channel_id=1, source_target_pairs={{0,6},{1,7},{2,4},{3,5},{4,2},{5,3},{6,0},{7,1},{8,14},{9,15},{10,... | collective-permute-start | bytes 294920 | tf_op jit(solution)/shard_map/ppermute | solution.py:40
  54.7 3.9 %collective-permute-done.10.received_ref = bf16[2,16,1536]{2,1,0:T(8,128)(2,1)S(1)} collective-permute-done((bf16[2,16,1536]{2,1,0:T(8,128)(2,1)S(1)}, bf16[2,16,1536]{2,1,0:T(8,128)(2,1)S(1)}, u32[]{:S(2)}, u32[]{:S(2)}) %collective-permute-start.10) | collective-permute-done | bytes 98336 | tf_op jit(solution)/shard_map/ppermute | solution.py:40
  58.7 0.1 activate.5.rest_0_.own_ref
  58.8 1.0 %collective-permute-done.16.received_ref = bf16[2,16,1536]{2,1,0:T(8,128)(2,1)S(1)} collective-permute-done((bf16[2,16,1536]{2,1,0:T(8,128)(2,1)S(1)}, bf16[2,16,1536]{2,1,0:T(8,128)(2,1)S(1)}, u32[]{:S(2)}, u32[]{:S(2)}) %collective-permute-start.16) | collective-permute-done | bytes 98336 | tf_op jit(solution)/shard_map/ppermute | solution.py:40
  59.8 0.2 collective-permute-done.18.received_ref
  60.1 1.7 %collective-permute-start.13 = (bf16[2,16,1536]{2,1,0:T(8,128)(2,1)S(1)}, bf16[2,16,1536]{2,1,0:T(8,128)(2,1)S(1)}, u32[]{:S(2)}, u32[]{:S(2)}) collective-permute-start(bf16[2,16,1536]{2,1,0:T(8,128)(2,1)S(1)} %activate.5.rest_0_.own_ref), channel_id=1, source_target_pairs={{0,2},{1,3},{2,0},{3,1},{4,6},{5,7},{6,4},{7,5},{8,10},{9,11},{10,... | collective-permute-start | bytes 294920 | tf_op jit(solution)/shard_map/ppermute | solution.py:40
  61.8 1.0 %collective-permute-start.14 = (bf16[2,16,1536]{2,1,0:T(8,128)(2,1)S(1)}, bf16[2,16,1536]{2,1,0:T(8,128)(2,1)S(1)}, u32[]{:S(2)}, u32[]{:S(2)}) collective-permute-start(bf16[2,16,1536]{2,1,0:T(8,128)(2,1)S(1)} %activate.5.rest_0_.own_ref), channel_id=1, source_target_pairs={{0,4},{1,5},{2,6},{3,7},{4,0},{5,1},{6,2},{7,3},{8,12},{9,13},{10,... | collective-permute-start | bytes 294920 | tf_op jit(solution)/shard_map/ppermute | solution.py:40
  62.8 1.7 %collective-permute-start.15 = (bf16[2,16,1536]{2,1,0:T(8,128)(2,1)S(1)}, bf16[2,16,1536]{2,1,0:T(8,128)(2,1)S(1)}, u32[]{:S(2)}, u32[]{:S(2)}) collective-permute-start(bf16[2,16,1536]{2,1,0:T(8,128)(2,1)S(1)} %activate.5.rest_0_.own_ref), channel_id=1, source_target_pairs={{0,6},{1,7},{2,4},{3,5},{4,2},{5,3},{6,0},{7,1},{8,14},{9,15},{10,... | collective-permute-start | bytes 294920 | tf_op jit(solution)/shard_map/ppermute | solution.py:40
  64.6 0.8 collective-permute-start.17
  65.5 1.3 %input_grads.3.rest_0_.refs_0_ = f32[128,1280]{1,0:T(8,128)S(1)} custom-call(bf16[2,128,1536]{2,1,0:T(8,128)(2,1)S(1)} %join.10.grad_ref.refs_0_, bf16[1280,4608]{1,0:T(8,128)(2,1)S(1)} %get-tuple-element.25.refs_4_.wi_ref), custom_call_target="tpu_custom_call" | custom-call | flops 503316480 | bytes 3932160 | tf_op jit(solution)/shard_map/input_grads/pallas_call | solution.py:314
  66.8 7.5 %collective-permute-done.17.received_ref = bf16[2,32,1536]{2,1,0:T(8,128)(2,1)S(1)} collective-permute-done((bf16[2,32,1536]{2,1,0:T(8,128)(2,1)S(1)}, bf16[2,32,1536]{2,1,0:T(8,128)(2,1)S(1)}, u32[]{:S(2)}, u32[]{:S(2)}) %collective-permute-start.17) | collective-permute-done | bytes 196640 | tf_op jit(solution)/shard_map/ppermute | solution.py:40
  74.3 0.1 collective-permute-start.21
  74.5 0.5 collective-permute-start.20
  75.0 0.3 convolution_convert_fusion.xt_ref
  75.3 0.8 collective-permute-done.21.received_ref
  76.1 1.3 %input_grads.4.rest_0_.refs_0_ = f32[128,1280]{1,0:T(8,128)S(1)} custom-call(bf16[2,128,1536]{2,1,0:T(8,128)(2,1)S(1)} %join.12.grad_ref.refs_1_, bf16[1280,4608]{1,0:T(8,128)(2,1)S(1)} %get-tuple-element.25.refs_4_.wi_ref, f32[128,1280]{1,0:T(8,128)S(1)} %input_grads.3.rest_0_.refs_0_), custom_call_target="tpu_custom_call" | custom-call | flops 503316480 | bytes 3932160 | tf_op jit(solution)/shard_map/input_grads/pallas_call | solution.py:314
  77.4 0.2 join.13.grad_ref.refs_2_
  77.7 1.3 %input_grads.5 = f32[128,1280]{1,0:T(8,128)S(1)} custom-call(bf16[2,128,1536]{2,1,0:T(8,128)(2,1)S(1)} %join.13.grad_ref.refs_2_, bf16[1280,4608]{1,0:T(8,128)(2,1)S(1)} %get-tuple-element.25.refs_4_.wi_ref, f32[128,1280]{1,0:T(8,128)S(1)} %input_grads.4.rest_0_.refs_0_), custom_call_target="tpu_custom_call" | custom-call | flops 503316480 | bytes 3932160 | tf_op jit(solution)/shard_map/input_grads/pallas_call | solution.py:314
  79.0 2.5 %collective-permute-start.24 = (bf16[32,1280]{1,0:T(8,128)(2,1)S(1)}, bf16[32,1280]{1,0:T(8,128)(2,1)S(1)}, u32[]{:S(2)}, u32[]{:S(2)}) collective-permute-start(bf16[32,1280]{1,0:T(8,128)(2,1)S(1)} %get-tuple-element.48), channel_id=1, source_target_pairs={{0,24},{8,16},{16,8},{24,0},{1,25},{9,17},{17,9},{25,1},{2,26},{10... | collective-permute-start | bytes 245768 | tf_op jit(solution)/shard_map/ppermute | solution.py:40
  81.6 0.5 collective-permute-start.23
  82.1 0.5 collective-permute-start.22
  82.6 10.6 %weight_grads.1 = (bf16[1280,4608]{1,0:T(8,128)(2,1)}, bf16[4608,1280]{1,0:T(8,128)(2,1)}) custom-call(bf16[1280,128]{1,0:T(8,128)(2,1)S(1)} %convolution_convert_fusion.xt_ref, bf16[128,1280]{1,0:T(8,128)(2,1)S(1)} %slice_bitcast_fusion.gs_ref, bf16[2,128,1536]{2,1,0:T(8,128)(2,1)S(1)} %join.10.grad_ref.refs_0_, ...), custom_call_target="tpu_custom_call" | custom-call | flops 3019898880 | bytes 23592960 | tf_op jit(solution)/shard_map/weight_grads/pallas_call | solution.py:351
  93.3 0.7 fusion.1
  (40 shorter events, 0.9 us)
Async XLA Ops:
  1.6 12.3 %collective-permute-start = (bf16[2,32,1280]{2,1,0:T(8,128)(2,1)S(1)}, bf16[2,32,1280]{2,1,0:T(8,128)(2,1)S(1)}, u32[]{:S(2)}, u32[]{:S(2)}) collective-permute-start(bf16[2,32,1280]{2,1,0:T(8,128)(2,1)S(1)} %pad_maximum_fusion.1.refs_0_), channel_id=1, source_target_pairs={{0,8},{8,0},{16,24},{24,16},{1,9},{9,1},{17,25},{25,17},{2,10},{10... | collective-permute-start | bytes 491528 | tf_op jit(solution)/shard_map/ppermute | solution.py:40
  4.6 9.3 %collective-permute-start.1 = (bf16[2,32,1280]{2,1,0:T(8,128)(2,1)S(1)}, bf16[2,32,1280]{2,1,0:T(8,128)(2,1)S(1)}, u32[]{:S(2)}, u32[]{:S(2)}) collective-permute-start(bf16[2,32,1280]{2,1,0:T(8,128)(2,1)S(1)} %pad_maximum_fusion.1.refs_0_), channel_id=1, source_target_pairs={{0,16},{8,24},{16,0},{24,8},{1,17},{9,25},{17,1},{25,9},{2,18},{10... | collective-permute-start | bytes 491528 | tf_op jit(solution)/shard_map/ppermute | solution.py:40
  6.1 7.8 %collective-permute-start.2 = (bf16[2,32,1280]{2,1,0:T(8,128)(2,1)S(1)}, bf16[2,32,1280]{2,1,0:T(8,128)(2,1)S(1)}, u32[]{:S(2)}, u32[]{:S(2)}) collective-permute-start(bf16[2,32,1280]{2,1,0:T(8,128)(2,1)S(1)} %pad_maximum_fusion.1.refs_0_), channel_id=1, source_target_pairs={{0,24},{8,16},{16,8},{24,0},{1,25},{9,17},{17,9},{25,1},{2,26},{10... | collective-permute-start | bytes 491528 | tf_op jit(solution)/shard_map/ppermute | solution.py:40
  16.8 3.0 %collective-permute-start.3 = (bf16[2,64,1536]{2,1,0:T(8,128)(2,1)S(1)}, bf16[2,64,1536]{2,1,0:T(8,128)(2,1)S(1)}, u32[]{:S(2)}, u32[]{:S(2)}) collective-permute-start(bf16[2,64,1536]{2,1,0:T(8,128)(2,1)S(1)} %get-tuple-element.27.refs_6_), channel_id=1, source_target_pairs={{0,1},{1,0},{2,3},{3,2},{4,5},{5,4},{6,7},{7,6},{8,9},{9,8},{10,11... | collective-permute-start | bytes 1179656 | tf_op jit(solution)/shard_map/ppermute | solution.py:40
  19.9 5.5 %collective-permute-start.5 = (bf16[2,64,1536]{2,1,0:T(8,128)(2,1)S(1)}, bf16[2,64,1536]{2,1,0:T(8,128)(2,1)S(1)}, u32[]{:S(2)}, u32[]{:S(2)}) collective-permute-start(bf16[2,64,1536]{2,1,0:T(8,128)(2,1)S(1)} %relay.2.refs_6_), channel_id=1, source_target_pairs={{0,1},{1,0},{2,3},{3,2},{4,5},{5,4},{6,7},{7,6},{8,9},{9,8},{10,11... | collective-permute-start | bytes 1179656 | tf_op jit(solution)/shard_map/ppermute | solution.py:40
  20.5 7.2 %collective-permute-start.4 = (bf16[2,32,1536]{2,1,0:T(8,128)(2,1)S(1)}, bf16[2,32,1536]{2,1,0:T(8,128)(2,1)S(1)}, u32[]{:S(2)}, u32[]{:S(2)}) collective-permute-start(bf16[2,32,1536]{2,1,0:T(8,128)(2,1)S(1)} %get-tuple-element.30.rest_0_), channel_id=1, source_target_pairs={{0,2},{1,3},{2,0},{3,1},{4,6},{5,7},{6,4},{7,5},{8,10},{9,11},{10,... | collective-permute-start | bytes 589832 | tf_op jit(solution)/shard_map/ppermute | solution.py:40
  27.7 1.9 %collective-permute-start.6 = (bf16[2,64,1536]{2,1,0:T(8,128)(2,1)S(1)}, bf16[2,64,1536]{2,1,0:T(8,128)(2,1)S(1)}, u32[]{:S(2)}, u32[]{:S(2)}) collective-permute-start(bf16[2,64,1536]{2,1,0:T(8,128)(2,1)S(1)} %relay.3.rest_0_), channel_id=1, source_target_pairs={{0,1},{1,0},{2,3},{3,2},{4,5},{5,4},{6,7},{7,6},{8,9},{9,8},{10,11... | collective-permute-start | bytes 1179656 | tf_op jit(solution)/shard_map/ppermute | solution.py:40
  27.8 7.8 %collective-permute-start.9 = (bf16[2,32,1536]{2,1,0:T(8,128)(2,1)S(1)}, bf16[2,32,1536]{2,1,0:T(8,128)(2,1)S(1)}, u32[]{:S(2)}, u32[]{:S(2)}) collective-permute-start(bf16[2,32,1536]{2,1,0:T(8,128)(2,1)S(1)} %get-tuple-element.35.rest_0_), channel_id=1, source_target_pairs={{0,2},{1,3},{2,0},{3,1},{4,6},{5,7},{6,4},{7,5},{8,10},{9,11},{10,... | collective-permute-start | bytes 589832 | tf_op jit(solution)/shard_map/ppermute | solution.py:40
  29.7 16.0 %collective-permute-start.7 = (bf16[2,32,1536]{2,1,0:T(8,128)(2,1)S(1)}, bf16[2,32,1536]{2,1,0:T(8,128)(2,1)S(1)}, u32[]{:S(2)}, u32[]{:S(2)}) collective-permute-start(bf16[2,32,1536]{2,1,0:T(8,128)(2,1)S(1)} %get-tuple-element.38.rest_0_), channel_id=1, source_target_pairs={{0,2},{1,3},{2,0},{3,1},{4,6},{5,7},{6,4},{7,5},{8,10},{9,11},{10,... | collective-permute-start | bytes 589832 | tf_op jit(solution)/shard_map/ppermute | solution.py:40
  31.4 12.8 %collective-permute-start.8 = (bf16[2,16,1536]{2,1,0:T(8,128)(2,1)S(1)}, bf16[2,16,1536]{2,1,0:T(8,128)(2,1)S(1)}, u32[]{:S(2)}, u32[]{:S(2)}) collective-permute-start(bf16[2,16,1536]{2,1,0:T(8,128)(2,1)S(1)} %get-tuple-element.36.rest_0_), channel_id=1, source_target_pairs={{0,6},{1,7},{2,4},{3,5},{4,2},{5,3},{6,0},{7,1},{8,14},{9,15},{10,... | collective-permute-start | bytes 294920 | tf_op jit(solution)/shard_map/ppermute | solution.py:40
  35.6 10.2 %collective-permute-start.12 = (bf16[2,16,1536]{2,1,0:T(8,128)(2,1)S(1)}, bf16[2,16,1536]{2,1,0:T(8,128)(2,1)S(1)}, u32[]{:S(2)}, u32[]{:S(2)}) collective-permute-start(bf16[2,16,1536]{2,1,0:T(8,128)(2,1)S(1)} %get-tuple-element.41.rest_0_), channel_id=1, source_target_pairs={{0,6},{1,7},{2,4},{3,5},{4,2},{5,3},{6,0},{7,1},{8,14},{9,15},{10,... | collective-permute-start | bytes 294920 | tf_op jit(solution)/shard_map/ppermute | solution.py:40
  44.3 6.5 %collective-permute-start.11 = (bf16[2,16,1536]{2,1,0:T(8,128)(2,1)S(1)}, bf16[2,16,1536]{2,1,0:T(8,128)(2,1)S(1)}, u32[]{:S(2)}, u32[]{:S(2)}) collective-permute-start(bf16[2,16,1536]{2,1,0:T(8,128)(2,1)S(1)} %activate.3.rest_0_.own_ref), channel_id=1, source_target_pairs={{0,6},{1,7},{2,4},{3,5},{4,2},{5,3},{6,0},{7,1},{8,14},{9,15},{10,... | collective-permute-start | bytes 294920 | tf_op jit(solution)/shard_map/ppermute | solution.py:40
  45.9 19.4 %copy-start = (bf16[32,1280]{1,0:T(8,128)(2,1)S(1)}, bf16[32,1280]{1,0:T(8,128)(2,1)}, u32[]{:S(2)}) copy-start(bf16[32,1280]{1,0:T(8,128)(2,1)} %param.5) | copy-start | bytes 245764
  45.9 19.4 %copy-start.1 = (bf16[32,1280]{1,0:T(8,128)(2,1)S(1)}, bf16[32,1280]{1,0:T(8,128)(2,1)}, u32[]{:S(2)}) copy-start(bf16[32,1280]{1,0:T(8,128)(2,1)} %param.4) | copy-start | bytes 245764
  50.8 9.2 %collective-permute-start.18 = (bf16[2,32,1536]{2,1,0:T(8,128)(2,1)S(1)}, bf16[2,32,1536]{2,1,0:T(8,128)(2,1)S(1)}, u32[]{:S(2)}, u32[]{:S(2)}) collective-permute-start(bf16[2,32,1536]{2,1,0:T(8,128)(2,1)S(1)} %join.7.rest_0_.own_ref), channel_id=1, source_target_pairs={{0,2},{1,3},{2,0},{3,1},{4,6},{5,7},{6,4},{7,5},{8,10},{9,11},{10,... | collective-permute-start | bytes 589832 | tf_op jit(solution)/shard_map/ppermute | solution.py:40
  50.9 7.8 %collective-permute-start.10 = (bf16[2,16,1536]{2,1,0:T(8,128)(2,1)S(1)}, bf16[2,16,1536]{2,1,0:T(8,128)(2,1)S(1)}, u32[]{:S(2)}, u32[]{:S(2)}) collective-permute-start(bf16[2,16,1536]{2,1,0:T(8,128)(2,1)S(1)} %get-tuple-element.43.rest_0_), channel_id=1, source_target_pairs={{0,6},{1,7},{2,4},{3,5},{4,2},{5,3},{6,0},{7,1},{8,14},{9,15},{10,... | collective-permute-start | bytes 294920 | tf_op jit(solution)/shard_map/ppermute | solution.py:40
  52.3 7.4 %collective-permute-start.16 = (bf16[2,16,1536]{2,1,0:T(8,128)(2,1)S(1)}, bf16[2,16,1536]{2,1,0:T(8,128)(2,1)S(1)}, u32[]{:S(2)}, u32[]{:S(2)}) collective-permute-start(bf16[2,16,1536]{2,1,0:T(8,128)(2,1)S(1)} %activate.4.rest_0_.own_ref), channel_id=1, source_target_pairs={{0,6},{1,7},{2,4},{3,5},{4,2},{5,3},{6,0},{7,1},{8,14},{9,15},{10,... | collective-permute-start | bytes 294920 | tf_op jit(solution)/shard_map/ppermute | solution.py:40
  60.0 5.4 %collective-permute-start.19 = (bf16[2,64,1536]{2,1,0:T(8,128)(2,1)S(1)}, bf16[2,64,1536]{2,1,0:T(8,128)(2,1)S(1)}, u32[]{:S(2)}, u32[]{:S(2)}) collective-permute-start(bf16[2,64,1536]{2,1,0:T(8,128)(2,1)S(1)} %join.9.own_ref.rest_0_), channel_id=1, source_target_pairs={{0,1},{1,0},{2,3},{3,2},{4,5},{5,4},{6,7},{7,6},{8,9},{9,8},{10,11... | collective-permute-start | bytes 1179656 | tf_op jit(solution)/shard_map/ppermute | solution.py:40
  60.1 14.3 %collective-permute-start.13 = (bf16[2,16,1536]{2,1,0:T(8,128)(2,1)S(1)}, bf16[2,16,1536]{2,1,0:T(8,128)(2,1)S(1)}, u32[]{:S(2)}, u32[]{:S(2)}) collective-permute-start(bf16[2,16,1536]{2,1,0:T(8,128)(2,1)S(1)} %activate.5.rest_0_.own_ref), channel_id=1, source_target_pairs={{0,2},{1,3},{2,0},{3,1},{4,6},{5,7},{6,4},{7,5},{8,10},{9,11},{10,... | collective-permute-start | bytes 294920 | tf_op jit(solution)/shard_map/ppermute | solution.py:40
  61.8 12.5 %collective-permute-start.14 = (bf16[2,16,1536]{2,1,0:T(8,128)(2,1)S(1)}, bf16[2,16,1536]{2,1,0:T(8,128)(2,1)S(1)}, u32[]{:S(2)}, u32[]{:S(2)}) collective-permute-start(bf16[2,16,1536]{2,1,0:T(8,128)(2,1)S(1)} %activate.5.rest_0_.own_ref), channel_id=1, source_target_pairs={{0,4},{1,5},{2,6},{3,7},{4,0},{5,1},{6,2},{7,3},{8,12},{9,13},{10,... | collective-permute-start | bytes 294920 | tf_op jit(solution)/shard_map/ppermute | solution.py:40
  62.8 11.5 %collective-permute-start.15 = (bf16[2,16,1536]{2,1,0:T(8,128)(2,1)S(1)}, bf16[2,16,1536]{2,1,0:T(8,128)(2,1)S(1)}, u32[]{:S(2)}, u32[]{:S(2)}) collective-permute-start(bf16[2,16,1536]{2,1,0:T(8,128)(2,1)S(1)} %activate.5.rest_0_.own_ref), channel_id=1, source_target_pairs={{0,6},{1,7},{2,4},{3,5},{4,2},{5,3},{6,0},{7,1},{8,14},{9,15},{10,... | collective-permute-start | bytes 294920 | tf_op jit(solution)/shard_map/ppermute | solution.py:40
  64.6 9.7 %collective-permute-start.17 = (bf16[2,32,1536]{2,1,0:T(8,128)(2,1)S(1)}, bf16[2,32,1536]{2,1,0:T(8,128)(2,1)S(1)}, u32[]{:S(2)}, u32[]{:S(2)}) collective-permute-start(bf16[2,32,1536]{2,1,0:T(8,128)(2,1)S(1)} %join.8.rest_0_.own_ref), channel_id=1, source_target_pairs={{0,2},{1,3},{2,0},{3,1},{4,6},{5,7},{6,4},{7,5},{8,10},{9,11},{10,... | collective-permute-start | bytes 589832 | tf_op jit(solution)/shard_map/ppermute | solution.py:40
  74.3 1.8 %collective-permute-start.21 = (bf16[2,64,1536]{2,1,0:T(8,128)(2,1)S(1)}, bf16[2,64,1536]{2,1,0:T(8,128)(2,1)S(1)}, u32[]{:S(2)}, u32[]{:S(2)}) collective-permute-start(bf16[2,64,1536]{2,1,0:T(8,128)(2,1)S(1)} %join.11.rest_0_.own_ref), channel_id=1, source_target_pairs={{0,1},{1,0},{2,3},{3,2},{4,5},{5,4},{6,7},{7,6},{8,9},{9,8},{10,11... | collective-permute-start | bytes 1179656 | tf_op jit(solution)/shard_map/ppermute | solution.py:40
  74.5 3.0 %collective-permute-start.20 = (bf16[2,64,1536]{2,1,0:T(8,128)(2,1)S(1)}, bf16[2,64,1536]{2,1,0:T(8,128)(2,1)S(1)}, u32[]{:S(2)}, u32[]{:S(2)}) collective-permute-start(bf16[2,64,1536]{2,1,0:T(8,128)(2,1)S(1)} %join_line.1.rest_0_.own_ref), channel_id=1, source_target_pairs={{0,1},{1,0},{2,3},{3,2},{4,5},{5,4},{6,7},{7,6},{8,9},{9,8},{10,11... | collective-permute-start | bytes 1179656 | tf_op jit(solution)/shard_map/ppermute | solution.py:40
  79.0 14.2 %collective-permute-start.24 = (bf16[32,1280]{1,0:T(8,128)(2,1)S(1)}, bf16[32,1280]{1,0:T(8,128)(2,1)S(1)}, u32[]{:S(2)}, u32[]{:S(2)}) collective-permute-start(bf16[32,1280]{1,0:T(8,128)(2,1)S(1)} %get-tuple-element.48), channel_id=1, source_target_pairs={{0,24},{8,16},{16,8},{24,0},{1,25},{9,17},{17,9},{25,1},{2,26},{10... | collective-permute-start | bytes 245768 | tf_op jit(solution)/shard_map/ppermute | solution.py:40
  81.6 11.7 %collective-permute-start.23 = (bf16[32,1280]{1,0:T(8,128)(2,1)S(1)}, bf16[32,1280]{1,0:T(8,128)(2,1)S(1)}, u32[]{:S(2)}, u32[]{:S(2)}) collective-permute-start(bf16[32,1280]{1,0:T(8,128)(2,1)S(1)} %get-tuple-element.49), channel_id=1, source_target_pairs={{0,16},{8,24},{16,0},{24,8},{1,17},{9,25},{17,1},{25,9},{2,18},{10... | collective-permute-start | bytes 245768 | tf_op jit(solution)/shard_map/ppermute | solution.py:40
  82.1 11.2 %collective-permute-start.22 = (bf16[32,1280]{1,0:T(8,128)(2,1)S(1)}, bf16[32,1280]{1,0:T(8,128)(2,1)S(1)}, u32[]{:S(2)}, u32[]{:S(2)}) collective-permute-start(bf16[32,1280]{1,0:T(8,128)(2,1)S(1)} %get-tuple-element.47), channel_id=1, source_target_pairs={{0,8},{8,0},{16,24},{24,16},{1,9},{9,1},{17,25},{25,17},{2,10},{10... | collective-permute-start | bytes 245768 | tf_op jit(solution)/shard_map/ppermute | solution.py:40

commit v8 on v6

--- a/solution.py
+++ b/solution.py
@@ -11,7 +11,7 @@
 BF16 = jnp.bfloat16
 F32 = jnp.float32
 LOAD_BYTES = 24 * 1024 * 1024
-CHUNKS = 3
+CHUNKS = 2
 PIECE = 384
 VMEM_BYTES = 40 * 1024 * 1024
 SMALL_BYTES = 16 * 1024 * 1024

time: 94.1 us -> 94.1 us (level)
  starting transfers between devices: 30.3 us -> 36.6 us
  waiting for transfers between devices: 28.6 us -> 22.6 us
    ppermute x24 -> x18, starting transfers between devices: 30.3 us -> 36.6 us  [exchange(): return lax.ppermute(array, axis, [(i, i ^ step) for i in range(size)])]
    ppermute x24 -> x18, waiting for transfers between devices: 28.6 us -> 22.6 us  [exchange(): return lax.ppermute(array, axis, [(i, i ^ step) for i in range(size)])]
    pallas_call x3 -> x2, Pallas kernels: 8.59 us -> 8.7 us  [forward(): pl.pallas_call(kernel, grid=(1,), out_shape=(jax.ShapeDtypeStruct((2, hal...]
    pallas_call x3 -> x2, Pallas kernels: 3.85 us -> 3.78 us  [input_grads(): pl.pallas_call(kernel, grid=(1,), out_shape=jax.ShapeDtypeStruct((total,...]
  transfers between devices with their start and end apart: 24 -> 18, of which waited for: 11 -> 6; matrix products, arithmetic and copies ran while one was open for 0% -> 0% of each run, Pallas kernels for 29% -> 27%
where the time goes in v8:
time: 94.1 us; the launch traced here: 93.9 us
  starting transfers between devices  36.6 us (39%)
  Pallas kernels  31.7 us (34%)
  waiting for transfers between devices  22.6 us (24%)
  other arithmetic  1.73 us (2%)
    ppermute x18, starting transfers between devices, exchange(): return lax.ppermute(array, axis, [(i, i ^ step) for i in range(size)])  36.6 us
    ppermute x18, waiting for transfers between devices, exchange(): return lax.ppermute(array, axis, [(i, i ^ step) for i in range(size)])  22.6 us
    pallas_call x1, Pallas kernels, weight_grads(): pl.pallas_call(kernel, grid=(2 * len(finals),), out_shape=(jax.ShapeDtype...  10.5 us
    pallas_call x2, Pallas kernels, forward(): pl.pallas_call(kernel, grid=(1,), out_shape=(jax.ShapeDtypeStruct((2, hal...  8.7 us
    pallas_call x1, Pallas kernels, load(): pl.pallas_call(kernel, out_shape=tuple((jax.ShapeDtypeStruct(w.shape, w.d...  7.72 us
    pallas_call x2, Pallas kernels, input_grads(): pl.pallas_call(kernel, grid=(1,), out_shape=jax.ShapeDtypeStruct((total,...  3.78 us
  transfers between devices with their start and end apart: 18, of which 6 were waited for; matrix products, arithmetic and copies ran while one was open for 0% of the time, Pallas kernels for 27%

profile of v8, /device:TPU:0, one launch (start us, length us, event | category | flops | bytes accessed | tf_op | source)
XLA Modules:
  0.0 93.9 jit_solution(13932279059590022031)
XLA Ops:
  0.6 0.9 %pad_maximum_fusion.1.refs_0_ = bf16[2,32,1280]{2,1,0:T(8,128)(2,1)S(1)} fusion(bf16[1,32,1280]{2,1,0:T(8,128)(2,1)} %bitcast.8, bf16[1,32,1280]{2,1,0:T(8,128)(2,1)} %bitcast.10), kind=kLoop, calls=%fused_computation.7 | loop fusion | flops 81920 | bytes 327680 | tf_op jit(solution)/shard_map/stack | solution.py:340
  1.6 3.0 %collective-permute-start = (bf16[2,32,1280]{2,1,0:T(8,128)(2,1)S(1)}, bf16[2,32,1280]{2,1,0:T(8,128)(2,1)S(1)}, u32[]{:S(2)}, u32[]{:S(2)}) collective-permute-start(bf16[2,32,1280]{2,1,0:T(8,128)(2,1)S(1)} %pad_maximum_fusion.1.refs_0_), channel_id=1, source_target_pairs={{0,8},{8,0},{16,24},{24,16},{1,9},{9,1},{17,25},{25,17},{2,10},{10... | collective-permute-start | bytes 491528 | tf_op jit(solution)/shard_map/ppermute | solution.py:40
  4.6 1.5 %collective-permute-start.1 = (bf16[2,32,1280]{2,1,0:T(8,128)(2,1)S(1)}, bf16[2,32,1280]{2,1,0:T(8,128)(2,1)S(1)}, u32[]{:S(2)}, u32[]{:S(2)}) collective-permute-start(bf16[2,32,1280]{2,1,0:T(8,128)(2,1)S(1)} %pad_maximum_fusion.1.refs_0_), channel_id=1, source_target_pairs={{0,16},{8,24},{16,0},{24,8},{1,17},{9,25},{17,1},{25,9},{2,18},{10... | collective-permute-start | bytes 491528 | tf_op jit(solution)/shard_map/ppermute | solution.py:40
  6.1 0.0 collective-permute-start.2
  6.1 7.7 %load.1 = (bf16[1280,4608]{1,0:T(8,128)(2,1)S(1)}, bf16[4608,1280]{1,0:T(8,128)(2,1)S(1)}) custom-call(bf16[1280,4608]{1,0:T(8,128)(2,1)} %refs_0_.1, bf16[4608,1280]{1,0:T(8,128)(2,1)} %refs_1_.1), custom_call_target="tpu_custom_call" | custom-call | bytes 47185920 | tf_op jit(solution)/shard_map/load/pallas_call | solution.py:84
  13.9 0.0 collective-permute-done.refs_1_
  13.9 0.0 collective-permute-done.1.refs_2_
  13.9 4.3 %forward.2 = (f32[2,64,2304]{2,1,0:T(8,128)S(1)}, bf16[2,64,2304]{2,1,0:T(8,128)(2,1)S(1)}) custom-call(s32[1]{0:T(128)} %bitcast.rank_ref, bf16[2,32,1280]{2,1,0:T(8,128)(2,1)S(1)} %pad_maximum_fusion.1.refs_0_, bf16[2,32,1280]{2,1,0:T(8,128)(2,1)S(1)} %collective-permute-done.refs_1_, bf16[2,32,1280]{2,1,0:T(8,128)(2,1)S(1)} %collective-permute-done.1.refs_2_, ...), custom_call_target="tpu_custom_call" | custom-call | flops 1509949440 | bytes 11796480 | tf_op jit(solution)/shard_map/forward/pallas_call | solution.py:129
  18.2 0.1 collective-permute-start.3
  18.3 4.4 %forward.3 = (f32[2,64,2304]{2,1,0:T(8,128)S(1)}, bf16[2,64,2304]{2,1,0:T(8,128)(2,1)S(1)}) custom-call(s32[1]{0:T(128)} %bitcast.rank_ref, bf16[2,32,1280]{2,1,0:T(8,128)(2,1)S(1)} %pad_maximum_fusion.1.refs_0_, bf16[2,32,1280]{2,1,0:T(8,128)(2,1)S(1)} %collective-permute-done.refs_1_, bf16[2,32,1280]{2,1,0:T(8,128)(2,1)S(1)} %collective-permute-done.1.refs_2_, ...), custom_call_target="tpu_custom_call" | custom-call | flops 1509949440 | bytes 11796480 | tf_op jit(solution)/shard_map/forward/pallas_call | solution.py:129
  22.7 0.0 collective-permute-done.3.received_ref
  22.7 0.1 halve.4
  22.9 0.7 collective-permute-start.4
  23.5 2.0 %collective-permute-start.6 = (bf16[2,32,2304]{2,1,0:T(8,128)(2,1)S(1)}, bf16[2,32,2304]{2,1,0:T(8,128)(2,1)S(1)}, u32[]{:S(2)}, u32[]{:S(2)}) collective-permute-start(bf16[2,32,2304]{2,1,0:T(8,128)(2,1)S(1)} %get-tuple-element.25.rest_0_), channel_id=1, source_target_pairs={{0,2},{1,3},{2,0},{3,1},{4,6},{5,7},{6,4},{7,5},{8,10},{9,11},{10,... | collective-permute-start | bytes 884744 | tf_op jit(solution)/shard_map/ppermute | solution.py:40
  25.6 0.0 collective-permute-done.4.received_ref
  25.6 0.1 halve.5
  25.7 1.7 %collective-permute-start.5 = (bf16[2,32,2304]{2,1,0:T(8,128)(2,1)S(1)}, bf16[2,32,2304]{2,1,0:T(8,128)(2,1)S(1)}, u32[]{:S(2)}, u32[]{:S(2)}) collective-permute-start(bf16[2,32,2304]{2,1,0:T(8,128)(2,1)S(1)} %get-tuple-element.27.rest_0_), channel_id=1, source_target_pairs={{0,2},{1,3},{2,0},{3,1},{4,6},{5,7},{6,4},{7,5},{8,10},{9,11},{10,... | collective-permute-start | bytes 884744 | tf_op jit(solution)/shard_map/ppermute | solution.py:40
  27.4 6.0 %collective-permute-done.6.received_ref = bf16[2,32,2304]{2,1,0:T(8,128)(2,1)S(1)} collective-permute-done((bf16[2,32,2304]{2,1,0:T(8,128)(2,1)S(1)}, bf16[2,32,2304]{2,1,0:T(8,128)(2,1)S(1)}, u32[]{:S(2)}, u32[]{:S(2)}) %collective-permute-start.6) | collective-permute-done | bytes 294944 | tf_op jit(solution)/shard_map/ppermute | solution.py:40
  33.4 0.1 halve.6
  33.4 4.2 %collective-permute-start.8 = (bf16[2,16,2304]{2,1,0:T(8,128)(2,1)S(1)}, bf16[2,16,2304]{2,1,0:T(8,128)(2,1)S(1)}, u32[]{:S(2)}, u32[]{:S(2)}) collective-permute-start(bf16[2,16,2304]{2,1,0:T(8,128)(2,1)S(1)} %get-tuple-element.29.rest_0_), channel_id=1, source_target_pairs={{0,6},{1,7},{2,4},{3,5},{4,2},{5,3},{6,0},{7,1},{8,14},{9,15},{10,... | collective-permute-start | bytes 442376 | tf_op jit(solution)/shard_map/ppermute | solution.py:40
  37.6 1.7 %collective-permute-done.5.received_ref = bf16[2,32,2304]{2,1,0:T(8,128)(2,1)S(1)} collective-permute-done((bf16[2,32,2304]{2,1,0:T(8,128)(2,1)S(1)}, bf16[2,32,2304]{2,1,0:T(8,128)(2,1)S(1)}, u32[]{:S(2)}, u32[]{:S(2)}) %collective-permute-start.5) | collective-permute-done | bytes 294944 | tf_op jit(solution)/shard_map/ppermute | solution.py:40
  39.3 0.1 halve.7
  39.3 6.9 %collective-permute-start.7 = (bf16[2,16,2304]{2,1,0:T(8,128)(2,1)S(1)}, bf16[2,16,2304]{2,1,0:T(8,128)(2,1)S(1)}, u32[]{:S(2)}, u32[]{:S(2)}) collective-permute-start(bf16[2,16,2304]{2,1,0:T(8,128)(2,1)S(1)} %get-tuple-element.31.rest_0_), channel_id=1, source_target_pairs={{0,6},{1,7},{2,4},{3,5},{4,2},{5,3},{6,0},{7,1},{8,14},{9,15},{10,... | collective-permute-start | bytes 442376 | tf_op jit(solution)/shard_map/ppermute | solution.py:40
  46.2 0.1 activate.2.rest_0_.own_ref
  46.3 0.0 copy-start
  46.3 0.0 copy-start.1
  46.3 0.1 collective-permute-start.10
  46.4 4.1 %collective-permute-done.7.received_ref = bf16[2,16,2304]{2,1,0:T(8,128)(2,1)S(1)} collective-permute-done((bf16[2,16,2304]{2,1,0:T(8,128)(2,1)S(1)}, bf16[2,16,2304]{2,1,0:T(8,128)(2,1)S(1)}, u32[]{:S(2)}, u32[]{:S(2)}) %collective-permute-start.7) | collective-permute-done | bytes 147488 | tf_op jit(solution)/shard_map/ppermute | solution.py:40
  50.5 0.1 activate.3.rest_0_.own_ref
  50.6 2.9 %collective-permute-start.9 = (bf16[2,16,2304]{2,1,0:T(8,128)(2,1)S(1)}, bf16[2,16,2304]{2,1,0:T(8,128)(2,1)S(1)}, u32[]{:S(2)}, u32[]{:S(2)}) collective-permute-start(bf16[2,16,2304]{2,1,0:T(8,128)(2,1)S(1)} %activate.3.rest_0_.own_ref), channel_id=1, source_target_pairs={{0,6},{1,7},{2,4},{3,5},{4,2},{5,3},{6,0},{7,1},{8,14},{9,15},{10,... | collective-permute-start | bytes 442376 | tf_op jit(solution)/shard_map/ppermute | solution.py:40
  53.5 0.7 collective-permute-done.10.received_ref
  54.2 6.8 %collective-permute-start.12 = (bf16[2,32,2304]{2,1,0:T(8,128)(2,1)S(1)}, bf16[2,32,2304]{2,1,0:T(8,128)(2,1)S(1)}, u32[]{:S(2)}, u32[]{:S(2)}) collective-permute-start(bf16[2,32,2304]{2,1,0:T(8,128)(2,1)S(1)} %join.6.rest_0_.own_ref), channel_id=1, source_target_pairs={{0,2},{1,3},{2,0},{3,1},{4,6},{5,7},{6,4},{7,5},{8,10},{9,11},{10,... | collective-permute-start | bytes 884744 | tf_op jit(solution)/shard_map/ppermute | solution.py:40
  61.1 3.0 %collective-permute-start.11 = (bf16[2,32,2304]{2,1,0:T(8,128)(2,1)S(1)}, bf16[2,32,2304]{2,1,0:T(8,128)(2,1)S(1)}, u32[]{:S(2)}, u32[]{:S(2)}) collective-permute-start(bf16[2,32,2304]{2,1,0:T(8,128)(2,1)S(1)} %join.7.rest_0_.own_ref), channel_id=1, source_target_pairs={{0,2},{1,3},{2,0},{3,1},{4,6},{5,7},{6,4},{7,5},{8,10},{9,11},{10,... | collective-permute-start | bytes 884744 | tf_op jit(solution)/shard_map/ppermute | solution.py:40
  64.2 4.7 %collective-permute-done.12.received_ref = bf16[2,32,2304]{2,1,0:T(8,128)(2,1)S(1)} collective-permute-done((bf16[2,32,2304]{2,1,0:T(8,128)(2,1)S(1)}, bf16[2,32,2304]{2,1,0:T(8,128)(2,1)S(1)}, u32[]{:S(2)}, u32[]{:S(2)}) %collective-permute-start.12) | collective-permute-done | bytes 294944 | tf_op jit(solution)/shard_map/ppermute | solution.py:40
  68.9 0.1 collective-permute-start.14
  69.0 5.5 %collective-permute-done.11.received_ref = bf16[2,32,2304]{2,1,0:T(8,128)(2,1)S(1)} collective-permute-done((bf16[2,32,2304]{2,1,0:T(8,128)(2,1)S(1)}, bf16[2,32,2304]{2,1,0:T(8,128)(2,1)S(1)}, u32[]{:S(2)}, u32[]{:S(2)}) %collective-permute-start.11) | collective-permute-done | bytes 294944 | tf_op jit(solution)/shard_map/ppermute | solution.py:40
  74.5 0.1 collective-permute-start.13
  74.6 0.3 convolution_convert_fusion.xt_ref
  74.9 0.0 collective-permute-done.14.received_ref
  74.9 0.1 join.10.grad_ref.refs_0_
  75.0 1.9 %input_grads.2.rest_0_.refs_0_ = f32[128,1280]{1,0:T(8,128)S(1)} custom-call(bf16[2,128,2304]{2,1,0:T(8,128)(2,1)S(1)} %join.10.grad_ref.refs_0_, bf16[1280,4608]{1,0:T(8,128)(2,1)S(1)} %get-tuple-element.19.refs_4_.wi_ref), custom_call_target="tpu_custom_call" | custom-call | flops 754974720 | bytes 5898240 | tf_op jit(solution)/shard_map/input_grads/pallas_call | solution.py:275
  76.9 0.3 join.11.grad_ref.refs_1_
  77.2 1.9 %input_grads.3 = f32[128,1280]{1,0:T(8,128)S(1)} custom-call(bf16[2,128,2304]{2,1,0:T(8,128)(2,1)S(1)} %join.11.grad_ref.refs_1_, bf16[1280,4608]{1,0:T(8,128)(2,1)S(1)} %get-tuple-element.19.refs_4_.wi_ref, f32[128,1280]{1,0:T(8,128)S(1)} %input_grads.2.rest_0_.refs_0_), custom_call_target="tpu_custom_call" | custom-call | flops 754974720 | bytes 5898240 | tf_op jit(solution)/shard_map/input_grads/pallas_call | solution.py:275
  79.2 2.5 %collective-permute-start.17 = (bf16[32,1280]{1,0:T(8,128)(2,1)S(1)}, bf16[32,1280]{1,0:T(8,128)(2,1)S(1)}, u32[]{:S(2)}, u32[]{:S(2)}) collective-permute-start(bf16[32,1280]{1,0:T(8,128)(2,1)S(1)} %get-tuple-element.36), channel_id=1, source_target_pairs={{0,24},{8,16},{16,8},{24,0},{1,25},{9,17},{17,9},{25,1},{2,26},{10... | collective-permute-start | bytes 245768 | tf_op jit(solution)/shard_map/ppermute | solution.py:40
  81.7 0.5 collective-permute-start.16
  82.2 0.5 collective-permute-start.15
  82.7 10.5 %weight_grads.1 = (bf16[1280,4608]{1,0:T(8,128)(2,1)}, bf16[4608,1280]{1,0:T(8,128)(2,1)}) custom-call(bf16[1280,128]{1,0:T(8,128)(2,1)S(1)} %convolution_convert_fusion.xt_ref, bf16[128,1280]{1,0:T(8,128)(2,1)S(1)} %slice_bitcast_fusion.gs_ref, bf16[2,128,2304]{2,1,0:T(8,128)(2,1)S(1)} %join.10.grad_ref.refs_0_, bf16[2,128,2304]{2,1,0:T(8,128)(2,1)S(1)} %join.11.grad_ref.refs_1_), custom_call_target="tpu_custom_call" | custom-call | flops 3019898880 | bytes 23592960 | tf_op jit(solution)/shard_map/weight_grads/pallas_call | solution.py:312
  93.2 0.7 fusion.1
  (18 shorter events, 0.3 us)
Async XLA Ops:
  1.6 12.3 %collective-permute-start = (bf16[2,32,1280]{2,1,0:T(8,128)(2,1)S(1)}, bf16[2,32,1280]{2,1,0:T(8,128)(2,1)S(1)}, u32[]{:S(2)}, u32[]{:S(2)}) collective-permute-start(bf16[2,32,1280]{2,1,0:T(8,128)(2,1)S(1)} %pad_maximum_fusion.1.refs_0_), channel_id=1, source_target_pairs={{0,8},{8,0},{16,24},{24,16},{1,9},{9,1},{17,25},{25,17},{2,10},{10... | collective-permute-start | bytes 491528 | tf_op jit(solution)/shard_map/ppermute | solution.py:40
  4.6 9.3 %collective-permute-start.1 = (bf16[2,32,1280]{2,1,0:T(8,128)(2,1)S(1)}, bf16[2,32,1280]{2,1,0:T(8,128)(2,1)S(1)}, u32[]{:S(2)}, u32[]{:S(2)}) collective-permute-start(bf16[2,32,1280]{2,1,0:T(8,128)(2,1)S(1)} %pad_maximum_fusion.1.refs_0_), channel_id=1, source_target_pairs={{0,16},{8,24},{16,0},{24,8},{1,17},{9,25},{17,1},{25,9},{2,18},{10... | collective-permute-start | bytes 491528 | tf_op jit(solution)/shard_map/ppermute | solution.py:40
  6.1 7.8 %collective-permute-start.2 = (bf16[2,32,1280]{2,1,0:T(8,128)(2,1)S(1)}, bf16[2,32,1280]{2,1,0:T(8,128)(2,1)S(1)}, u32[]{:S(2)}, u32[]{:S(2)}) collective-permute-start(bf16[2,32,1280]{2,1,0:T(8,128)(2,1)S(1)} %pad_maximum_fusion.1.refs_0_), channel_id=1, source_target_pairs={{0,24},{8,16},{16,8},{24,0},{1,25},{9,17},{17,9},{25,1},{2,26},{10... | collective-permute-start | bytes 491528 | tf_op jit(solution)/shard_map/ppermute | solution.py:40
  18.2 4.4 %collective-permute-start.3 = (bf16[2,64,2304]{2,1,0:T(8,128)(2,1)S(1)}, bf16[2,64,2304]{2,1,0:T(8,128)(2,1)S(1)}, u32[]{:S(2)}, u32[]{:S(2)}) collective-permute-start(bf16[2,64,2304]{2,1,0:T(8,128)(2,1)S(1)} %get-tuple-element.21.refs_6_), channel_id=1, source_target_pairs={{0,1},{1,0},{2,3},{3,2},{4,5},{5,4},{6,7},{7,6},{8,9},{9,8},{10,11... | collective-permute-start | bytes 1769480 | tf_op jit(solution)/shard_map/ppermute | solution.py:40
  22.9 2.7 %collective-permute-start.4 = (bf16[2,64,2304]{2,1,0:T(8,128)(2,1)S(1)}, bf16[2,64,2304]{2,1,0:T(8,128)(2,1)S(1)}, u32[]{:S(2)}, u32[]{:S(2)}) collective-permute-start(bf16[2,64,2304]{2,1,0:T(8,128)(2,1)S(1)} %relay.1.rest_0_), channel_id=1, source_target_pairs={{0,1},{1,0},{2,3},{3,2},{4,5},{5,4},{6,7},{7,6},{8,9},{9,8},{10,11... | collective-permute-start | bytes 1769480 | tf_op jit(solution)/shard_map/ppermute | solution.py:40
  23.5 9.8 %collective-permute-start.6 = (bf16[2,32,2304]{2,1,0:T(8,128)(2,1)S(1)}, bf16[2,32,2304]{2,1,0:T(8,128)(2,1)S(1)}, u32[]{:S(2)}, u32[]{:S(2)}) collective-permute-start(bf16[2,32,2304]{2,1,0:T(8,128)(2,1)S(1)} %get-tuple-element.25.rest_0_), channel_id=1, source_target_pairs={{0,2},{1,3},{2,0},{3,1},{4,6},{5,7},{6,4},{7,5},{8,10},{9,11},{10,... | collective-permute-start | bytes 884744 | tf_op jit(solution)/shard_map/ppermute | solution.py:40
  25.7 13.6 %collective-permute-start.5 = (bf16[2,32,2304]{2,1,0:T(8,128)(2,1)S(1)}, bf16[2,32,2304]{2,1,0:T(8,128)(2,1)S(1)}, u32[]{:S(2)}, u32[]{:S(2)}) collective-permute-start(bf16[2,32,2304]{2,1,0:T(8,128)(2,1)S(1)} %get-tuple-element.27.rest_0_), channel_id=1, source_target_pairs={{0,2},{1,3},{2,0},{3,1},{4,6},{5,7},{6,4},{7,5},{8,10},{9,11},{10,... | collective-permute-start | bytes 884744 | tf_op jit(solution)/shard_map/ppermute | solution.py:40
  33.4 12.8 %collective-permute-start.8 = (bf16[2,16,2304]{2,1,0:T(8,128)(2,1)S(1)}, bf16[2,16,2304]{2,1,0:T(8,128)(2,1)S(1)}, u32[]{:S(2)}, u32[]{:S(2)}) collective-permute-start(bf16[2,16,2304]{2,1,0:T(8,128)(2,1)S(1)} %get-tuple-element.29.rest_0_), channel_id=1, source_target_pairs={{0,6},{1,7},{2,4},{3,5},{4,2},{5,3},{6,0},{7,1},{8,14},{9,15},{10,... | collective-permute-start | bytes 442376 | tf_op jit(solution)/shard_map/ppermute | solution.py:40
  39.3 11.1 %collective-permute-start.7 = (bf16[2,16,2304]{2,1,0:T(8,128)(2,1)S(1)}, bf16[2,16,2304]{2,1,0:T(8,128)(2,1)S(1)}, u32[]{:S(2)}, u32[]{:S(2)}) collective-permute-start(bf16[2,16,2304]{2,1,0:T(8,128)(2,1)S(1)} %get-tuple-element.31.rest_0_), channel_id=1, source_target_pairs={{0,6},{1,7},{2,4},{3,5},{4,2},{5,3},{6,0},{7,1},{8,14},{9,15},{10,... | collective-permute-start | bytes 442376 | tf_op jit(solution)/shard_map/ppermute | solution.py:40
  46.3 17.8 %copy-start = (bf16[32,1280]{1,0:T(8,128)(2,1)S(1)}, bf16[32,1280]{1,0:T(8,128)(2,1)}, u32[]{:S(2)}) copy-start(bf16[32,1280]{1,0:T(8,128)(2,1)} %param.5) | copy-start | bytes 245764
  46.3 17.8 %copy-start.1 = (bf16[32,1280]{1,0:T(8,128)(2,1)S(1)}, bf16[32,1280]{1,0:T(8,128)(2,1)}, u32[]{:S(2)}) copy-start(bf16[32,1280]{1,0:T(8,128)(2,1)} %param.4) | copy-start | bytes 245764
  46.3 7.8 %collective-permute-start.10 = (bf16[2,16,2304]{2,1,0:T(8,128)(2,1)S(1)}, bf16[2,16,2304]{2,1,0:T(8,128)(2,1)S(1)}, u32[]{:S(2)}, u32[]{:S(2)}) collective-permute-start(bf16[2,16,2304]{2,1,0:T(8,128)(2,1)S(1)} %activate.2.rest_0_.own_ref), channel_id=1, source_target_pairs={{0,6},{1,7},{2,4},{3,5},{4,2},{5,3},{6,0},{7,1},{8,14},{9,15},{10,... | collective-permute-start | bytes 442376 | tf_op jit(solution)/shard_map/ppermute | solution.py:40
  50.6 10.5 %collective-permute-start.9 = (bf16[2,16,2304]{2,1,0:T(8,128)(2,1)S(1)}, bf16[2,16,2304]{2,1,0:T(8,128)(2,1)S(1)}, u32[]{:S(2)}, u32[]{:S(2)}) collective-permute-start(bf16[2,16,2304]{2,1,0:T(8,128)(2,1)S(1)} %activate.3.rest_0_.own_ref), channel_id=1, source_target_pairs={{0,6},{1,7},{2,4},{3,5},{4,2},{5,3},{6,0},{7,1},{8,14},{9,15},{10,... | collective-permute-start | bytes 442376 | tf_op jit(solution)/shard_map/ppermute | solution.py:40
  54.2 14.7 %collective-permute-start.12 = (bf16[2,32,2304]{2,1,0:T(8,128)(2,1)S(1)}, bf16[2,32,2304]{2,1,0:T(8,128)(2,1)S(1)}, u32[]{:S(2)}, u32[]{:S(2)}) collective-permute-start(bf16[2,32,2304]{2,1,0:T(8,128)(2,1)S(1)} %join.6.rest_0_.own_ref), channel_id=1, source_target_pairs={{0,2},{1,3},{2,0},{3,1},{4,6},{5,7},{6,4},{7,5},{8,10},{9,11},{10,... | collective-permute-start | bytes 884744 | tf_op jit(solution)/shard_map/ppermute | solution.py:40
  61.1 13.4 %collective-permute-start.11 = (bf16[2,32,2304]{2,1,0:T(8,128)(2,1)S(1)}, bf16[2,32,2304]{2,1,0:T(8,128)(2,1)S(1)}, u32[]{:S(2)}, u32[]{:S(2)}) collective-permute-start(bf16[2,32,2304]{2,1,0:T(8,128)(2,1)S(1)} %join.7.rest_0_.own_ref), channel_id=1, source_target_pairs={{0,2},{1,3},{2,0},{3,1},{4,6},{5,7},{6,4},{7,5},{8,10},{9,11},{10,... | collective-permute-start | bytes 884744 | tf_op jit(solution)/shard_map/ppermute | solution.py:40
  68.9 6.0 %collective-permute-start.14 = (bf16[2,64,2304]{2,1,0:T(8,128)(2,1)S(1)}, bf16[2,64,2304]{2,1,0:T(8,128)(2,1)S(1)}, u32[]{:S(2)}, u32[]{:S(2)}) collective-permute-start(bf16[2,64,2304]{2,1,0:T(8,128)(2,1)S(1)} %join.8.rest_0_.own_ref), channel_id=1, source_target_pairs={{0,1},{1,0},{2,3},{3,2},{4,5},{5,4},{6,7},{7,6},{8,9},{9,8},{10,11... | collective-permute-start | bytes 1769480 | tf_op jit(solution)/shard_map/ppermute | solution.py:40
  74.5 2.4 %collective-permute-start.13 = (bf16[2,64,2304]{2,1,0:T(8,128)(2,1)S(1)}, bf16[2,64,2304]{2,1,0:T(8,128)(2,1)S(1)}, u32[]{:S(2)}, u32[]{:S(2)}) collective-permute-start(bf16[2,64,2304]{2,1,0:T(8,128)(2,1)S(1)} %join.9.rest_0_.own_ref), channel_id=1, source_target_pairs={{0,1},{1,0},{2,3},{3,2},{4,5},{5,4},{6,7},{7,6},{8,9},{9,8},{10,11... | collective-permute-start | bytes 1769480 | tf_op jit(solution)/shard_map/ppermute | solution.py:40
  79.2 14.0 %collective-permute-start.17 = (bf16[32,1280]{1,0:T(8,128)(2,1)S(1)}, bf16[32,1280]{1,0:T(8,128)(2,1)S(1)}, u32[]{:S(2)}, u32[]{:S(2)}) collective-permute-start(bf16[32,1280]{1,0:T(8,128)(2,1)S(1)} %get-tuple-element.36), channel_id=1, source_target_pairs={{0,24},{8,16},{16,8},{24,0},{1,25},{9,17},{17,9},{25,1},{2,26},{10... | collective-permute-start | bytes 245768 | tf_op jit(solution)/shard_map/ppermute | solution.py:40
  81.7 11.5 %collective-permute-start.16 = (bf16[32,1280]{1,0:T(8,128)(2,1)S(1)}, bf16[32,1280]{1,0:T(8,128)(2,1)S(1)}, u32[]{:S(2)}, u32[]{:S(2)}) collective-permute-start(bf16[32,1280]{1,0:T(8,128)(2,1)S(1)} %get-tuple-element.37), channel_id=1, source_target_pairs={{0,16},{8,24},{16,0},{24,8},{1,17},{9,25},{17,1},{25,9},{2,18},{10... | collective-permute-start | bytes 245768 | tf_op jit(solution)/shard_map/ppermute | solution.py:40
  82.2 11.0 %collective-permute-start.15 = (bf16[32,1280]{1,0:T(8,128)(2,1)S(1)}, bf16[32,1280]{1,0:T(8,128)(2,1)S(1)}, u32[]{:S(2)}, u32[]{:S(2)}) collective-permute-start(bf16[32,1280]{1,0:T(8,128)(2,1)S(1)} %get-tuple-element.35), channel_id=1, source_target_pairs={{0,8},{8,0},{16,24},{24,16},{1,9},{9,1},{17,25},{25,17},{2,10},{10... | collective-permute-start | bytes 245768 | tf_op jit(solution)/shard_map/ppermute | solution.py:40
